TPU v7x, 32 devices: a whole 2x2x4 slice. The times are simulated.
32 devices in a mesh: grp: 2 (over x), dim: 8 (over z, y), blk: 2 (over core).
Axes of the slice: x: 2, y: 2, z: 4, core: 2. Of those that a mesh axis runs over, the one named last changes fastest.
Arguments:
- particles: float32 [1024, 131072], P(('grp', 'blk'), 'dim'), parts along dimension 0, may hold values from -30 to 30, as said below
- scores: float32 [1024, 131072], P(('grp', 'blk'), 'dim'), parts along dimension 0, may hold values from -0.00048828125 to 0.00048828125
Outputs:
- velocity: float32 [1024, 131072], P(('grp', 'blk'), 'dim'), parts along dimension 0
There are 2 independent parts, one for each index of `grp`. A program takes and returns all parts, laid end to end along the dimension named above; each array names one. Nothing has to cross between parts.
Inputs may be any that keep to these rules, and one draw needn't show every extreme that they name: `particles`: finite positions.
All inputs are finite; a program needn't handle non-finite values.
Results may differ from a plain program's by a relative error of at most 0.000084.
Values sent between devices are 32-bit elements; how exact they have to be, the bound alone decides.
No kernel may reach another device: no remote copies, remote signals or barrier semaphores. Data moves between devices by JAX's collectives and lax.ppermute only.
A program may use at most 192 MiB of HBM per device.

v0:
```python
import math

import jax
import jax.numpy as jnp
from jax import lax
from jax.sharding import PartitionSpec as P


def from_behind(array, axis, by):
    count = lax.axis_size(axis)
    return lax.ppermute(array, axis, [(i, (i + by) % count) for i in range(count)])


def exact_dot(left, right):
    return jnp.dot(left, right, precision=lax.Precision.HIGHEST, preferred_element_type=jnp.float32)


def body(particles, scores):
    row_count = particles.shape[0]
    cycle_size = lax.axis_size("blk")
    total_rows = row_count * cycle_size
    scale_base = total_rows * total_rows * math.log(total_rows)
    row_norms = jnp.sum(particles * particles, axis=1)
    column_total, norm_total = lax.psum((jnp.sum(particles, axis=0), jnp.sum(row_norms)), "blk")
    local_part = 2.0 * total_rows * norm_total - 2.0 * jnp.sum(column_total * column_total)
    spread = lax.psum(local_part, "dim")
    held_points = [particles]
    held_scores = [scores]
    partials = [row_norms[:, None] + row_norms[None, :] - 2.0 * exact_dot(particles, particles.T)]
    visitor = (particles, scores)
    visitor = from_behind((visitor[0], visitor[1]), "blk", 1)
    other_norms = jnp.sum(visitor[0] * visitor[0], axis=1)
    partials.append(
        row_norms[:, None] + other_norms[None, :] - 2.0 * exact_dot(particles, visitor[0].T)
    )
    held_points.append(visitor[0])
    held_scores.append(visitor[1])
    all_points = jnp.concatenate(held_points, axis=0)
    all_scores = jnp.concatenate(held_scores, axis=0)
    stacked = jnp.concatenate(partials, axis=1)
    distance = lax.psum(stacked, "dim")
    kernel_width = spread / scale_base
    kernel = jnp.exp(-distance / kernel_width)
    weight = jnp.sum(kernel, axis=1)
    pulled = exact_dot(kernel, all_scores)
    averaged = exact_dot(kernel, all_points)
    return 0.5 * kernel_width * pulled + particles * weight[:, None] - averaged


def solution(mesh):
    return jax.shard_map(
        body,
        mesh=mesh,
        in_specs=(P(("grp", "blk"), "dim"), P(("grp", "blk"), "dim")),
        out_specs=P(("grp", "blk"), "dim"),
        check_vma=False,
    )
```

profile of v0, /device:TPU:0, one launch (start us, length us, event | category | flops | bytes accessed | tf_op | source)
XLA Modules:
  0.0 217.9 jit_solution(16783960210081661764)
XLA Ops:
  6.5 0.0 all-reduce.3.cloned.1.call-start
  6.5 0.5 collective-permute-start
  7.0 0.1 collective-permute-start.1
  7.0 9.4 %fusion.21 = (f32[16384]{0:T(1024)}, f32[256]{0:T(256)S(1)}, f32[]{:T(128)}) fusion(f32[256,16384]{1,0:T(8,128)} %param.2), kind=kLoop, calls=%fused_computation.24 | loop fusion | flops 16760575 | bytes 16843780 | tf_op jit(solution)/shard_map/reduce_sum | solution.py:24
  16.5 0.0 all-reduce.3.cloned.1.call-update
  16.5 0.0 all-reduce.5.cloned.1.call-start
  16.6 17.7 %fusion.17 = f32[256,256]{0,1:T(8,128)S(1)} fusion(f32[256,16384]{1,0:T(8,128)} %param.2, f32[256]{0:T(256)S(1)} %get-tuple-element.6), kind=kOutput, calls=%fused_computation.16 | convolution fusion | flops 12885098496 | bytes 17040384 | tf_op jit(solution)/shard_map/dot_general | solution.py:15
  34.3 0.0 collective-permute-done
  34.3 7.0 %multiply_reduce_fusion = f32[256]{0:T(256)S(1)} fusion(f32[256,16384]{1,0:T(8,128)} %collective-permute-done), kind=kLoop, calls=%fused_computation.11 | loop fusion | flops 8388352 | bytes 16778240 | tf_op jit(solution)/shard_map/reduce_sum | solution.py:32
  41.3 17.7 %add_subtract_fusion = f32[256,256]{0,1:T(8,128)S(1)} fusion(f32[256]{0:T(256)S(1)} %multiply_reduce_fusion, f32[256,16384]{1,0:T(8,128)} %param.2, f32[256,16384]{1,0:T(8,128)} %collective-permute-done, f32[256]{0:T(256)S(1)} %get-tuple-element.6), kind=kOutput, calls=%fused_computation.19 | convolution fusion | flops 12885098496 | bytes 33818624 | tf_op jit(solution)/shard_map/dot_general | solution.py:15
  59.0 0.8 pad_maximum_fusion
  59.8 0.0 all-reduce.5.cloned.1.call-update
  59.9 3.1 %psum.28 = f32[]{:T(128)} all-reduce(f32[]{:T(128)} %get-tuple-element.7), channel_id=1, replica_groups=mesh['grp'=2,'dim'=8,'blk'=2] {'blk'}, use_global_device_ids=true, to_apply=%region_1.0 | all-reduce | flops 1 | bytes 8 | tf_op jit(solution)/shard_map/psum | solution.py:24
  63.5 0.0 all-reduce.3.cloned.1.call-done
  63.5 1.5 multiply_reduce_fusion.3
  65.7 23.8 %psum.30 = f32[]{:T(128)} all-reduce(f32[]{:T(128)S(6)} %sub.12), channel_id=1, replica_groups=mesh['grp'=2,'dim'=8,'blk'=2] {'dim'}, use_global_device_ids=true, to_apply=%region_5.0 | all-reduce | flops 1 | bytes 8 | tf_op jit(solution)/shard_map/psum | solution.py:26
  90.8 44.2 %all-reduce.5.cloned.1.call-done = f32[256,512]{0,1:T(8,128)} async-done(((f32[256,512]{0,1:T(8,128)}), f32[256,512]{0,1:T(8,128)}) %all-reduce.5.cloned.1.call-update) | async-done | bytes 524304 | tf_op jit(solution)/shard_map/psum | solution.py:41
  135.0 1.2 fusion.20
  136.2 0.0 copy-start
  136.2 35.8 %fusion.4 = f32[256,16384]{1,0:T(8,128)} fusion(f32[256,16384]{1,0:T(8,128)} %collective-permute-done, f32[256,16384]{1,0:T(8,128)} %param.2, f32[256,512]{0,1:T(8,128)} %all-reduce.5.cloned.1.call-done, f32[]{:T(128)S(6)} %div.9), kind=kOutput, calls=%fused_computation.4 | convolution fusion | flops 25778454528 | bytes 50855940 | tf_op jit(solution)/shard_map/dot_general | solution.py:15
  172.0 0.0 collective-permute-done.1
  172.0 0.0 copy-done
  172.0 39.1 %fusion.14 = f32[256,16384]{1,0:T(8,128)} fusion(f32[256,16384]{1,0:T(8,128)} %fusion.4, f32[256,16384]{1,0:T(8,128)} %collective-permute-done.1, f32[256,16384]{1,0:T(8,128)} %param.3, f32[256,16384]{1,0:T(8,128)} %param.2, f32[256]{0:T(256)S(1)} %fusion.20, f32[]{:T(128)S(6)} %mul_shard_map.7, f32[256,512]{0,1:T(8,128)S(1)} %copy-done, f32[]{:T(128)S(6)} %div.9), kind=kOutput, calls=%fused_computation.10 | convolution fusion | flops 25795231744 | bytes 84411400 | tf_op jit(solution)/shard_map/dot_general | solution.py:15
Async XLA Ops:
  6.5 57.0 %all-reduce.3.cloned.1.call-start = ((), (), s32[]{:S(2)}) async-start(), calls=%async_computation | async-start | bytes 131072 | tf_op jit(solution)/shard_map/psum | solution.py:24
  6.5 27.7 %collective-permute-start = (f32[256,16384]{1,0:T(8,128)}, f32[256,16384]{1,0:T(8,128)}, u32[]{:S(2)}, u32[]{:S(2)}) collective-permute-start(f32[256,16384]{1,0:T(8,128)} %param.2), channel_id=1, source_target_pairs={{0,1},{1,0},{2,3},{3,2},{4,5},{5,4},{6,7},{7,6},{8,9},{9,8},{10,11... | collective-permute-start | bytes 50331656 | tf_op jit(solution)/shard_map/ppermute | solution.py:11
  7.0 165.0 %collective-permute-start.1 = (f32[256,16384]{1,0:T(8,128)}, f32[256,16384]{1,0:T(8,128)}, u32[]{:S(2)}, u32[]{:S(2)}) collective-permute-start(f32[256,16384]{1,0:T(8,128)} %param.3), channel_id=1, source_target_pairs={{0,1},{1,0},{2,3},{3,2},{4,5},{5,4},{6,7},{7,6},{8,9},{9,8},{10,11... | collective-permute-start | bytes 50331656 | tf_op jit(solution)/shard_map/ppermute | solution.py:11
  16.5 118.5 %all-reduce.5.cloned.1.call-start = ((), (), s32[]{:S(2)}) async-start(), calls=%async_computation.1 | async-start | bytes 1048576 | tf_op jit(solution)/shard_map/psum | solution.py:41
  136.2 35.8 %copy-start = (f32[256,512]{0,1:T(8,128)S(1)}, f32[256,512]{0,1:T(8,128)}, u32[]{:S(2)}) copy-start(f32[256,512]{0,1:T(8,128)} %all-reduce.5.cloned.1.call-done) | copy-start | bytes 1572868
Sparse Core Ops, SparseCore 0:
  16.6 39.4 all-reduce.2
  60.0 74.9 all-reduce.4
where the time goes:
time: 218 us
  matrix products  110 us (50%)
  waiting for transfers between devices  44.2 us (20%)
  blocking collectives  26.8 us (12%)
  other arithmetic  19.9 us (9%)
  between operations  16 us (7%)
    dot_general x4, matrix products, exact_dot(): jnp.dot(left, right, precision=lax.Precision.HIGHEST, preferred_element_t...  110 us
    psum x1, waiting for transfers between devices, body(): distance = lax.psum(stacked, 'dim')  44.2 us
    psum x1, blocking collectives, body(): spread = lax.psum(local_part, 'dim')  23.8 us
    reduce_sum x1, other arithmetic, body(): jnp.sum(particles, axis=0)  9.43 us
    reduce_sum x1, other arithmetic, body(): other_norms = jnp.sum(visitor[0] * visitor[0], axis=1)  7 us
  transfers between devices with their start and end apart: 4, of which 1 were waited for; matrix products, arithmetic and copies ran while one was open for 42% of the time, Pallas kernels for 0%

commit v1 on v0

v1 whole, which is shorter than its diff:
```python
import functools
import math

import jax
import jax.numpy as jnp
from jax import lax
from jax.experimental import pallas as pl
from jax.experimental.pallas import tpu as pltpu
from jax.sharding import PartitionSpec as P

CHUNKS = 4
TILE = 1024
VMEM_LIMIT = 40 * 1024 * 1024


def params():
    return pltpu.CompilerParams(vmem_limit_bytes=VMEM_LIMIT)


def split(x):
    hi = x.astype(jnp.bfloat16)
    lo = (x - hi.astype(jnp.float32)).astype(jnp.bfloat16)
    return hi, lo


def nt_dot(left, right):
    return lax.dot_general(left, right, (((1,), (1,)), ((), ())), preferred_element_type=jnp.float32)


def nn_dot(left, right):
    return jnp.dot(left, right, preferred_element_type=jnp.float32)


def lane_sums(values):
    total = values[:, :128]
    for start in range(128, values.shape[1], 128):
        total = total + values[:, start:start + 128]
    return total


def whole(array_or_shape):
    shape = getattr(array_or_shape, "shape", array_or_shape)
    return pl.BlockSpec(shape, lambda i: (0,) * len(shape))


def f32(*shape):
    return jax.ShapeDtypeStruct(shape, jnp.float32)


def write_shards(distance_ref, shard_refs):
    count = len(shard_refs)
    rows = shard_refs[0].shape[0]
    me = lax.axis_index("dim")
    for step, shard_ref in enumerate(shard_refs):
        owner = lax.rem(me + step, count)
        shard_ref[...] = distance_ref[pl.ds(pl.multiple_of(owner * rows, rows), rows), :]


def read_shards(shard_refs, distance_ref):
    count = len(shard_refs)
    rows = shard_refs[0].shape[0]
    me = lax.axis_index("dim")
    for step, shard_ref in enumerate(shard_refs):
        owner = lax.rem(me - step + count, count)
        distance_ref[pl.ds(pl.multiple_of(owner * rows, rows), rows), :] = shard_ref[...]


def own_kernel(first, last, *refs):
    refs = list(refs)
    x_ref = refs.pop(0)
    gram_in, cross_in, squares_in = (None, None, None) if first else [refs.pop(0) for _ in range(3)]
    copy_ref = refs.pop(0)
    gram_ref, cross_ref, squares_ref = [refs.pop(0) for _ in range(3)]

    @pl.when(pl.program_id(0) == 0)
    def _():
        gram_ref[...] = jnp.zeros_like(gram_ref) if first else gram_in[...]
        cross_ref[...] = jnp.zeros_like(cross_ref) if first else cross_in[...]
        squares_ref[...] = jnp.zeros_like(squares_ref) if first else squares_in[...]

    x = x_ref[...]
    copy_ref[...] = x
    hi, lo = split(x)
    gram_ref[...] += nt_dot(hi, hi)
    cross_ref[...] += nt_dot(hi, lo)
    squares_ref[...] += lane_sums(x * x)

    if last:
        distance_ref = refs.pop()
        shard_refs = refs

        @pl.when(pl.program_id(0) == pl.num_programs(0) - 1)
        def _():
            mixed = cross_ref[...]
            gram = gram_ref[...] + mixed + mixed.T
            norms = jnp.sum(squares_ref[...], axis=1, keepdims=True)
            distance_ref[...] = norms + norms.T - 2.0 * gram
            write_shards(distance_ref, shard_refs)


def own_part(particles, carried, chunk, chunks, count):
    rows, columns = particles.shape
    width = columns // chunks
    tile = min(TILE, width)
    tiles = width // tile
    first, last = chunk == 0, chunk == chunks - 1
    offset = chunk * tiles
    shard = f32(rows // count, rows)
    outs = [f32(rows, width), f32(rows, rows), f32(rows, rows), f32(rows, 128)] + ([shard] * count if last else [])
    out_specs = [pl.BlockSpec((rows, tile), lambda i: (0, i))] + [whole(o) for o in outs[1:]]
    results = pl.pallas_call(
        functools.partial(own_kernel, first, last),
        grid=(tiles,),
        in_specs=[pl.BlockSpec((rows, tile), lambda i: (0, offset + i))] + [whole(c) for c in carried],
        out_specs=out_specs,
        out_shape=outs,
        scratch_shapes=[pltpu.VMEM((rows, rows), jnp.float32)] if last else [],
        compiler_params=params(),
        cost_estimate=pl.CostEstimate(flops=4 * rows * rows * width, bytes_accessed=8 * rows * width, transcendentals=0),
        name="own_gram",
    )(particles, *carried)
    return results[0], results[1:4], results[4:]


def pair_kernel(first, last, *refs):
    refs = list(refs)
    mine_ref, other_ref = refs.pop(0), refs.pop(0)
    own_squares = refs.pop(0) if last else None
    gram_in, squares_in = (None, None) if first else [refs.pop(0) for _ in range(2)]
    gram_ref, squares_ref = [refs.pop(0) for _ in range(2)]

    @pl.when(pl.program_id(0) == 0)
    def _():
        gram_ref[...] = jnp.zeros_like(gram_ref) if first else gram_in[...]
        squares_ref[...] = jnp.zeros_like(squares_ref) if first else squares_in[...]

    other = other_ref[...]
    my_hi, my_lo = split(mine_ref[...])
    hi, lo = split(other)
    gram_ref[...] += nt_dot(my_hi, hi) + nt_dot(my_lo, hi) + nt_dot(my_hi, lo)
    squares_ref[...] += lane_sums(other * other)

    if last:
        distance_ref = refs.pop()
        shard_refs = refs

        @pl.when(pl.program_id(0) == pl.num_programs(0) - 1)
        def _():
            norms = jnp.sum(own_squares[...], axis=1, keepdims=True)
            others = jnp.sum(squares_ref[...], axis=1, keepdims=True)
            distance_ref[...] = norms + others.T - 2.0 * gram_ref[...]
            write_shards(distance_ref, shard_refs)


def pair_part(particles, visitor, own_squares, carried, chunk, chunks, count):
    rows, columns = particles.shape
    width = columns // chunks
    tile = min(TILE, width)
    tiles = width // tile
    first, last = chunk == 0, chunk == chunks - 1
    offset = chunk * tiles
    outs = [f32(rows, rows), f32(rows, 128)] + ([f32(rows // count, rows)] * count if last else [])
    extra = ([own_squares] if last else []) + list(carried)
    results = pl.pallas_call(
        functools.partial(pair_kernel, first, last),
        grid=(tiles,),
        in_specs=[
            pl.BlockSpec((rows, tile), lambda i: (0, offset + i)),
            pl.BlockSpec((rows, tile), lambda i: (0, i)),
        ] + [whole(e) for e in extra],
        out_specs=[whole(o) for o in outs],
        out_shape=outs,
        scratch_shapes=[pltpu.VMEM((rows, rows), jnp.float32)] if last else [],
        compiler_params=params(),
        cost_estimate=pl.CostEstimate(flops=6 * rows * rows * width, bytes_accessed=8 * rows * width, transcendentals=0),
        name="pair_gram",
    )(particles, visitor, *extra)
    return results[:2], results[2:]


def exchange(shards):
    count = len(shards)
    arrived = [shards[0]]
    for step in range(1, count):
        arrived.append(lax.ppermute(shards[step], "dim", [(i, (i + step) % count) for i in range(count)]))
    total = arrived[0]
    for part in arrived[1:]:
        total = total + part
    gathered = [total]
    for step in range(1, count):
        gathered.append(lax.ppermute(total, "dim", [(i, (i + step) % count) for i in range(count)]))
    return gathered


def own_distance_kernel(*refs):
    shard_refs, (distance_ref, sum_ref) = refs[:-2], refs[-2:]
    read_shards(shard_refs, distance_ref)
    rows = distance_ref.shape[0]
    down = lax.broadcasted_iota(jnp.int32, (rows, rows), 0)
    across = lax.broadcasted_iota(jnp.int32, (rows, rows), 1)
    distance = jnp.where(down == across, 0.0, distance_ref[...])
    distance_ref[...] = distance
    sum_ref[...] = jnp.broadcast_to(jnp.sum(distance), sum_ref.shape)


def own_distance(shards):
    rows = shards[0].shape[1]
    return pl.pallas_call(
        own_distance_kernel,
        out_shape=[f32(rows, rows), f32(8, 128)],
        compiler_params=params(),
        name="own_distance",
    )(*shards)


def weights_kernel(scale_base, *refs):
    own_ref, own_sum, other_sum = refs[:3]
    shard_refs = refs[3:-7]
    own_hi, own_lo, pair_hi, pair_lo, weight_ref, half_ref, pair_ref = refs[-7:]
    read_shards(shard_refs, pair_ref)
    pair = pair_ref[...]
    rows = pair.shape[0]
    spread = jnp.sum(pair) * 2.0 + jnp.sum(own_sum[0:1, 0:1] + other_sum[0:1, 0:1])
    width = jnp.full((1, 1), spread / scale_base, jnp.float32)
    inverse = -1.0 / width
    down = lax.broadcasted_iota(jnp.int32, (rows, rows), 0)
    across = lax.broadcasted_iota(jnp.int32, (rows, rows), 1)
    own_weights = jnp.where(down == across, 0.0, jnp.exp(own_ref[...] * inverse))
    pair_weights = jnp.exp(pair * inverse)
    own_hi[...], own_lo[...] = split(own_weights)
    pair_hi[...], pair_lo[...] = split(pair_weights)
    weight = jnp.sum(own_weights, axis=1, keepdims=True) + jnp.sum(pair_weights, axis=1, keepdims=True)
    weight_ref[...] = jnp.broadcast_to(weight, weight_ref.shape)
    half_ref[...] = jnp.broadcast_to(0.5 * width, half_ref.shape)


def weights_part(own, own_sum, other_sum, shards, scale_base):
    rows = own.shape[0]
    half = jax.ShapeDtypeStruct((rows, rows), jnp.bfloat16)
    return pl.pallas_call(
        functools.partial(weights_kernel, scale_base),
        out_shape=[half, half, half, half, f32(rows, 128), f32(8, 128)],
        scratch_shapes=[pltpu.VMEM((rows, rows), jnp.float32)],
        compiler_params=params(),
        name="kernel_weights",
    )(own, own_sum, other_sum, *shards)


def velocity_kernel(x_ref, s_ref, other_x, other_s, own_hi, own_lo, pair_hi, pair_lo, weight_ref, half_ref, *refs):
    out_ref = refs[-1]
    half = half_ref[0:1, 0:1]
    x = x_ref[...]
    driven = half * s_ref[...]
    hi, lo = split(driven - x)
    out = driven + weight_ref[:, 0:1] * x
    out = out + nn_dot(own_hi[...], hi) + nn_dot(own_hi[...], lo) + nn_dot(own_lo[...], hi)
    hi, lo = split(half * other_s[...] - other_x[...])
    out = out + nn_dot(pair_hi[...], hi) + nn_dot(pair_hi[...], lo) + nn_dot(pair_lo[...], hi)
    out_ref[...] = out


def velocity_part(particles, scores, visitor, visitor_scores, weights, earlier, chunk, chunks):
    rows, columns = particles.shape
    width = columns // chunks
    tile = min(TILE, width)
    tiles = width // tile
    offset = chunk * tiles
    mine = pl.BlockSpec((rows, tile), lambda i: (0, offset + i))
    other = pl.BlockSpec((rows, tile), lambda i: (0, i))
    before = [] if earlier is None else [earlier]
    operands = [particles, scores, visitor, visitor_scores, *weights, *before]
    return pl.pallas_call(
        velocity_kernel,
        grid=(tiles,),
        in_specs=[mine, mine, other, other] + [whole(w) for w in weights] + [pl.BlockSpec(memory_space=pl.ANY)] * len(before),
        out_specs=mine,
        out_shape=f32(rows, columns),
        input_output_aliases={len(operands) - 1: 0} if before else {},
        compiler_params=params(),
        cost_estimate=pl.CostEstimate(flops=12 * rows * rows * width, bytes_accessed=20 * rows * width, transcendentals=0),
        name="velocity",
    )(*operands)


def cut_kernel(width, *refs):
    source, outs, sems = refs[0], refs[1:-1], refs[-1]
    copies = [
        pltpu.make_async_copy(source.at[:, pl.ds(c * width, width)], out, sems.at[c]) for c, out in enumerate(outs)
    ]
    for copy in copies:
        copy.start()
    for copy in copies:
        copy.wait()


def cut(array, chunks):
    rows, columns = array.shape
    width = columns // chunks
    return pl.pallas_call(
        functools.partial(cut_kernel, width),
        in_specs=[pl.BlockSpec(memory_space=pl.ANY)],
        out_specs=[pl.BlockSpec(memory_space=pl.ANY)] * chunks,
        out_shape=[f32(rows, width)] * chunks,
        scratch_shapes=[pltpu.SemaphoreType.DMA((chunks,))],
        compiler_params=params(),
        cost_estimate=pl.CostEstimate(flops=0, bytes_accessed=8 * rows * columns, transcendentals=0),
        name="cut_scores",
    )(array)


def swap(array):
    return lax.ppermute(array, "blk", [(0, 1), (1, 0)])


def body(particles, scores):
    rows, columns = particles.shape
    count = lax.axis_size("dim")
    total_rows = rows * lax.axis_size("blk")
    scale_base = total_rows * total_rows * math.log(total_rows)

    visitors, carried = [], []
    for chunk in range(CHUNKS):
        copy, carried, shards = own_part(particles, carried, chunk, CHUNKS, count)
        visitors.append(swap(copy))
    own_squares = carried[2]
    visitor_scores = [swap(part) for part in cut(scores, CHUNKS)]

    own, own_sum = own_distance(exchange(shards))
    cross = [((d, b), ((d + 1) % count, 1 - b)) for d in range(count) for b in range(2)]
    other_sum = lax.ppermute(own_sum, ("dim", "blk"), [(d * 2 + b, e * 2 + f) for (d, b), (e, f) in cross])

    carried = []
    for chunk in range(CHUNKS):
        carried, shards = pair_part(particles, visitors[chunk], own_squares, carried, chunk, CHUNKS, count)
    weights = weights_part(own, own_sum, other_sum, exchange(shards), scale_base)

    velocity = None
    for chunk in range(CHUNKS):
        velocity = velocity_part(particles, scores, visitors[chunk], visitor_scores[chunk], weights, velocity, chunk, CHUNKS)
    return velocity


def solution(mesh):
    return jax.shard_map(
        body,
        mesh=mesh,
        in_specs=(P(("grp", "blk"), "dim"), P(("grp", "blk"), "dim")),
        out_specs=P(("grp", "blk"), "dim"),
        check_vma=False,
    )
```

time: 218 us -> 490 us (2.25)
  Pallas kernels: 0 us -> 336 us
  matrix products: 110 us -> 0 us
  starting transfers between devices: 0.55 us -> 56 us
  waiting for transfers between devices: 44.2 us -> 93.4 us
  blocking collectives: 26.8 us -> 0 us
  other arithmetic: 19.9 us -> 0.04 us
  between operations: 16 us -> 0.12 us
    pallas_call x0 -> x15, Pallas kernels: none -> 336 us  [the longest x1 255 us: cut(): pl.pallas_call(functools.partial(cut_kernel, width), in_specs=[pl.BlockSp...]
    dot_general x4 -> x0, matrix products: 110 us -> none  [exact_dot(): jnp.dot(left, right, precision=lax.Precision.HIGHEST, preferred_element_t...]
    ppermute x2 -> x37, waiting for transfers between devices: 0.01 us -> 93.4 us  [the longest x14 60.3 us: exchange(): lax.ppermute(shards[step], 'dim', [(i, (i + step) % count) for i in range...]
    ppermute x2 -> x37, starting transfers between devices: 0.51 us -> 56 us  [the longest x14 40.7 us: exchange(): lax.ppermute(total, 'dim', [(i, (i + step) % count) for i in range(count)])]
    psum x2 -> x0, waiting for transfers between devices: 44.2 us -> none  [the longest x1 44.2 us: body(): distance = lax.psum(stacked, 'dim')]
    psum x2 -> x0, blocking collectives: 26.8 us -> none  [the longest x1 23.8 us: body(): spread = lax.psum(local_part, 'dim')]
    reduce_sum x4 -> x0, other arithmetic: 19.1 us -> none  [the longest x1 9.43 us: body(): jnp.sum(particles, axis=0)]
  transfers between devices with their start and end apart: 4 -> 37, of which waited for: 1 -> 27; matrix products, arithmetic and copies ran while one was open for 42% -> 0% of each run, Pallas kernels for 0% -> 63%
where the time goes in v1:
time: 490 us; the launch traced here: 489 us
  Pallas kernels  336 us (69%)
  waiting for transfers between devices  93.4 us (19%)
  starting transfers between devices  56 us (11%)
    pallas_call x1, Pallas kernels, cut(): pl.pallas_call(functools.partial(cut_kernel, width), in_specs=[pl.BlockSp...  255 us
    ppermute x14, waiting for transfers between devices, exchange(): lax.ppermute(shards[step], 'dim', [(i, (i + step) % count) for i in range...  60.3 us
    ppermute x14, starting transfers between devices, exchange(): lax.ppermute(total, 'dim', [(i, (i + step) % count) for i in range(count)])  40.7 us
    pallas_call x4, Pallas kernels, velocity_part(): pl.pallas_call(velocity_kernel, grid=(tiles,), in_specs=[mine, mine, othe...  37.1 us
    ppermute x14, waiting for transfers between devices, exchange(): lax.ppermute(total, 'dim', [(i, (i + step) % count) for i in range(count)])  27.5 us
    pallas_call x4, Pallas kernels, own_part(): pl.pallas_call(functools.partial(own_kernel, first, last), grid=(tiles,),...  22.1 us
    pallas_call x4, Pallas kernels, pair_part(): pl.pallas_call(functools.partial(pair_kernel, first, last), grid=(tiles,)...  20.4 us
    ppermute x14, starting transfers between devices, exchange(): lax.ppermute(shards[step], 'dim', [(i, (i + step) % count) for i in range...  13.2 us
  transfers between devices with their start and end apart: 37, of which 27 were waited for; matrix products, arithmetic and copies ran while one was open for 0% of the time, Pallas kernels for 63%

profile of v1, /device:TPU:0, one launch (start us, length us, event | category | flops | bytes accessed | tf_op | source)
XLA Modules:
  0.0 489.2 jit_solution(10435623449451167278)
XLA Ops:
  0.0 5.2 %own_gram.4 = (f32[256,4096]{1,0:T(8,128)}, f32[256,256]{1,0:T(8,128)S(1)}, f32[256,256]{1,0:T(8,128)S(1)}, f32[256,128]{1,0:T(8,128)S(1)}) custom-call(f32[256,16384]{1,0:T(8,128)} %x_ref.7), custom_call_target="tpu_custom_call" | custom-call | flops 1073741824 | bytes 8388608 | tf_op jit(solution)/shard_map/own_gram/pallas_call | solution.py:111
  5.3 5.3 %own_gram.5 = (f32[256,4096]{1,0:T(8,128)}, f32[256,256]{1,0:T(8,128)S(1)}, f32[256,256]{1,0:T(8,128)S(1)}, f32[256,128]{1,0:T(8,128)S(1)}) custom-call(f32[256,16384]{1,0:T(8,128)} %x_ref.7, f32[256,256]{1,0:T(8,128)S(1)} %get-tuple-element.53.refs_1_, f32[256,256]{1,0:T(8,128)S(1)} %get-tuple-element.54.refs_2_, f32[256,128]{1,0:T(8,128)S(1)} %get-tuple-element.55.refs_3_), custom_call_target="tpu_custom_call" | custom-call | flops 1073741824 | bytes 8388608 | tf_op jit(solution)/shard_map/own_gram/pallas_call | solution.py:111
  10.5 5.3 %own_gram.6 = (f32[256,4096]{1,0:T(8,128)}, f32[256,256]{1,0:T(8,128)S(1)}, f32[256,256]{1,0:T(8,128)S(1)}, f32[256,128]{1,0:T(8,128)S(1)}) custom-call(f32[256,16384]{1,0:T(8,128)} %x_ref.7, f32[256,256]{1,0:T(8,128)S(1)} %get-tuple-element.56.refs_1_, f32[256,256]{1,0:T(8,128)S(1)} %get-tuple-element.57.refs_2_, f32[256,128]{1,0:T(8,128)S(1)} %get-tuple-element.58.refs_3_), custom_call_target="tpu_custom_call" | custom-call | flops 1073741824 | bytes 8388608 | tf_op jit(solution)/shard_map/own_gram/pallas_call | solution.py:111
  16.7 6.3 %own_gram.7 = (f32[256,4096]{1,0:T(8,128)}, f32[256,256]{1,0:T(8,128)}, f32[256,256]{1,0:T(8,128)}, f32[256,128]{1,0:T(8,128)S(1)}, f32[32,256]{1,0:T(8,128)S(1)...) custom-call(f32[256,16384]{1,0:T(8,128)} %x_ref.7, ...), custom_call_target="tpu_custom_call" | custom-call | flops 1073741824 | bytes 8388608 | tf_op jit(solution)/shard_map/own_gram/pallas_call | solution.py:111
  26.0 4.9 %collective-permute-done.2 = f32[32,256]{1,0:T(8,128)S(1)} collective-permute-done((f32[32,256]{1,0:T(8,128)S(1)}, f32[32,256]{1,0:T(8,128)S(1)}, u32[]{:S(2)}, u32[]{:S(2)}) %collective-permute-start.2) | collective-permute-done | bytes 32800 | tf_op jit(solution)/shard_map/ppermute | solution.py:185
  31.0 5.7 %collective-permute-done.3 = f32[32,256]{1,0:T(8,128)S(1)} collective-permute-done((f32[32,256]{1,0:T(8,128)S(1)}, f32[32,256]{1,0:T(8,128)S(1)}, u32[]{:S(2)}, u32[]{:S(2)}) %collective-permute-start.3) | collective-permute-done | bytes 32800 | tf_op jit(solution)/shard_map/ppermute | solution.py:185
  36.7 6.0 %collective-permute-done.4 = f32[32,256]{1,0:T(8,128)S(1)} collective-permute-done((f32[32,256]{1,0:T(8,128)S(1)}, f32[32,256]{1,0:T(8,128)S(1)}, u32[]{:S(2)}, u32[]{:S(2)}) %collective-permute-start.4) | collective-permute-done | bytes 32800 | tf_op jit(solution)/shard_map/ppermute | solution.py:185
  42.7 4.8 collective-permute-done.5
  47.5 4.8 collective-permute-done.6
  60.6 4.4 collective-permute-start.15
  70.8 3.5 collective-permute-start.13
  75.9 3.8 collective-permute-start.12
  81.7 3.8 collective-permute-start.11
  90.3 255.2 %cut_scores.1 = (f32[256,4096]{1,0:T(8,128)}, f32[256,4096]{1,0:T(8,128)S(1)}, f32[256,4096]{1,0:T(8,128)S(1)}, f32[256,4096]{1,0:T(8,128)}) custom-call(f32[256,16384]{1,0:T(8,128)} %s_ref.7), custom_call_target="tpu_custom_call" | custom-call | bytes 33554432 | tf_op jit(solution)/shard_map/cut_scores/pallas_call | solution.py:299
  350.6 4.5 pair_gram.4
  355.2 5.2 %pair_gram.5 = (f32[256,256]{1,0:T(8,128)S(1)}, f32[256,128]{1,0:T(8,128)S(1)}) custom-call(f32[256,16384]{1,0:T(8,128)} %x_ref.7, f32[256,4096]{1,0:T(8,128)} %collective-permute-done.18.refs_1_.other_x, f32[256,256]{1,0:T(8,128)S(1)} %get-tuple-element.78.refs_2_, f32[256,128]{1,0:T(8,128)S(1)} %get-tuple-element.79.refs_3_), custom_call_target="tpu_custom_call" | custom-call | flops 1610612736 | bytes 8388608 | tf_op jit(solution)/shard_map/pair_gram/pallas_call | solution.py:164
  360.4 4.5 pair_gram.6
  365.6 6.2 %pair_gram.7 = (f32[256,256]{1,0:T(8,128)}, f32[256,128]{1,0:T(8,128)}, f32[32,256]{1,0:T(8,128)S(1)}, f32[32,256]{1,0:T(8,128)S(1)}, f32[32,256]{1,0:T(8,128)S(...) custom-call(f32[256,16384]{1,0:T(8,128)} %x_ref.7, ...), custom_call_target="tpu_custom_call" | custom-call | flops 1610612736 | bytes 8388608 | tf_op jit(solution)/shard_map/pair_gram/pallas_call | solution.py:164
  373.2 5.2 %collective-permute-done.20 = f32[32,256]{1,0:T(8,128)S(1)} collective-permute-done((f32[32,256]{1,0:T(8,128)S(1)}, f32[32,256]{1,0:T(8,128)S(1)}, u32[]{:S(2)}, u32[]{:S(2)}) %collective-permute-start.20) | collective-permute-done | bytes 32800 | tf_op jit(solution)/shard_map/ppermute | solution.py:185
  378.4 5.7 %collective-permute-done.21 = f32[32,256]{1,0:T(8,128)S(1)} collective-permute-done((f32[32,256]{1,0:T(8,128)S(1)}, f32[32,256]{1,0:T(8,128)S(1)}, u32[]{:S(2)}, u32[]{:S(2)}) %collective-permute-start.21) | collective-permute-done | bytes 32800 | tf_op jit(solution)/shard_map/ppermute | solution.py:185
  384.1 5.7 %collective-permute-done.22 = f32[32,256]{1,0:T(8,128)S(1)} collective-permute-done((f32[32,256]{1,0:T(8,128)S(1)}, f32[32,256]{1,0:T(8,128)S(1)}, u32[]{:S(2)}, u32[]{:S(2)}) %collective-permute-start.22) | collective-permute-done | bytes 32800 | tf_op jit(solution)/shard_map/ppermute | solution.py:185
  389.8 4.8 collective-permute-done.23
  394.6 4.8 collective-permute-done.24
  408.0 5.7 %collective-permute-done.16.refs_2_ = f32[8,128]{1,0:T(8,128)S(1)} collective-permute-done((f32[8,128]{1,0:T(8,128)S(1)}, f32[8,128]{1,0:T(8,128)S(1)}, u32[]{:S(2)}, u32[]{:S(2)}) %collective-permute-start.16) | collective-permute-done | bytes 4128 | tf_op jit(solution)/shard_map/ppermute | solution.py:330
  426.4 3.8 collective-permute-start.30
  432.1 3.8 collective-permute-start.29
  440.9 4.1 collective-permute-done.28.refs_5_
  446.9 4.6 collective-permute-done.27.refs_4_
  452.0 8.3 %velocity.4.refs_0_ = f32[256,16384]{1,0:T(8,128)} custom-call(f32[256,16384]{1,0:T(8,128)} %x_ref.7, f32[256,16384]{1,0:T(8,128)} %s_ref.7, f32[256,4096]{1,0:T(8,128)S(1)} %collective-permute-done.19.refs_1_.other_x, f32[256,4096]{1,0:T(8,128)S(1)} %collective-permute-done.36.other_s, bf16[256,256]{1,0:T(8,128)(2,1)S(1)} %get-tuple-element.92.own_hi, ...), custom_call_target="tpu_custom_call" | custom-call | flops 3221225472 | bytes 20971520 | tf_op jit(solution)/shard_map/velocity/pallas_call | solution.py:272
  460.4 9.9 %velocity.5.refs_0_ = f32[256,16384]{1,0:T(8,128)} custom-call(f32[256,16384]{1,0:T(8,128)} %x_ref.7, f32[256,16384]{1,0:T(8,128)} %s_ref.7, f32[256,4096]{1,0:T(8,128)} %collective-permute-done.18.refs_1_.other_x, f32[256,4096]{1,0:T(8,128)} %collective-permute-done.35.other_s, ...), custom_call_target="tpu_custom_call", output_to_operand_aliasing={{}: (10, {})} | custom-call | flops 3221225472 | bytes 20971520 | tf_op jit(solution)/shard_map/velocity/pallas_call | solution.py:272
  470.2 9.0 %velocity.6.refs_0_ = f32[256,16384]{1,0:T(8,128)} custom-call(f32[256,16384]{1,0:T(8,128)} %x_ref.7, f32[256,16384]{1,0:T(8,128)} %s_ref.7, f32[256,4096]{1,0:T(8,128)S(1)} %collective-permute-done.17.refs_1_.other_x, f32[256,4096]{1,0:T(8,128)} %collective-permute-done.34.other_s, ...), custom_call_target="tpu_custom_call", output_to_operand_aliasing={{}: (10, {})} | custom-call | flops 3221225472 | bytes 20971520 | tf_op jit(solution)/shard_map/velocity/pallas_call | solution.py:272
  479.3 9.9 %velocity.7 = f32[256,16384]{1,0:T(8,128)} custom-call(f32[256,16384]{1,0:T(8,128)} %x_ref.7, f32[256,16384]{1,0:T(8,128)} %s_ref.7, f32[256,4096]{1,0:T(8,128)} %collective-permute-done.refs_1_.other_x, f32[256,4096]{1,0:T(8,128)} %collective-permute-done.1.other_s, bf16[256,256]{1,0:T(8,128)(2,1)S(1)} %get-tuple-element.92.own_hi, ...), custom_call_target="tpu_custom_call", output_to_operand_aliasing={{}: (10, {})} | custom-call | flops 3221225472 | bytes 20971520 | tf_op jit(solution)/shard_map/velocity/pallas_call | solution.py:272
  (63 shorter events, 64.1 us)
Async XLA Ops:
  15.8 333.8 %collective-permute-start.17 = (f32[256,4096]{1,0:T(8,128)}, f32[256,4096]{1,0:T(8,128)S(1)}, u32[]{:S(2)}, u32[]{:S(2)}) collective-permute-start(f32[256,4096]{1,0:T(8,128)} %get-tuple-element.75), channel_id=1, source_target_pairs={{0,1},{1,0},{2,3},{3,2},{4,5},{5,4},{6,7},{7,6},{8,9},{9,8},{10,11... | collective-permute-start | bytes 12582920 | tf_op jit(solution)/shard_map/ppermute | solution.py:312
  16.2 333.9 %collective-permute-start.18 = (f32[256,4096]{1,0:T(8,128)}, f32[256,4096]{1,0:T(8,128)}, u32[]{:S(2)}, u32[]{:S(2)}) collective-permute-start(f32[256,4096]{1,0:T(8,128)} %get-tuple-element.76), channel_id=1, source_target_pairs={{0,1},{1,0},{2,3},{3,2},{4,5},{5,4},{6,7},{7,6},{8,9},{9,8},{10,11... | collective-permute-start | bytes 12582920 | tf_op jit(solution)/shard_map/ppermute | solution.py:312
  16.3 333.9 %collective-permute-start.19 = (f32[256,4096]{1,0:T(8,128)}, f32[256,4096]{1,0:T(8,128)S(1)}, u32[]{:S(2)}, u32[]{:S(2)}) collective-permute-start(f32[256,4096]{1,0:T(8,128)} %get-tuple-element.77), channel_id=1, source_target_pairs={{0,1},{1,0},{2,3},{3,2},{4,5},{5,4},{6,7},{7,6},{8,9},{9,8},{10,11... | collective-permute-start | bytes 12582920 | tf_op jit(solution)/shard_map/ppermute | solution.py:312
  23.0 341.9 %collective-permute-start = (f32[256,4096]{1,0:T(8,128)}, f32[256,4096]{1,0:T(8,128)}, u32[]{:S(2)}, u32[]{:S(2)}) collective-permute-start(f32[256,4096]{1,0:T(8,128)} %get-tuple-element.62), channel_id=1, source_target_pairs={{0,1},{1,0},{2,3},{3,2},{4,5},{5,4},{6,7},{7,6},{8,9},{9,8},{10,11... | collective-permute-start | bytes 12582920 | tf_op jit(solution)/shard_map/ppermute | solution.py:312
  23.1 7.9 %collective-permute-start.2 = (f32[32,256]{1,0:T(8,128)S(1)}, f32[32,256]{1,0:T(8,128)S(1)}, u32[]{:S(2)}, u32[]{:S(2)}) collective-permute-start(f32[32,256]{1,0:T(8,128)S(1)} %get-tuple-element.65), channel_id=1, source_target_pairs={{0,2},{2,4},{4,6},{6,8},{8,10},{10,12},{12,14},{14,0},{1,3},{3,5},... | collective-permute-start | bytes 98312 | tf_op jit(solution)/shard_map/ppermute | solution.py:185
  31.0 5.7 %collective-permute-start.3 = (f32[32,256]{1,0:T(8,128)S(1)}, f32[32,256]{1,0:T(8,128)S(1)}, u32[]{:S(2)}, u32[]{:S(2)}) collective-permute-start(f32[32,256]{1,0:T(8,128)S(1)} %get-tuple-element.66), channel_id=1, source_target_pairs={{0,4},{2,6},{4,8},{6,10},{8,12},{10,14},{12,0},{14,2},{1,5},{3,7},... | collective-permute-start | bytes 98312 | tf_op jit(solution)/shard_map/ppermute | solution.py:185
  36.7 6.0 %collective-permute-start.4 = (f32[32,256]{1,0:T(8,128)S(1)}, f32[32,256]{1,0:T(8,128)S(1)}, u32[]{:S(2)}, u32[]{:S(2)}) collective-permute-start(f32[32,256]{1,0:T(8,128)S(1)} %get-tuple-element.67), channel_id=1, source_target_pairs={{0,6},{2,8},{4,10},{6,12},{8,14},{10,0},{12,2},{14,4},{1,7},{3,9},... | collective-permute-start | bytes 98312 | tf_op jit(solution)/shard_map/ppermute | solution.py:185
  42.7 4.8 collective-permute-start.5
  47.5 4.8 collective-permute-start.6
  52.3 4.4 collective-permute-start.7
  60.6 6.0 %collective-permute-start.15 = (f32[32,256]{1,0:T(8,128)S(1)}, f32[32,256]{1,0:T(8,128)S(1)}, u32[]{:S(2)}, u32[]{:S(2)}) collective-permute-start(f32[32,256]{1,0:T(8,128)S(1)} %add_add_fusion.1.refs_0_), channel_id=1, source_target_pairs={{0,14},{2,0},{4,2},{6,4},{8,6},{10,8},{12,10},{14,12},{1,15},{3,1}... | collective-permute-start | bytes 98312 | tf_op jit(solution)/shard_map/ppermute | solution.py:191
  70.8 5.1 %collective-permute-start.13 = (f32[32,256]{1,0:T(8,128)S(1)}, f32[32,256]{1,0:T(8,128)S(1)}, u32[]{:S(2)}, u32[]{:S(2)}) collective-permute-start(f32[32,256]{1,0:T(8,128)S(1)} %add_add_fusion.1.refs_0_), channel_id=1, source_target_pairs={{0,10},{2,12},{4,14},{6,0},{8,2},{10,4},{12,6},{14,8},{1,11},{3,13... | collective-permute-start | bytes 98312 | tf_op jit(solution)/shard_map/ppermute | solution.py:191
  75.9 5.7 %collective-permute-start.12 = (f32[32,256]{1,0:T(8,128)S(1)}, f32[32,256]{1,0:T(8,128)S(1)}, u32[]{:S(2)}, u32[]{:S(2)}) collective-permute-start(f32[32,256]{1,0:T(8,128)S(1)} %add_add_fusion.1.refs_0_), channel_id=1, source_target_pairs={{0,8},{2,10},{4,12},{6,14},{8,0},{10,2},{12,4},{14,6},{1,9},{3,11}... | collective-permute-start | bytes 98312 | tf_op jit(solution)/shard_map/ppermute | solution.py:191
  81.7 5.7 %collective-permute-start.11 = (f32[32,256]{1,0:T(8,128)S(1)}, f32[32,256]{1,0:T(8,128)S(1)}, u32[]{:S(2)}, u32[]{:S(2)}) collective-permute-start(f32[32,256]{1,0:T(8,128)S(1)} %add_add_fusion.1.refs_0_), channel_id=1, source_target_pairs={{0,6},{2,8},{4,10},{6,12},{8,14},{10,0},{12,2},{14,4},{1,7},{3,9},... | collective-permute-start | bytes 98312 | tf_op jit(solution)/shard_map/ppermute | solution.py:191
  87.4 262.2 %collective-permute-start.10 = (f32[32,256]{1,0:T(8,128)S(1)}, f32[32,256]{1,0:T(8,128)S(1)}, u32[]{:S(2)}, u32[]{:S(2)}) collective-permute-start(f32[32,256]{1,0:T(8,128)S(1)} %add_add_fusion.1.refs_0_), channel_id=1, source_target_pairs={{0,4},{2,6},{4,8},{6,10},{8,12},{10,14},{12,0},{14,2},{1,5},{3,7},... | collective-permute-start | bytes 98312 | tf_op jit(solution)/shard_map/ppermute | solution.py:191
  349.6 102.4 %collective-permute-start.36 = (f32[256,4096]{1,0:T(8,128)}, f32[256,4096]{1,0:T(8,128)S(1)}, u32[]{:S(2)}, u32[]{:S(2)}) collective-permute-start(f32[256,4096]{1,0:T(8,128)} %get-tuple-element.100), channel_id=1, source_target_pairs={{0,1},{1,0},{2,3},{3,2},{4,5},{5,4},{6,7},{7,6},{8,9},{9,8},{10,11... | collective-permute-start | bytes 12582920 | tf_op jit(solution)/shard_map/ppermute | solution.py:312
  349.6 110.8 %collective-permute-start.35 = (f32[256,4096]{1,0:T(8,128)}, f32[256,4096]{1,0:T(8,128)}, u32[]{:S(2)}, u32[]{:S(2)}) collective-permute-start(f32[256,4096]{1,0:T(8,128)} %copy-done.1), channel_id=1, source_target_pairs={{0,1},{1,0},{2,3},{3,2},{4,5},{5,4},{6,7},{7,6},{8,9},{9,8},{10,11... | collective-permute-start | bytes 12582920 | tf_op jit(solution)/shard_map/ppermute | solution.py:312
  350.1 120.1 %collective-permute-start.34 = (f32[256,4096]{1,0:T(8,128)}, f32[256,4096]{1,0:T(8,128)}, u32[]{:S(2)}, u32[]{:S(2)}) collective-permute-start(f32[256,4096]{1,0:T(8,128)} %copy-done), channel_id=1, source_target_pairs={{0,1},{1,0},{2,3},{3,2},{4,5},{5,4},{6,7},{7,6},{8,9},{9,8},{10,11... | collective-permute-start | bytes 12582920 | tf_op jit(solution)/shard_map/ppermute | solution.py:312
  350.2 129.1 %collective-permute-start.1 = (f32[256,4096]{1,0:T(8,128)}, f32[256,4096]{1,0:T(8,128)}, u32[]{:S(2)}, u32[]{:S(2)}) collective-permute-start(f32[256,4096]{1,0:T(8,128)} %get-tuple-element.63), channel_id=1, source_target_pairs={{0,1},{1,0},{2,3},{3,2},{4,5},{5,4},{6,7},{7,6},{8,9},{9,8},{10,11... | collective-permute-start | bytes 12582920 | tf_op jit(solution)/shard_map/ppermute | solution.py:312
  364.9 6.8 %collective-permute-start.9 = (f32[32,256]{1,0:T(8,128)S(1)}, f32[32,256]{1,0:T(8,128)S(1)}, u32[]{:S(2)}, u32[]{:S(2)}) collective-permute-start(f32[32,256]{1,0:T(8,128)S(1)} %add_add_fusion.1.refs_0_), channel_id=1, source_target_pairs={{0,2},{2,4},{4,6},{6,8},{8,10},{10,12},{12,14},{14,0},{1,3},{3,5},... | collective-permute-start | bytes 98312 | tf_op jit(solution)/shard_map/ppermute | solution.py:191
  371.8 6.6 %collective-permute-start.20 = (f32[32,256]{1,0:T(8,128)S(1)}, f32[32,256]{1,0:T(8,128)S(1)}, u32[]{:S(2)}, u32[]{:S(2)}) collective-permute-start(f32[32,256]{1,0:T(8,128)S(1)} %get-tuple-element.85), channel_id=1, source_target_pairs={{0,2},{2,4},{4,6},{6,8},{8,10},{10,12},{12,14},{14,0},{1,3},{3,5},... | collective-permute-start | bytes 98312 | tf_op jit(solution)/shard_map/ppermute | solution.py:185
  378.4 5.7 %collective-permute-start.21 = (f32[32,256]{1,0:T(8,128)S(1)}, f32[32,256]{1,0:T(8,128)S(1)}, u32[]{:S(2)}, u32[]{:S(2)}) collective-permute-start(f32[32,256]{1,0:T(8,128)S(1)} %get-tuple-element.86), channel_id=1, source_target_pairs={{0,4},{2,6},{4,8},{6,10},{8,12},{10,14},{12,0},{14,2},{1,5},{3,7},... | collective-permute-start | bytes 98312 | tf_op jit(solution)/shard_map/ppermute | solution.py:185
  384.1 5.7 %collective-permute-start.22 = (f32[32,256]{1,0:T(8,128)S(1)}, f32[32,256]{1,0:T(8,128)S(1)}, u32[]{:S(2)}, u32[]{:S(2)}) collective-permute-start(f32[32,256]{1,0:T(8,128)S(1)} %get-tuple-element.87), channel_id=1, source_target_pairs={{0,6},{2,8},{4,10},{6,12},{8,14},{10,0},{12,2},{14,4},{1,7},{3,9},... | collective-permute-start | bytes 98312 | tf_op jit(solution)/shard_map/ppermute | solution.py:185
  389.8 4.8 collective-permute-start.23
  394.6 4.8 collective-permute-start.24
  399.4 4.6 collective-permute-start.25
  408.0 5.7 %collective-permute-start.16 = (f32[8,128]{1,0:T(8,128)S(1)}, f32[8,128]{1,0:T(8,128)S(1)}, u32[]{:S(2)}, u32[]{:S(2)}) collective-permute-start(f32[8,128]{1,0:T(8,128)S(1)} %get-tuple-element.73.refs_1_), channel_id=1, source_target_pairs={{0,3},{1,2},{2,5},{3,4},{4,7},{5,6},{6,9},{7,8},{8,11},{9,10},{10,... | collective-permute-start | bytes 12296 | tf_op jit(solution)/shard_map/ppermute | solution.py:330
  421.5 4.8 collective-permute-start.31
  426.4 5.7 %collective-permute-start.30 = (f32[32,256]{1,0:T(8,128)S(1)}, f32[32,256]{1,0:T(8,128)S(1)}, u32[]{:S(2)}, u32[]{:S(2)}) collective-permute-start(f32[32,256]{1,0:T(8,128)S(1)} %add_add_fusion.refs_3_), channel_id=1, source_target_pairs={{0,8},{2,10},{4,12},{6,14},{8,0},{10,2},{12,4},{14,6},{1,9},{3,11}... | collective-permute-start | bytes 98312 | tf_op jit(solution)/shard_map/ppermute | solution.py:191
  432.1 5.7 %collective-permute-start.29 = (f32[32,256]{1,0:T(8,128)S(1)}, f32[32,256]{1,0:T(8,128)S(1)}, u32[]{:S(2)}, u32[]{:S(2)}) collective-permute-start(f32[32,256]{1,0:T(8,128)S(1)} %add_add_fusion.refs_3_), channel_id=1, source_target_pairs={{0,6},{2,8},{4,10},{6,12},{8,14},{10,0},{12,2},{14,4},{1,7},{3,9},... | collective-permute-start | bytes 98312 | tf_op jit(solution)/shard_map/ppermute | solution.py:191
  437.8 7.2 %collective-permute-start.28 = (f32[32,256]{1,0:T(8,128)S(1)}, f32[32,256]{1,0:T(8,128)S(1)}, u32[]{:S(2)}, u32[]{:S(2)}) collective-permute-start(f32[32,256]{1,0:T(8,128)S(1)} %add_add_fusion.refs_3_), channel_id=1, source_target_pairs={{0,4},{2,6},{4,8},{6,10},{8,12},{10,14},{12,0},{14,2},{1,5},{3,7},... | collective-permute-start | bytes 98312 | tf_op jit(solution)/shard_map/ppermute | solution.py:191
  444.9 6.6 %collective-permute-start.27 = (f32[32,256]{1,0:T(8,128)S(1)}, f32[32,256]{1,0:T(8,128)S(1)}, u32[]{:S(2)}, u32[]{:S(2)}) collective-permute-start(f32[32,256]{1,0:T(8,128)S(1)} %add_add_fusion.refs_3_), channel_id=1, source_target_pairs={{0,2},{2,4},{4,6},{6,8},{8,10},{10,12},{12,14},{14,0},{1,3},{3,5},... | collective-permute-start | bytes 98312 | tf_op jit(solution)/shard_map/ppermute | solution.py:191
  (7 other events, 23.9 us)

commit v2 on v0

v2 whole, which is shorter than its diff:
```python
import math

import jax
import jax.numpy as jnp
from jax import lax
from jax.sharding import PartitionSpec as P


def dot3(left, right):
    return jnp.dot(left, right, precision=lax.Precision.HIGH, preferred_element_type=jnp.float32)


def total_over_dim(block):
    count = lax.axis_size("dim")
    rows, columns = block.shape
    parts = block.reshape(count, rows // count, columns)
    arrived = lax.all_to_all(parts, "dim", 0, 0)
    total = jnp.sum(arrived, axis=0)
    copies = jnp.broadcast_to(total[None], arrived.shape)
    return lax.all_to_all(copies, "dim", 0, 0).reshape(rows, columns)


def swap(array):
    return lax.ppermute(array, "blk", [(0, 1), (1, 0)])


def body(particles, scores):
    rows = particles.shape[0]
    count = lax.axis_size("dim")
    total_rows = rows * lax.axis_size("blk")
    scale_base = total_rows * total_rows * math.log(total_rows)

    visitor = swap(particles)
    visitor_scores = swap(scores)

    diagonal = lax.broadcasted_iota(jnp.int32, (rows, rows), 0) == lax.broadcasted_iota(jnp.int32, (rows, rows), 1)
    norms = jnp.sum(particles * particles, axis=1)
    own = norms[:, None] + norms[None, :] - 2.0 * dot3(particles, particles.T)
    own = total_over_dim(jnp.where(diagonal, norms[:, None], own))
    norms = jnp.sum(jnp.where(diagonal, own, 0.0), axis=1)
    own = jnp.where(diagonal, 0.0, own)
    summary = jnp.stack([norms, jnp.full((rows,), jnp.sum(own))])
    across = [(d * 2 + b, (d + 1) % count * 2 + 1 - b) for d in range(count) for b in range(2)]
    other = lax.ppermute(summary, ("dim", "blk"), across)

    visitor, other = lax.optimization_barrier((visitor, other))
    gram = total_over_dim(dot3(particles, visitor.T))
    pair = norms[:, None] + other[0][None, :] - 2.0 * gram

    width = (summary[1, 0] + other[1, 0] + 2.0 * jnp.sum(pair)) / scale_base
    own_weights = jnp.where(diagonal, 0.0, jnp.exp(-own / width))
    pair_weights = jnp.exp(-pair / width)
    weight = jnp.sum(own_weights, axis=1) + jnp.sum(pair_weights, axis=1)
    half = 0.5 * width
    weights = jnp.concatenate([own_weights, pair_weights], axis=1)
    moved = jnp.concatenate([half * scores - particles, half * visitor_scores - visitor], axis=0)
    return half * scores + particles * weight[:, None] + dot3(weights, moved)


def solution(mesh):
    return jax.shard_map(
        body,
        mesh=mesh,
        in_specs=(P(("grp", "blk"), "dim"), P(("grp", "blk"), "dim")),
        out_specs=P(("grp", "blk"), "dim"),
        check_vma=False,
    )
```

time: 218 us -> 174 us (0.80)
  matrix products: 110 us -> 69.6 us
  other arithmetic: 19.9 us -> 44.5 us
  waiting for transfers between devices: 44.2 us -> 20.3 us
  between operations: 16 us -> 2.02 us
  starting transfers between devices: 0.55 us -> 7.75 us
  local copies, waits for them, and re-layouts: 0.01 us -> 2.9 us
    psum x2 -> x0, waiting for transfers between devices: 44.2 us -> none  [the longest x1 44.2 us: body(): distance = lax.psum(stacked, 'dim')]
    dot_general x4 -> x3, matrix products: 110 us -> 69.6 us  [dot3(): jnp.dot(left, right, precision=lax.Precision.HIGH, preferred_element_type...]
    sub x0 -> x2, other arithmetic: none -> 35.5 us  [the longest x1 17.7 us: body(): half * visitor_scores - visitor]
    psum x2 -> x0, blocking collectives: 26.8 us -> none  [the longest x1 23.8 us: body(): spread = lax.psum(local_part, 'dim')]
    all_to_all x0 -> x2, blocking collectives: none -> 26.8 us  [total_over_dim(): arrived = lax.all_to_all(parts, 'dim', 0, 0)]
    all_to_all x0 -> x2, waiting for transfers between devices: none -> 14.6 us  [total_over_dim(): return lax.all_to_all(copies, 'dim', 0, 0).reshape(rows, columns)]
    reduce_sum x4 -> x5, other arithmetic: 19.1 us -> 8.15 us  [the longest x1 7 us: body(): norms = jnp.sum(particles * particles, axis=1)]
    all_to_all x0 -> x2, starting transfers between devices: none -> 7.18 us  [total_over_dim(): return lax.all_to_all(copies, 'dim', 0, 0).reshape(rows, columns)]
  transfers between devices with their start and end apart: 4 -> 5, of which waited for: 1 -> 3; matrix products, arithmetic and copies ran while one was open for 42% -> 39% of each run, Pallas kernels for 0% -> 0%
where the time goes in v2:
time: 174 us
  matrix products  69.6 us (40%)
  other arithmetic  44.5 us (26%)
  blocking collectives  26.8 us (15%)
  waiting for transfers between devices  20.3 us (12%)
  starting transfers between devices  7.75 us (4%)
  local copies, waits for them, and re-layouts  2.9 us (2%)
  between operations  2.02 us (1%)
    dot_general x3, matrix products, dot3(): jnp.dot(left, right, precision=lax.Precision.HIGH, preferred_element_type...  69.6 us
    all_to_all x2, blocking collectives, total_over_dim(): arrived = lax.all_to_all(parts, 'dim', 0, 0)  26.8 us
    sub x1, other arithmetic, body(): half * visitor_scores - visitor  17.7 us
    sub x1, other arithmetic, body(): half * scores - particles  17.7 us
    all_to_all x2, waiting for transfers between devices, total_over_dim(): return lax.all_to_all(copies, 'dim', 0, 0).reshape(rows, columns)  14.6 us
    all_to_all x2, starting transfers between devices, total_over_dim(): return lax.all_to_all(copies, 'dim', 0, 0).reshape(rows, columns)  7.18 us
    reduce_sum x1, other arithmetic, body(): norms = jnp.sum(particles * particles, axis=1)  7 us
    ppermute x1, waiting for transfers between devices, body(): other = lax.ppermute(summary, ('dim', 'blk'), across)  5.69 us
  transfers between devices with their start and end apart: 5, of which 3 were waited for; matrix products, arithmetic and copies ran while one was open for 39% of the time, Pallas kernels for 0%

profile of v2, /device:TPU:0, one launch (start us, length us, event | category | flops | bytes accessed | tf_op | source)
XLA Modules:
  0.0 173.9 jit_solution(7371298090828962776)
XLA Ops:
  0.0 0.5 collective-permute-start
  0.5 0.1 collective-permute-start.2
  0.5 7.0 %multiply_reduce_fusion = f32[256]{0:T(256)S(1)} fusion(f32[256,16384]{1,0:T(8,128)} %param.2), kind=kLoop, calls=%fused_computation.6 | loop fusion | flops 8388352 | bytes 16778240 | tf_op jit(solution)/shard_map/reduce_sum | solution.py:37
  7.5 13.5 %fusion.8 = f32[256,256]{1,0:T(8,128)S(1)} fusion(f32[256,16384]{1,0:T(8,128)} %param.2, f32[256]{0:T(256)S(1)} %multiply_reduce_fusion), kind=kOutput, calls=%fused_computation.10 | convolution fusion | flops 6442778624 | bytes 17040384 | tf_op jit(solution)/shard_map/dot_general | solution.py:10
  21.0 16.2 %all_to_all.20 = f32[8,32,256]{2,1,0:T(8,128)S(1)} all-to-all(f32[8,32,256]{2,1,0:T(8,128)S(1)} %bitcast.28), channel_id=1, replica_groups=mesh['grp'=2,'dim'=8,'blk'=2] {'dim'}, dimensions={0} | all-to-all | bytes 524288 | tf_op jit(solution)/shard_map/all_to_all | solution.py:17
  37.2 0.7 broadcast_in_dim.36
  37.9 3.6 %all-to-all-start.1 = ((f32[8,32,256]{2,1,0:T(8,128)}), f32[8,32,256]{2,1,0:T(8,128)S(1)}, u32[]{:S(2)}, u32[]{:S(2)}) async-start(f32[8,32,256]{2,1,0:T(8,128)} %broadcast_in_dim.36), calls=%async_computation.1 | async-start | bytes 524288 | tf_op jit(solution)/shard_map/all_to_all | solution.py:20
  41.5 8.6 %all-to-all-done.1 = f32[8,32,256]{2,1,0:T(8,128)S(1)} async-done(((f32[8,32,256]{2,1,0:T(8,128)}), f32[8,32,256]{2,1,0:T(8,128)S(1)}, u32[]{:S(2)}, u32[]{:S(2)}) %all-to-all-start.1) | async-done | bytes 262176 | tf_op jit(solution)/shard_map/all_to_all | solution.py:20
  50.0 0.8 fusion.20
  50.8 0.1 stack.6
  50.9 0.7 stack.7
  51.6 0.1 collective-permute-start.1
  51.7 5.7 %collective-permute-done.1 = f32[2,256]{1,0:T(2,128)S(1)} collective-permute-done((f32[2,256]{1,0:T(2,128)S(1)}, f32[2,256]{1,0:T(2,128)S(1)}, u32[]{:S(2)}, u32[]{:S(2)}) %collective-permute-start.1) | collective-permute-done | bytes 2080 | tf_op jit(solution)/shard_map/ppermute | solution.py:44
  57.4 0.0 collective-permute-done
  57.4 24.9 %fusion.23 = f32[256,256]{0,1:T(8,128)S(1)} fusion(f32[256,16384]{1,0:T(8,128)} %collective-permute-done, f32[256,16384]{1,0:T(8,128)} %param.2), kind=kOutput, calls=%fused_computation.35 | convolution fusion | flops 6442450944 | bytes 33816576 | tf_op jit(solution)/shard_map/dot_general | solution.py:10
  82.2 10.6 %all_to_all.21 = f32[8,32,256]{2,1,0:T(8,128)S(1)} all-to-all(f32[8,32,256]{2,1,0:T(8,128)S(1)} %bitcast.29), channel_id=1, replica_groups=mesh['grp'=2,'dim'=8,'blk'=2] {'dim'}, dimensions={0} | all-to-all | bytes 524288 | tf_op jit(solution)/shard_map/all_to_all | solution.py:17
  92.9 0.7 broadcast_in_dim.37
  93.6 3.6 %all-to-all-start.3 = ((f32[8,32,256]{2,1,0:T(8,128)}), f32[8,32,256]{2,1,0:T(8,128)S(1)}, u32[]{:S(2)}, u32[]{:S(2)}) async-start(f32[8,32,256]{2,1,0:T(8,128)} %broadcast_in_dim.37), calls=%async_computation.3 | async-start | bytes 524288 | tf_op jit(solution)/shard_map/all_to_all | solution.py:20
  97.2 0.1 add.77
  97.3 0.5 slice.7
  99.1 6.1 %all-to-all-done.3 = f32[8,32,256]{2,1,0:T(8,128)S(1)} async-done(((f32[8,32,256]{2,1,0:T(8,128)}), f32[8,32,256]{2,1,0:T(8,128)S(1)}, u32[]{:S(2)}, u32[]{:S(2)}) %all-to-all-start.3) | async-done | bytes 262176 | tf_op jit(solution)/shard_map/all_to_all | solution.py:20
  105.2 0.7 broadcast_multiply_fusion
  106.6 0.3 exponential_reduce_fusion
  106.9 0.1 add.75
  107.0 17.7 %multiply_subtract_fusion.1 = f32[256,16384]{1,0:T(8,128)} fusion(f32[256,16384]{1,0:T(8,128)} %param.2, f32[256,16384]{1,0:T(8,128)} %param.3, f32[]{:T(128)S(6)} %mul_shard_map.3), kind=kLoop, calls=%fused_computation.7 | loop fusion | flops 8388608 | bytes 50331652 | tf_op jit(solution)/shard_map/sub | solution.py:56
  124.7 0.0 collective-permute-done.2
  124.7 17.7 %multiply_subtract_fusion = f32[256,16384]{1,0:T(8,128)} fusion(f32[256,16384]{1,0:T(8,128)} %collective-permute-done, f32[256,16384]{1,0:T(8,128)} %collective-permute-done.2, f32[]{:T(128)S(6)} %mul_shard_map.3), kind=kLoop, calls=%fused_computation.5 | loop fusion | flops 8388608 | bytes 50331652 | tf_op jit(solution)/shard_map/sub | solution.py:56
  142.5 0.2 fusion.14
  142.7 31.3 %fusion.4 = f32[256,16384]{1,0:T(8,128)} fusion(f32[256,16384]{1,0:T(8,128)} %multiply_subtract_fusion, f32[256,16384]{1,0:T(8,128)} %multiply_subtract_fusion.1, f32[256,16384]{1,0:T(8,128)} %param.2, f32[256,16384]{1,0:T(8,128)} %param.3, f32[256]{0:T(256)S(1)} %add.75, f32[]{:T(128)S(6)} %mul_shard_map.3, f32[256,256]{1,0:T(8,128)S(1)} %get-tuple-element.13, ...), kind=kOutput, calls=%fused_computation.4 | convolution fusion | flops 12910198784 | bytes 84411392 | tf_op jit(solution)/shard_map/dot_general | solution.py:10
  (5 shorter events, 0.1 us)
Async XLA Ops:
  0.0 57.4 %collective-permute-start = (f32[256,16384]{1,0:T(8,128)}, f32[256,16384]{1,0:T(8,128)}, u32[]{:S(2)}, u32[]{:S(2)}) collective-permute-start(f32[256,16384]{1,0:T(8,128)} %param.2), channel_id=1, source_target_pairs={{0,1},{1,0},{2,3},{3,2},{4,5},{5,4},{6,7},{7,6},{8,9},{9,8},{10,11... | collective-permute-start | bytes 50331656 | tf_op jit(solution)/shard_map/ppermute | solution.py:24
  0.5 124.3 %collective-permute-start.2 = (f32[256,16384]{1,0:T(8,128)}, f32[256,16384]{1,0:T(8,128)}, u32[]{:S(2)}, u32[]{:S(2)}) collective-permute-start(f32[256,16384]{1,0:T(8,128)} %param.3), channel_id=1, source_target_pairs={{0,1},{1,0},{2,3},{3,2},{4,5},{5,4},{6,7},{7,6},{8,9},{9,8},{10,11... | collective-permute-start | bytes 50331656 | tf_op jit(solution)/shard_map/ppermute | solution.py:24
  37.9 12.2 %all-to-all-start.1 = ((f32[8,32,256]{2,1,0:T(8,128)}), f32[8,32,256]{2,1,0:T(8,128)S(1)}, u32[]{:S(2)}, u32[]{:S(2)}) async-start(f32[8,32,256]{2,1,0:T(8,128)} %broadcast_in_dim.36), calls=%async_computation.1 | async-start | bytes 524288 | tf_op jit(solution)/shard_map/all_to_all | solution.py:20
  51.6 5.8 %collective-permute-start.1 = (f32[2,256]{1,0:T(2,128)S(1)}, f32[2,256]{1,0:T(2,128)S(1)}, u32[]{:S(2)}, u32[]{:S(2)}) collective-permute-start(f32[2,256]{1,0:T(2,128)S(1)} %stack.7), channel_id=1, source_target_pairs={{0,3},{1,2},{2,5},{3,4},{4,7},{5,6},{6,9},{7,8},{8,11},{9,10},{10,... | collective-permute-start | bytes 6152 | tf_op jit(solution)/shard_map/ppermute | solution.py:44
  93.6 11.6 %all-to-all-start.3 = ((f32[8,32,256]{2,1,0:T(8,128)}), f32[8,32,256]{2,1,0:T(8,128)S(1)}, u32[]{:S(2)}, u32[]{:S(2)}) async-start(f32[8,32,256]{2,1,0:T(8,128)} %broadcast_in_dim.37), calls=%async_computation.3 | async-start | bytes 524288 | tf_op jit(solution)/shard_map/all_to_all | solution.py:20

commit v3 on v2

v3 whole, which is shorter than its diff:
```python
import functools
import math

import jax
import jax.numpy as jnp
from jax import lax
from jax.experimental import pallas as pl
from jax.experimental.pallas import tpu as pltpu
from jax.sharding import PartitionSpec as P

GRAM_TILE = 2048
VELOCITY_TILE = 1024
MIB = 1024 * 1024


def params(limit):
    return pltpu.CompilerParams(vmem_limit_bytes=limit * MIB)


def split(x):
    hi = x.astype(jnp.bfloat16)
    lo = (x - hi.astype(jnp.float32)).astype(jnp.bfloat16)
    return hi, lo


def nt_dot(left, right):
    return lax.dot_general(left, right, (((1,), (1,)), ((), ())), preferred_element_type=jnp.float32)


def nn_dot(left, right):
    return jnp.dot(left, right, preferred_element_type=jnp.float32)


def lane_sums(values):
    total = values[:, :128]
    for start in range(128, values.shape[1], 128):
        total = total + values[:, start:start + 128]
    return total


def whole(array):
    return pl.BlockSpec(array.shape, lambda i: (0,) * len(array.shape))


def f32(*shape):
    return jax.ShapeDtypeStruct(shape, jnp.float32)


def on_diagonal(rows):
    return lax.broadcasted_iota(jnp.int32, (rows, rows), 0) == lax.broadcasted_iota(jnp.int32, (rows, rows), 1)


def own_kernel(x_ref, out_ref, gram_ref, squares_ref):
    @pl.when(pl.program_id(0) == 0)
    def _():
        gram_ref[...] = jnp.zeros_like(gram_ref)
        squares_ref[...] = jnp.zeros_like(squares_ref)

    x = x_ref[...]
    hi, lo = split(x)
    gram_ref[...] += nt_dot(jnp.concatenate([hi, lo], axis=0), hi)
    squares_ref[...] += lane_sums(x * x)

    @pl.when(pl.program_id(0) == pl.num_programs(0) - 1)
    def _():
        rows = out_ref.shape[0]
        mixed = gram_ref[rows:, :]
        gram = gram_ref[:rows, :] + mixed + mixed.T
        norms = jnp.sum(squares_ref[...], axis=1, keepdims=True)
        out_ref[...] = jnp.where(on_diagonal(rows), norms, norms + norms.T - 2.0 * gram)


def own_part(particles):
    rows, columns = particles.shape
    tile = min(GRAM_TILE, columns)
    out = f32(rows, rows)
    return pl.pallas_call(
        own_kernel,
        grid=(columns // tile,),
        in_specs=[pl.BlockSpec((rows, tile), lambda i: (0, i))],
        out_specs=whole(out),
        out_shape=out,
        scratch_shapes=[pltpu.VMEM((2 * rows, rows), jnp.float32), pltpu.VMEM((rows, 128), jnp.float32)],
        compiler_params=params(20),
        cost_estimate=pl.CostEstimate(flops=4 * rows * rows * columns, bytes_accessed=4 * rows * columns, transcendentals=0),
        name="own_gram",
    )(particles)


def pair_kernel(mine_ref, other_ref, gram_ref):
    @pl.when(pl.program_id(0) == 0)
    def _():
        gram_ref[...] = jnp.zeros_like(gram_ref)

    rows = gram_ref.shape[0]
    my_hi, my_lo = split(mine_ref[...])
    hi, lo = split(other_ref[...])
    both = nt_dot(jnp.concatenate([my_hi, my_lo], axis=0), hi)
    gram_ref[...] += both[:rows] + both[rows:] + nt_dot(my_hi, lo)


def pair_part(particles, visitor):
    rows, columns = particles.shape
    tile = min(GRAM_TILE, columns)
    out = f32(rows, rows)
    block = pl.BlockSpec((rows, tile), lambda i: (0, i))
    return pl.pallas_call(
        pair_kernel,
        grid=(columns // tile,),
        in_specs=[block, block],
        out_specs=whole(out),
        out_shape=out,
        compiler_params=params(24),
        cost_estimate=pl.CostEstimate(flops=6 * rows * rows * columns, bytes_accessed=8 * rows * columns, transcendentals=0),
        name="pair_gram",
    )(particles, visitor)


def sum_kernel(arrived_ref, out_ref):
    total = arrived_ref[0]
    for step in range(1, arrived_ref.shape[0]):
        total = total + arrived_ref[step]
    for step in range(out_ref.shape[0]):
        out_ref[step] = total


def summed_shards(block):
    count = lax.axis_size("dim")
    rows, columns = block.shape
    arrived = lax.all_to_all(block.reshape(count, rows // count, columns), "dim", 0, 0)
    return pl.pallas_call(sum_kernel, out_shape=f32(*arrived.shape), compiler_params=params(8), name="sum_shards")(arrived)


def gathered(copies):
    count, rows, columns = copies.shape
    return lax.all_to_all(copies, "dim", 0, 0).reshape(count * rows, columns)


def summary_kernel(own_ref, out_ref):
    own = own_ref[...]
    rows = own.shape[0]
    diagonal = on_diagonal(rows)
    norms = jnp.sum(jnp.where(diagonal, own, 0.0), axis=0, keepdims=True)
    total = jnp.sum(jnp.where(diagonal, 0.0, own))
    out_ref[...] = jnp.concatenate([norms, jnp.full((7, rows), total)], axis=0)


def summary_part(own):
    return pl.pallas_call(summary_kernel, out_shape=f32(8, own.shape[0]), compiler_params=params(8), name="summary")(own)


def weights_kernel(scale_base, own_ref, summary_ref, other_ref, gram_ref, hi_ref, lo_ref, weight_ref, half_ref):
    own = own_ref[...]
    rows = own.shape[0]
    diagonal = on_diagonal(rows)
    norms = jnp.sum(jnp.where(diagonal, own, 0.0), axis=1, keepdims=True)
    pair = norms + other_ref[0:1, :] - 2.0 * gram_ref[...]
    spread = summary_ref[1:2, 0:1] + other_ref[1:2, 0:1] + 2.0 * jnp.sum(pair)
    width = spread / scale_base
    inverse = -1.0 / width
    own_weights = jnp.where(diagonal, 0.0, jnp.exp(own * inverse))
    pair_weights = jnp.exp(pair * inverse)
    weights = jnp.concatenate([own_weights, pair_weights], axis=1)
    hi_ref[...], lo_ref[...] = split(weights)
    weight_ref[...] = jnp.broadcast_to(jnp.sum(weights, axis=1, keepdims=True), weight_ref.shape)
    half_ref[...] = jnp.broadcast_to(0.5 * width, half_ref.shape)


def weights_part(own, summary, other, gram, scale_base):
    rows = own.shape[0]
    half = jax.ShapeDtypeStruct((rows, 2 * rows), jnp.bfloat16)
    return pl.pallas_call(
        functools.partial(weights_kernel, scale_base),
        out_shape=[half, half, f32(rows, 128), f32(8, 128)],
        compiler_params=params(12),
        name="kernel_weights",
    )(own, summary, other, gram)


def velocity_kernel(x_ref, s_ref, other_x, other_s, hi_ref, lo_ref, weight_ref, half_ref, out_ref):
    half = half_ref[0:1, 0:1]
    x = x_ref[...]
    driven = half * s_ref[...]
    moved_hi, moved_lo = split(jnp.concatenate([driven - x, half * other_s[...] - other_x[...]], axis=0))
    hi = hi_ref[...]
    left = jnp.concatenate([hi, hi, lo_ref[...]], axis=1)
    right = jnp.concatenate([moved_hi, moved_lo, moved_hi], axis=0)
    out_ref[...] = driven + weight_ref[:, 0:1] * x + nn_dot(left, right)


def velocity_part(particles, scores, visitor, visitor_scores, weights):
    rows, columns = particles.shape
    tile = min(VELOCITY_TILE, columns)
    block = pl.BlockSpec((rows, tile), lambda i: (0, i))
    return pl.pallas_call(
        velocity_kernel,
        grid=(columns // tile,),
        in_specs=[block] * 4 + [whole(w) for w in weights],
        out_specs=block,
        out_shape=f32(rows, columns),
        compiler_params=params(28),
        cost_estimate=pl.CostEstimate(flops=12 * rows * rows * columns, bytes_accessed=20 * rows * columns, transcendentals=0),
        name="velocity",
    )(particles, scores, visitor, visitor_scores, *weights)


def swap(array):
    return lax.ppermute(array, "blk", [(0, 1), (1, 0)])


def body(particles, scores):
    count = lax.axis_size("dim")
    total_rows = particles.shape[0] * lax.axis_size("blk")
    scale_base = total_rows * total_rows * math.log(total_rows)

    visitor = swap(particles)
    visitor_scores = swap(scores)

    own_copies = summed_shards(own_part(particles))
    visitor, own_copies = lax.optimization_barrier((visitor, own_copies))
    own = gathered(own_copies)
    summary = summary_part(own)
    across = [(d * 2 + b, (d + 1) % count * 2 + 1 - b) for d in range(count) for b in range(2)]
    other = lax.ppermute(summary, ("dim", "blk"), across)

    gram = pair_part(particles, visitor)
    gram, summary = lax.optimization_barrier((gram, summary))
    gram = gathered(summed_shards(gram))
    weights = weights_part(own, summary, other, gram, scale_base)
    return velocity_part(particles, scores, visitor, visitor_scores, weights)


def solution(mesh):
    return jax.shard_map(
        body,
        mesh=mesh,
        in_specs=(P(("grp", "blk"), "dim"), P(("grp", "blk"), "dim")),
        out_specs=P(("grp", "blk"), "dim"),
        check_vma=False,
    )
```

time: 174 us -> 117 us (0.67)
  matrix products: 69.6 us -> 0 us
  Pallas kernels: 0 us -> 53.2 us
  other arithmetic: 44.5 us -> 0 us
  local copies, waits for them, and re-layouts: 2.9 us -> 17.3 us
  waiting for transfers between devices: 20.3 us -> 8.17 us
  blocking collectives: 26.8 us -> 30.2 us
  between operations: 2.02 us -> 0.05 us
    dot_general x3 -> x0, matrix products: 69.6 us -> none  [dot3(): jnp.dot(left, right, precision=lax.Precision.HIGH, preferred_element_type...]
    pallas_call x0 -> x7, Pallas kernels: none -> 53.2 us  [the longest x1 30.6 us: velocity_part(): pl.pallas_call(velocity_kernel, grid=(columns // tile,), in_specs=[block]...]
    sub x2 -> x0, other arithmetic: 35.5 us -> none  [the longest x1 17.7 us: body(): half * visitor_scores - visitor]
    unnamed x0 -> x6, local copies, waits for them, and re-layouts: none -> 17.3 us
    all_to_all x2, waiting for transfers between devices: 14.6 us -> 1.76 us  [gathered(): return lax.all_to_all(copies, 'dim', 0, 0).reshape(count * rows, columns)]
    reduce_sum x5 -> x0, other arithmetic: 8.15 us -> none  [the longest x1 7 us: body(): norms = jnp.sum(particles * particles, axis=1)]
    all_to_all x2, blocking collectives: 26.8 us -> 30.2 us  [summed_shards(): lax.all_to_all(block.reshape(count, rows // count, columns), 'dim', 0, 0)]
  transfers between devices with their start and end apart: 5 -> 5, of which waited for: 3 -> 2; matrix products, arithmetic and copies ran while one was open for 39% -> 0% of each run, Pallas kernels for 0% -> 19%
where the time goes in v3:
time: 117 us
  Pallas kernels  53.2 us (45%)
  blocking collectives  30.2 us (26%)
  local copies, waits for them, and re-layouts  17.3 us (15%)
  waiting for transfers between devices  8.17 us (7%)
  starting transfers between devices  7.68 us (7%)
    pallas_call x1, Pallas kernels, velocity_part(): pl.pallas_call(velocity_kernel, grid=(columns // tile,), in_specs=[block]...  30.6 us
    all_to_all x2, blocking collectives, summed_shards(): lax.all_to_all(block.reshape(count, rows // count, columns), 'dim', 0, 0)  30.2 us
    unnamed x6, local copies, waits for them, and re-layouts  17.3 us
    pallas_call x1, Pallas kernels, pair_part(): pl.pallas_call(pair_kernel, grid=(columns // tile,), in_specs=[block, blo...  12.5 us
    pallas_call x1, Pallas kernels, own_part(): pl.pallas_call(own_kernel, grid=(columns // tile,), in_specs=[pl.BlockSpe...  7.88 us
    all_to_all x2, starting transfers between devices, gathered(): return lax.all_to_all(copies, 'dim', 0, 0).reshape(count * rows, columns)  7 us
    ppermute x1, waiting for transfers between devices, body(): other = lax.ppermute(summary, ('dim', 'blk'), across)  6.41 us
  transfers between devices with their start and end apart: 5, of which 2 were waited for; matrix products, arithmetic and copies ran while one was open for 0% of the time, Pallas kernels for 19%

profile of v3, /device:TPU:0, one launch (start us, length us, event | category | flops | bytes accessed | tf_op | source)
XLA Modules:
  0.0 116.6 jit_solution(467043344757226196)
XLA Ops:
  0.0 0.5 collective-permute-start
  0.5 0.1 collective-permute-start.1
  0.5 0.0 copy-start
  0.5 5.8 %copy-done = f32[256,16384]{1,0:T(8,128)S(1)} copy-done((f32[256,16384]{1,0:T(8,128)S(1)}, f32[256,16384]{1,0:T(8,128)}, u32[]{:S(2)}) %copy-start) | copy-done | bytes 16777240
  6.3 7.9 %own_gram.1 = f32[256,256]{1,0:T(8,128)S(1)} custom-call(f32[256,16384]{1,0:T(8,128)S(1)} %copy-done), custom_call_target="tpu_custom_call" | custom-call | flops 4294967296 | bytes 16777216 | tf_op jit(solution)/shard_map/own_gram/pallas_call | solution.py:77
  14.2 16.2 %all_to_all.20.arrived_ref = f32[8,32,256]{2,1,0:T(8,128)S(1)} all-to-all(f32[8,32,256]{2,1,0:T(8,128)S(1)} %bitcast.7), channel_id=1, replica_groups=mesh['grp'=2,'dim'=8,'blk'=2] {'dim'}, dimensions={0} | all-to-all | bytes 524288 | tf_op jit(solution)/shard_map/all_to_all | solution.py:130
  30.3 0.7 sum_shards.2
  31.1 0.0 collective-permute-done.other_ref.other_x
  31.1 3.6 %all-to-all-start.1 = ((f32[8,32,256]{2,1,0:T(8,128)}), f32[8,32,256]{2,1,0:T(8,128)S(1)}, u32[]{:S(2)}, u32[]{:S(2)}) async-start(f32[8,32,256]{2,1,0:T(8,128)} %sum_shards.2), calls=%async_computation.1 | async-start | bytes 524288 | tf_op jit(solution)/shard_map/all_to_all | solution.py:136
  34.7 0.0 copy-start.1
  34.7 5.8 %copy-done.1 = f32[256,16384]{1,0:T(8,128)S(1)} copy-done((f32[256,16384]{1,0:T(8,128)S(1)}, f32[256,16384]{1,0:T(8,128)}, u32[]{:S(2)}) %copy-start.1) | copy-done | bytes 16777240
  40.4 12.5 %pair_gram.1 = f32[256,256]{1,0:T(8,128)S(1)} custom-call(f32[256,16384]{1,0:T(8,128)S(1)} %copy-done.1, f32[256,16384]{1,0:T(8,128)} %collective-permute-done.other_ref.other_x), custom_call_target="tpu_custom_call" | custom-call | flops 6442450944 | bytes 33554432 | tf_op jit(solution)/shard_map/pair_gram/pallas_call | solution.py:107
  52.9 0.0 all-to-all-done.1
  52.9 0.2 summary.1.summary_ref
  53.1 14.0 %all_to_all.21.arrived_ref = f32[8,32,256]{2,1,0:T(8,128)S(1)} all-to-all(f32[8,32,256]{2,1,0:T(8,128)S(1)} %bitcast.6), channel_id=1, replica_groups=mesh['grp'=2,'dim'=8,'blk'=2] {'dim'}, dimensions={0} | all-to-all | bytes 524288 | tf_op jit(solution)/shard_map/all_to_all | solution.py:130
  67.1 0.7 sum_shards.3
  67.9 3.4 %all-to-all-start.3 = ((f32[8,32,256]{2,1,0:T(8,128)}), f32[8,32,256]{2,1,0:T(8,128)S(1)}, u32[]{:S(2)}, u32[]{:S(2)}) async-start(f32[8,32,256]{2,1,0:T(8,128)} %sum_shards.3), calls=%async_computation.3 | async-start | bytes 524288 | tf_op jit(solution)/shard_map/all_to_all | solution.py:136
  71.3 0.2 collective-permute-start.2
  71.5 6.4 %collective-permute-done.2.other_ref = f32[8,256]{1,0:T(8,128)S(1)} collective-permute-done((f32[8,256]{1,0:T(8,128)S(1)}, f32[8,256]{1,0:T(8,128)S(1)}, u32[]{:S(2)}, u32[]{:S(2)}) %collective-permute-start.2) | collective-permute-done | bytes 8224 | tf_op jit(solution)/shard_map/ppermute | solution.py:224
  77.9 1.8 %all-to-all-done.3 = f32[8,32,256]{2,1,0:T(8,128)S(1)} async-done(((f32[8,32,256]{2,1,0:T(8,128)}), f32[8,32,256]{2,1,0:T(8,128)S(1)}, u32[]{:S(2)}, u32[]{:S(2)}) %all-to-all-start.3) | async-done | bytes 262176 | tf_op jit(solution)/shard_map/all_to_all | solution.py:136
  79.6 0.6 kernel_weights.1
  80.2 0.0 collective-permute-done.1.other_s
  80.2 0.0 copy-start.2
  80.2 5.8 %copy-done.2 = f32[256,16384]{1,0:T(8,128)S(1)} copy-done((f32[256,16384]{1,0:T(8,128)S(1)}, f32[256,16384]{1,0:T(8,128)}, u32[]{:S(2)}) %copy-start.2) | copy-done | bytes 16777240
  86.0 30.6 %velocity.1 = f32[256,16384]{1,0:T(8,128)} custom-call(f32[256,16384]{1,0:T(8,128)S(1)} %copy-done.2, f32[256,16384]{1,0:T(8,128)} %s_ref.1, f32[256,16384]{1,0:T(8,128)} %collective-permute-done.other_ref.other_x, f32[256,16384]{1,0:T(8,128)} %collective-permute-done.1.other_s, bf16[256,512]{1,0:T(8,128)(2,1)S(1)} %get-tuple-element.17.hi_ref, ...), custom_call_target="tpu_custom_call" | custom-call | flops 12884901888 | bytes 83886080 | tf_op jit(solution)/shard_map/velocity/pallas_call | solution.py:195
Async XLA Ops:
  0.0 31.1 %collective-permute-start = (f32[256,16384]{1,0:T(8,128)}, f32[256,16384]{1,0:T(8,128)}, u32[]{:S(2)}, u32[]{:S(2)}) collective-permute-start(f32[256,16384]{1,0:T(8,128)} %x_ref.3), channel_id=1, source_target_pairs={{0,1},{1,0},{2,3},{3,2},{4,5},{5,4},{6,7},{7,6},{8,9},{9,8},{10,11... | collective-permute-start | bytes 50331656 | tf_op jit(solution)/shard_map/ppermute | solution.py:208
  0.5 79.7 %collective-permute-start.1 = (f32[256,16384]{1,0:T(8,128)}, f32[256,16384]{1,0:T(8,128)}, u32[]{:S(2)}, u32[]{:S(2)}) collective-permute-start(f32[256,16384]{1,0:T(8,128)} %s_ref.1), channel_id=1, source_target_pairs={{0,1},{1,0},{2,3},{3,2},{4,5},{5,4},{6,7},{7,6},{8,9},{9,8},{10,11... | collective-permute-start | bytes 50331656 | tf_op jit(solution)/shard_map/ppermute | solution.py:208
  0.5 5.8 %copy-start = (f32[256,16384]{1,0:T(8,128)S(1)}, f32[256,16384]{1,0:T(8,128)}, u32[]{:S(2)}) copy-start(f32[256,16384]{1,0:T(8,128)} %x_ref.3) | copy-start | bytes 50331652
  31.1 21.8 %all-to-all-start.1 = ((f32[8,32,256]{2,1,0:T(8,128)}), f32[8,32,256]{2,1,0:T(8,128)S(1)}, u32[]{:S(2)}, u32[]{:S(2)}) async-start(f32[8,32,256]{2,1,0:T(8,128)} %sum_shards.2), calls=%async_computation.1 | async-start | bytes 524288 | tf_op jit(solution)/shard_map/all_to_all | solution.py:136
  34.7 5.8 %copy-start.1 = (f32[256,16384]{1,0:T(8,128)S(1)}, f32[256,16384]{1,0:T(8,128)}, u32[]{:S(2)}) copy-start(f32[256,16384]{1,0:T(8,128)} %x_ref.3) | copy-start | bytes 50331652
  67.9 11.8 %all-to-all-start.3 = ((f32[8,32,256]{2,1,0:T(8,128)}), f32[8,32,256]{2,1,0:T(8,128)S(1)}, u32[]{:S(2)}, u32[]{:S(2)}) async-start(f32[8,32,256]{2,1,0:T(8,128)} %sum_shards.3), calls=%async_computation.3 | async-start | bytes 524288 | tf_op jit(solution)/shard_map/all_to_all | solution.py:136
  71.3 6.6 %collective-permute-start.2 = (f32[8,256]{1,0:T(8,128)S(1)}, f32[8,256]{1,0:T(8,128)S(1)}, u32[]{:S(2)}, u32[]{:S(2)}) collective-permute-start(f32[8,256]{1,0:T(8,128)S(1)} %summary.1.summary_ref), channel_id=1, source_target_pairs={{0,3},{1,2},{2,5},{3,4},{4,7},{5,6},{6,9},{7,8},{8,11},{9,10},{10,... | collective-permute-start | bytes 24584 | tf_op jit(solution)/shard_map/ppermute | solution.py:224
  80.2 5.8 %copy-start.2 = (f32[256,16384]{1,0:T(8,128)S(1)}, f32[256,16384]{1,0:T(8,128)}, u32[]{:S(2)}) copy-start(f32[256,16384]{1,0:T(8,128)} %x_ref.3) | copy-start | bytes 50331652

commit v4 on v2

v4 whole, which is shorter than its diff:
```python
import functools
import math

import jax
import jax.numpy as jnp
from jax import lax
from jax.experimental import pallas as pl
from jax.experimental.pallas import tpu as pltpu
from jax.sharding import PartitionSpec as P

GRAM_TILE = 2048
VELOCITY_TILE = 1024
CHUNKS = 4
MIB = 1024 * 1024
BOTH = ("dim", "blk")


def params(limit):
    return pltpu.CompilerParams(vmem_limit_bytes=limit * MIB)


def small_cost():
    return pl.CostEstimate(flops=1024, bytes_accessed=1024, transcendentals=0)


def split(x):
    hi = x.astype(jnp.bfloat16)
    lo = (x - hi.astype(jnp.float32)).astype(jnp.bfloat16)
    return hi, lo


def nt_dot(left, right):
    return lax.dot_general(left, right, (((1,), (1,)), ((), ())), preferred_element_type=jnp.float32)


def nn_dot(left, right):
    return jnp.dot(left, right, preferred_element_type=jnp.float32)


def lane_sums(values):
    total = values[:, :128]
    for start in range(128, values.shape[1], 128):
        total = total + values[:, start:start + 128]
    return total


def whole(array):
    return pl.BlockSpec(array.shape, lambda i, core: (0,) * len(array.shape))


def f32(*shape):
    return jax.ShapeDtypeStruct(shape, jnp.float32)


def on_diagonal(rows):
    return lax.broadcasted_iota(jnp.int32, (rows, rows), 0) == lax.broadcasted_iota(jnp.int32, (rows, rows), 1)


def call(kernel, name, grid, in_specs, out_specs, out_shape, limit, scratch=(), aliases=None):
    return pl.pallas_call(
        kernel,
        grid_spec=pltpu.PrefetchScalarGridSpec(
            num_scalar_prefetch=1, grid=grid, in_specs=in_specs, out_specs=out_specs, scratch_shapes=list(scratch)
        ),
        out_shape=out_shape,
        input_output_aliases=aliases or {},
        compiler_params=params(limit),
        cost_estimate=small_cost(),
        name=name,
    )


def own_kernel(first, core_ref, *refs):
    refs = list(refs)
    x_ref = refs.pop(0)
    gram_in, squares_in = (None, None) if first else (refs.pop(0), refs.pop(0))
    if first:
        copy_ref, gram_ref, squares_ref = refs
    else:
        out_ref, gram_ref, squares_ref = refs

    @pl.when(pl.program_id(0) == 0)
    def _():
        gram_ref[...] = jnp.zeros_like(gram_ref) if first else gram_in[...]
        squares_ref[...] = jnp.zeros_like(squares_ref) if first else squares_in[...]

    x = x_ref[...]
    if first:
        copy_ref[...] = x
    hi, lo = split(x)
    gram_ref[...] += nt_dot(jnp.concatenate([hi, lo], axis=0), hi)
    squares_ref[...] += lane_sums(x * x)

    if not first:
        @pl.when(pl.program_id(0) == pl.num_programs(0) - 1)
        def _():
            rows = out_ref.shape[0]
            mixed = gram_ref[rows:, :]
            gram = gram_ref[:rows, :] + mixed + mixed.T
            norms = jnp.sum(squares_ref[...], axis=1, keepdims=True)
            out_ref[...] = jnp.where(on_diagonal(rows), norms, norms + norms.T - 2.0 * gram)


def own_sent(core, particles):
    rows, columns = particles.shape
    width = columns // 2
    tile = min(GRAM_TILE, width)
    tiles = width // tile
    outs = [f32(rows, width), f32(2 * rows, rows), f32(rows, 128)]
    return call(
        functools.partial(own_kernel, True),
        "own_gram_sent",
        (tiles,),
        [pl.BlockSpec((rows, tile), lambda i, core: (0, (1 - core[0]) * tiles + i))],
        [pl.BlockSpec((rows, tile), lambda i, core: (0, i)), whole(outs[1]), whole(outs[2])],
        outs,
        52,
    )(core, particles)


def own_kept(core, particles, gram, squares):
    rows, columns = particles.shape
    width = columns // 2
    tile = min(GRAM_TILE, width)
    tiles = width // tile
    out = f32(rows, rows)
    return call(
        functools.partial(own_kernel, False),
        "own_gram_kept",
        (tiles,),
        [pl.BlockSpec((rows, tile), lambda i, core: (0, core[0] * tiles + i)), whole(gram), whole(squares)],
        whole(out),
        out,
        52,
        scratch=[pltpu.VMEM((2 * rows, rows), jnp.float32), pltpu.VMEM((rows, 128), jnp.float32)],
    )(core, particles, gram, squares)


def copy_kernel(core_ref, source_ref, out_ref):
    out_ref[...] = source_ref[...]


def sent_half(core, array):
    rows, columns = array.shape
    width = columns // 2
    tile = min(GRAM_TILE, width)
    tiles = width // tile
    return call(
        copy_kernel,
        "sent_half",
        (tiles,),
        [pl.BlockSpec((rows, tile), lambda i, core: (0, (1 - core[0]) * tiles + i))],
        pl.BlockSpec((rows, tile), lambda i, core: (0, i)),
        f32(rows, width),
        52,
    )(core, array)


def pair_kernel(core_ref, mine_ref, other_ref, out_ref, gram_ref):
    @pl.when(pl.program_id(0) == 0)
    def _():
        gram_ref[...] = jnp.zeros_like(gram_ref)

    rows = gram_ref.shape[0]
    my_hi, my_lo = split(mine_ref[...])
    hi, lo = split(other_ref[...])
    both = nt_dot(jnp.concatenate([my_hi, my_lo], axis=0), hi)
    gram_ref[...] += both[:rows] + both[rows:] + nt_dot(my_hi, lo)

    @pl.when(pl.program_id(0) == pl.num_programs(0) - 1)
    def _():
        gram = gram_ref[...]
        out_ref[...] = jnp.where(core_ref[0] == 0, gram, gram.T)


def pair_part(core, particles, visitor):
    rows, width = visitor.shape
    tile = min(GRAM_TILE, width)
    tiles = width // tile
    out = f32(rows, rows)
    return call(
        pair_kernel,
        "pair_gram",
        (tiles,),
        [
            pl.BlockSpec((rows, tile), lambda i, core: (0, core[0] * tiles + i)),
            pl.BlockSpec((rows, tile), lambda i, core: (0, i)),
        ],
        whole(out),
        out,
        40,
        scratch=[pltpu.VMEM((rows, rows), jnp.float32)],
    )(core, particles, visitor)


def sum_kernel(arrived_ref, out_ref):
    total = arrived_ref[0]
    for step in range(1, arrived_ref.shape[0]):
        total = total + arrived_ref[step]
    for step in range(out_ref.shape[0]):
        out_ref[step] = total


def summed_shards(block, axes, copies):
    count = lax.axis_size(axes)
    rows, columns = block.shape
    arrived = lax.all_to_all(block.reshape(count, rows // count, columns), axes, 0, 0)
    return pl.pallas_call(
        sum_kernel,
        out_shape=f32(copies, rows // count, columns),
        compiler_params=params(8),
        cost_estimate=small_cost(),
        name="sum_shards",
    )(arrived)


def weights_kernel(scale_base, core_ref, blocks_ref, gram_ref, hi_ref, lo_ref, weight_ref, half_ref, own_ref, other_ref):
    core = core_ref[0]
    rows = gram_ref.shape[0]
    step = blocks_ref.shape[1]
    for d in range(blocks_ref.shape[0] // 2):
        own_ref[d * step:(d + 1) * step, :] = blocks_ref[2 * d + core]
        other_ref[d * step:(d + 1) * step, :] = blocks_ref[2 * d + 1 - core]
    own, other, gram = own_ref[...], other_ref[...], gram_ref[...]
    diagonal = on_diagonal(rows)
    gram = jnp.where(core == 0, gram, gram.T)
    norms = jnp.sum(jnp.where(diagonal, own, 0.0), axis=1, keepdims=True)
    others = jnp.sum(jnp.where(diagonal, other, 0.0), axis=0, keepdims=True)
    pair = norms + others - 2.0 * gram
    own = jnp.where(diagonal, 0.0, own)
    other = jnp.where(diagonal, 0.0, other)
    spread = jnp.sum(own) + jnp.sum(other) + 2.0 * jnp.sum(pair)
    width = jnp.full((1, 1), spread, jnp.float32) / scale_base
    inverse = -1.0 / width
    own = jnp.where(diagonal, 0.0, jnp.exp(own * inverse))
    other = jnp.where(diagonal, 0.0, jnp.exp(other * inverse))
    pair = jnp.exp(pair * inverse)
    weights = jnp.concatenate(
        [jnp.concatenate([own, pair], axis=1), jnp.concatenate([pair.T, other], axis=1)], axis=0
    )
    hi_ref[...], lo_ref[...] = split(weights)
    weight_ref[...] = jnp.broadcast_to(jnp.sum(weights, axis=1, keepdims=True), weight_ref.shape)
    half_ref[...] = jnp.broadcast_to(0.5 * width, half_ref.shape)


def weights_part(core, blocks, gram, scale_base):
    rows = gram.shape[0]
    half = jax.ShapeDtypeStruct((2 * rows, 2 * rows), jnp.bfloat16)
    outs = [half, half, f32(2 * rows, 128), f32(8, 128)]
    return call(
        functools.partial(weights_kernel, scale_base),
        "kernel_weights",
        (1,),
        [whole(blocks), whole(gram)],
        [whole(o) for o in outs],
        outs,
        48,
        scratch=[pltpu.VMEM((rows, rows), jnp.float32)] * 2,
    )(core, blocks, gram)


def velocity_kernel(core_ref, x_ref, s_ref, other_x, other_s, hi_ref, lo_ref, weight_ref, half_ref, *refs):
    out_ref, sent_ref = refs[-2:]
    rows = x_ref.shape[0]
    half = half_ref[0:1, 0:1]
    x = jnp.concatenate([x_ref[...], other_x[...]], axis=0)
    driven = half * jnp.concatenate([s_ref[...], other_s[...]], axis=0)
    moved_hi, moved_lo = split(driven - x)
    hi = hi_ref[...]
    both = nn_dot(jnp.concatenate([hi, lo_ref[...]], axis=0), moved_hi)
    out = driven + weight_ref[:, 0:1] * x + both[:2 * rows] + both[2 * rows:] + nn_dot(hi, moved_lo)
    out_ref[...] = out[:rows]
    sent_ref[...] = out[rows:]


def velocity_part(core, particles, scores, visitor, visitor_scores, weights, earlier, chunk):
    rows, columns = particles.shape
    half = columns // 2
    width = half // CHUNKS
    tile = min(VELOCITY_TILE, width)
    tiles = width // tile
    start = chunk * tiles
    mine = pl.BlockSpec((rows, tile), lambda i, core: (0, core[0] * (half // tile) + start + i))
    other = pl.BlockSpec((rows, tile), lambda i, core: (0, start + i))
    before = [] if earlier is None else [earlier]
    operands = [core, particles, scores, visitor, visitor_scores, *weights, *before]
    return call(
        velocity_kernel,
        "velocity",
        (tiles,),
        [mine, mine, other, other] + [whole(w) for w in weights] + [pl.BlockSpec(memory_space=pl.ANY)] * len(before),
        [mine, pl.BlockSpec((rows, tile), lambda i, core: (0, i))],
        [f32(rows, columns), f32(rows, width)],
        40,
        aliases={len(operands) - 1: 0} if before else None,
    )(*operands)


def place_kernel(core_ref, part_ref, earlier_ref, out_ref):
    out_ref[...] = part_ref[...]


def place(core, part, earlier, chunk):
    rows, columns = earlier.shape
    half = columns // 2
    width = part.shape[1]
    tile = min(VELOCITY_TILE, width)
    start = chunk * (width // tile)
    return call(
        place_kernel,
        "place",
        (width // tile,),
        [pl.BlockSpec((rows, tile), lambda i, core: (0, i)), pl.BlockSpec(memory_space=pl.ANY)],
        pl.BlockSpec((rows, tile), lambda i, core: (0, (1 - core[0]) * (half // tile) + start + i)),
        f32(rows, columns),
        40,
        aliases={2: 0},
    )(core, part, earlier)


def swap(array):
    return lax.ppermute(array, "blk", [(0, 1), (1, 0)])


def body(particles, scores):
    total_rows = particles.shape[0] * lax.axis_size("blk")
    scale_base = total_rows * total_rows * math.log(total_rows)
    devices = lax.axis_size(BOTH)
    core = lax.axis_index("blk").reshape(1)

    copy, gram, squares = own_sent(core, particles)
    visitor = swap(copy)
    own = own_kept(core, particles, gram, squares)
    scores_late, _ = lax.optimization_barrier((scores, own))
    visitor_scores = swap(sent_half(core, scores_late))

    own_copies = summed_shards(own, "dim", devices)
    visitor, own_copies = lax.optimization_barrier((visitor, own_copies))
    blocks = lax.all_to_all(own_copies, BOTH, 0, 0)

    gram, blocks = lax.optimization_barrier((pair_part(core, particles, visitor), blocks))
    gram_copies = summed_shards(gram, BOTH, devices)
    gram = lax.all_to_all(gram_copies, BOTH, 0, 0).reshape(own.shape)
    weights = weights_part(core, blocks, gram, scale_base)

    velocity, parts = None, []
    for chunk in range(CHUNKS):
        velocity, part = velocity_part(core, particles, scores, visitor, visitor_scores, weights, velocity, chunk)
        parts.append(swap(part))
    for chunk in range(CHUNKS):
        velocity = place(core, parts[chunk], velocity, chunk)
    return velocity


def solution(mesh):
    return jax.shard_map(
        body,
        mesh=mesh,
        in_specs=(P(("grp", "blk"), "dim"), P(("grp", "blk"), "dim")),
        out_specs=P(("grp", "blk"), "dim"),
        check_vma=False,
    )
```

time: 174 us -> 127 us (0.73)
  matrix products: 69.6 us -> 0 us
  Pallas kernels: 0 us -> 63.7 us
  other arithmetic: 44.5 us -> 0 us
  blocking collectives: 26.8 us -> 42.9 us
  waiting for transfers between devices: 20.3 us -> 4.41 us
  local copies, waits for them, and re-layouts: 2.9 us -> 10.2 us
  starting transfers between devices: 7.75 us -> 5.18 us
  between operations: 2.02 us -> 0.07 us
    dot_general x3 -> x0, matrix products: 69.6 us -> none  [dot3(): jnp.dot(left, right, precision=lax.Precision.HIGH, preferred_element_type...]
    pallas_call x0 -> x15, Pallas kernels: none -> 63.7 us  [the longest x4 27.8 us: velocity_part(): call(velocity_kernel, 'velocity', (tiles,), [mine, mine, other, other] +...]
    sub x2 -> x0, other arithmetic: 35.5 us -> none  [the longest x1 17.7 us: body(): half * visitor_scores - visitor]
    all_to_all x2 -> x3, blocking collectives: 26.8 us -> 42.9 us  [the longest x2 30.1 us: summed_shards(): lax.all_to_all(block.reshape(count, rows // count, columns), axes, 0, 0)]
    all_to_all x2 -> x1, waiting for transfers between devices: 14.6 us -> 4.4 us  [body(): blocks = lax.all_to_all(own_copies, BOTH, 0, 0)]
    unnamed x0 -> x6, local copies, waits for them, and re-layouts: none -> 10.2 us
    reduce_sum x5 -> x0, other arithmetic: 8.15 us -> none  [the longest x1 7 us: body(): norms = jnp.sum(particles * particles, axis=1)]
    ppermute x1 -> x0, waiting for transfers between devices: 5.69 us -> none  [body(): other = lax.ppermute(summary, ('dim', 'blk'), across)]
  transfers between devices with their start and end apart: 5 -> 7, of which waited for: 3 -> 1; matrix products, arithmetic and copies ran while one was open for 39% -> 0% of each run, Pallas kernels for 0% -> 37%
where the time goes in v4:
time: 127 us; the launch traced here: 126 us
  Pallas kernels  63.7 us (50%)
  blocking collectives  42.9 us (34%)
  local copies, waits for them, and re-layouts  10.2 us (8%)
  starting transfers between devices  5.18 us (4%)
  waiting for transfers between devices  4.41 us (3%)
    all_to_all x2, blocking collectives, summed_shards(): lax.all_to_all(block.reshape(count, rows // count, columns), axes, 0, 0)  30.1 us
    pallas_call x4, Pallas kernels, velocity_part(): call(velocity_kernel, 'velocity', (tiles,), [mine, mine, other, other] +...  27.8 us
    all_to_all x1, blocking collectives, body(): gram = lax.all_to_all(gram_copies, BOTH, 0, 0).reshape(own.shape)  12.8 us
    unnamed x6, local copies, waits for them, and re-layouts  10.2 us
    pallas_call x1, Pallas kernels, own_sent(): call(functools.partial(own_kernel, True), 'own_gram_sent', (tiles,), [pl....  8.14 us
    pallas_call x1, Pallas kernels, sent_half(): call(copy_kernel, 'sent_half', (tiles,), [pl.BlockSpec((rows, tile), lamb...  7.16 us
    pallas_call x1, Pallas kernels, pair_part(): call(pair_kernel, 'pair_gram', (tiles,), [pl.BlockSpec((rows, tile), lamb...  6.68 us
    pallas_call x4, Pallas kernels, place(): call(place_kernel, 'place', (width // tile,), [pl.BlockSpec((rows, tile),...  6.17 us
  transfers between devices with their start and end apart: 7, of which 1 were waited for; matrix products, arithmetic and copies ran while one was open for 0% of the time, Pallas kernels for 37%

profile of v4, /device:TPU:0, one launch (start us, length us, event | category | flops | bytes accessed | tf_op | source)
XLA Modules:
  0.0 126.4 jit_solution(976588611150029871)
XLA Ops:
  0.0 8.1 %own_gram_sent.1 = (f32[256,8192]{1,0:T(8,128)}, f32[512,256]{1,0:T(8,128)S(1)}, f32[256,128]{1,0:T(8,128)S(1)}) custom-call(s32[1]{0:T(128)} %bitcast.core_ref, f32[256,16384]{1,0:T(8,128)} %x_ref.7), custom_call_target="tpu_custom_call" | custom-call | flops 1024 | bytes 1024 | tf_op jit(solution)/shard_map/own_gram_sent/pallas_call | solution.py:110
  8.1 0.5 collective-permute-start
  8.6 6.1 %own_gram_kept.1 = f32[256,256]{1,0:T(8,128)S(1)} custom-call(s32[1]{0:T(128)} %bitcast.core_ref, f32[256,16384]{1,0:T(8,128)} %x_ref.7, f32[512,256]{1,0:T(8,128)S(1)} %get-tuple-element.26.refs_1_, f32[256,128]{1,0:T(8,128)S(1)} %get-tuple-element.27.refs_2_), custom_call_target="tpu_custom_call" | custom-call | flops 1024 | bytes 1024 | tf_op jit(solution)/shard_map/own_gram_kept/pallas_call | solution.py:127
  14.7 7.2 %sent_half.1 = f32[256,8192]{1,0:T(8,128)} custom-call(s32[1]{0:T(128)} %bitcast.core_ref, f32[256,16384]{1,0:T(8,128)} %s_ref.7), custom_call_target="tpu_custom_call" | custom-call | flops 1024 | bytes 1024 | tf_op jit(solution)/shard_map/sent_half/pallas_call | solution.py:148
  21.8 0.1 collective-permute-start.1
  21.9 16.2 %all_to_all.20.arrived_ref = f32[8,32,256]{2,1,0:T(8,128)S(1)} all-to-all(f32[8,32,256]{2,1,0:T(8,128)S(1)} %bitcast.4), channel_id=1, replica_groups=mesh['grp'=2,'dim'=8,'blk'=2] {'dim'}, dimensions={0} | all-to-all | bytes 524288 | tf_op jit(solution)/shard_map/all_to_all | solution.py:207
  38.0 0.9 sum_shards.2
  38.9 0.0 collective-permute-done.other_ref.other_x
  38.9 3.4 %copy-done = f32[256,8192]{1,0:T(8,128)} copy-done((f32[256,8192]{1,0:T(8,128)}, f32[256,8192]{1,0:T(8,128)S(1)}, u32[]{:S(2)}) %copy-start) | copy-done | bytes 8388632
  42.3 3.7 %all-to-all-start.1 = ((f32[16,32,256]{2,1,0:T(8,128)}), f32[16,32,256]{2,1,0:T(8,128)S(1)}, u32[]{:S(2)}, u32[]{:S(2)}) async-start(f32[16,32,256]{2,1,0:T(8,128)} %sum_shards.2), calls=%async_computation.1 | async-start | bytes 1048576 | tf_op jit(solution)/shard_map/all_to_all | solution.py:339
  46.0 0.0 copy-start.1
  46.0 3.4 %copy-done.1 = f32[256,8192]{1,0:T(8,128)S(1)} copy-done((f32[256,8192]{1,0:T(8,128)S(1)}, f32[256,8192]{1,0:T(8,128)}, u32[]{:S(2)}) %copy-start.1) | copy-done | bytes 8388632
  49.4 6.7 %pair_gram.1 = f32[256,256]{1,0:T(8,128)S(1)} custom-call(s32[1]{0:T(128)} %bitcast.core_ref, f32[256,16384]{1,0:T(8,128)} %x_ref.7, f32[256,8192]{1,0:T(8,128)S(1)} %copy-done.1), custom_call_target="tpu_custom_call" | custom-call | flops 1024 | bytes 1024 | tf_op jit(solution)/shard_map/pair_gram/pallas_call | solution.py:181
  56.1 4.4 %all-to-all-done.1.blocks_ref = f32[16,32,256]{2,1,0:T(8,128)S(1)} async-done(((f32[16,32,256]{2,1,0:T(8,128)}), f32[16,32,256]{2,1,0:T(8,128)S(1)}, u32[]{:S(2)}, u32[]{:S(2)}) %all-to-all-start.1) | async-done | bytes 524320 | tf_op jit(solution)/shard_map/all_to_all | solution.py:339
  60.5 13.9 %all_to_all.21.arrived_ref = f32[16,16,256]{2,1,0:T(8,128)S(1)} all-to-all(f32[16,16,256]{2,1,0:T(8,128)S(1)} %bitcast.5), channel_id=1, replica_groups=mesh['grp'=2,'dim'=8,'blk'=2] {'dim','blk'}, dimensions={0} | all-to-all | bytes 524288 | tf_op jit(solution)/shard_map/all_to_all | solution.py:207
  74.4 12.8 %all_to_all.22 = f32[16,16,256]{2,1,0:T(8,128)S(1)} all-to-all(f32[16,16,256]{2,1,0:T(8,128)S(1)} %sum_shards.3), channel_id=1, replica_groups=mesh['grp'=2,'dim'=8,'blk'=2] {'dim','blk'}, dimensions={0} | all-to-all | bytes 524288 | tf_op jit(solution)/shard_map/all_to_all | solution.py:343
  87.3 0.7 kernel_weights.1
  88.0 0.0 copy-start.2
  88.0 3.4 %copy-done.2 = f32[256,8192]{1,0:T(8,128)S(1)} copy-done((f32[256,8192]{1,0:T(8,128)S(1)}, f32[256,8192]{1,0:T(8,128)}, u32[]{:S(2)}) %copy-start.2) | copy-done | bytes 8388632
  91.4 6.9 %velocity.4 = (f32[256,16384]{1,0:T(8,128)}, f32[256,2048]{1,0:T(8,128)S(1)}) custom-call(s32[1]{0:T(128)} %bitcast.core_ref, f32[256,16384]{1,0:T(8,128)} %x_ref.7, f32[256,16384]{1,0:T(8,128)} %s_ref.7, f32[256,8192]{1,0:T(8,128)S(1)} %copy-done.2, f32[256,8192]{1,0:T(8,128)} %collective-permute-done.1.other_s, ...), custom_call_target="tpu_custom_call" | custom-call | flops 1024 | bytes 1024 | tf_op jit(solution)/shard_map/velocity/pallas_call | solution.py:287
  98.3 0.0 collective-permute-start.5
  98.3 7.2 %velocity.5 = (f32[256,16384]{1,0:T(8,128)}, f32[256,2048]{1,0:T(8,128)}) custom-call(s32[1]{0:T(128)} %bitcast.core_ref, f32[256,16384]{1,0:T(8,128)} %x_ref.7, f32[256,16384]{1,0:T(8,128)} %s_ref.7, f32[256,8192]{1,0:T(8,128)S(1)} %copy-done.2, f32[256,8192]{1,0:T(8,128)} %collective-permute-done.1.other_s, ...), custom_call_target="tpu_custom_call", output_to_operand_aliasing={{0}: (9, {})} | custom-call | flops 1024 | bytes 1024 | tf_op jit(solution)/shard_map/velocity/pallas_call | solution.py:287
  105.5 6.9 %velocity.6 = (f32[256,16384]{1,0:T(8,128)}, f32[256,2048]{1,0:T(8,128)S(1)}) custom-call(s32[1]{0:T(128)} %bitcast.core_ref, f32[256,16384]{1,0:T(8,128)} %x_ref.7, f32[256,16384]{1,0:T(8,128)} %s_ref.7, f32[256,8192]{1,0:T(8,128)S(1)} %copy-done.2, f32[256,8192]{1,0:T(8,128)} %collective-permute-done.1.other_s, ...), custom_call_target="tpu_custom_call", output_to_operand_aliasing={{0}: (9, {})} | custom-call | flops 1024 | bytes 1024 | tf_op jit(solution)/shard_map/velocity/pallas_call | solution.py:287
  112.4 0.5 collective-permute-start.3
  112.8 0.0 collective-permute-start.4
  112.9 6.9 %velocity.7 = (f32[256,16384]{1,0:T(8,128)}, f32[256,2048]{1,0:T(8,128)S(1)}) custom-call(s32[1]{0:T(128)} %bitcast.core_ref, f32[256,16384]{1,0:T(8,128)} %x_ref.7, f32[256,16384]{1,0:T(8,128)} %s_ref.7, f32[256,8192]{1,0:T(8,128)S(1)} %copy-done.2, f32[256,8192]{1,0:T(8,128)} %collective-permute-done.1.other_s, ...), custom_call_target="tpu_custom_call", output_to_operand_aliasing={{0}: (9, {})} | custom-call | flops 1024 | bytes 1024 | tf_op jit(solution)/shard_map/velocity/pallas_call | solution.py:287
  119.7 0.5 collective-permute-start.2
  120.2 1.5 %place.4.earlier_ref = f32[256,16384]{1,0:T(8,128)} custom-call(s32[1]{0:T(128)} %bitcast.core_ref, f32[256,2048]{1,0:T(8,128)S(1)} %collective-permute-done.5.part_ref, f32[256,16384]{1,0:T(8,128)} %get-tuple-element.44.earlier_ref), custom_call_target="tpu_custom_call", output_to_operand_aliasing={{}: (2, {})} | custom-call | flops 1024 | bytes 1024 | tf_op jit(solution)/shard_map/place/pallas_call | solution.py:309
  121.8 0.0 collective-permute-done.4.part_ref
  121.8 1.5 %place.5.earlier_ref = f32[256,16384]{1,0:T(8,128)} custom-call(s32[1]{0:T(128)} %bitcast.core_ref, f32[256,2048]{1,0:T(8,128)S(1)} %collective-permute-done.4.part_ref, f32[256,16384]{1,0:T(8,128)} %place.4.earlier_ref), custom_call_target="tpu_custom_call", output_to_operand_aliasing={{}: (2, {})} | custom-call | flops 1024 | bytes 1024 | tf_op jit(solution)/shard_map/place/pallas_call | solution.py:309
  123.3 1.5 %place.6.earlier_ref = f32[256,16384]{1,0:T(8,128)} custom-call(s32[1]{0:T(128)} %bitcast.core_ref, f32[256,2048]{1,0:T(8,128)S(1)} %collective-permute-done.3.part_ref, f32[256,16384]{1,0:T(8,128)} %place.5.earlier_ref), custom_call_target="tpu_custom_call", output_to_operand_aliasing={{}: (2, {})} | custom-call | flops 1024 | bytes 1024 | tf_op jit(solution)/shard_map/place/pallas_call | solution.py:309
  124.9 1.5 %place.7 = f32[256,16384]{1,0:T(8,128)} custom-call(s32[1]{0:T(128)} %bitcast.core_ref, f32[256,2048]{1,0:T(8,128)S(1)} %collective-permute-done.2.part_ref, f32[256,16384]{1,0:T(8,128)} %place.6.earlier_ref), custom_call_target="tpu_custom_call", output_to_operand_aliasing={{}: (2, {})} | custom-call | flops 1024 | bytes 1024 | tf_op jit(solution)/shard_map/place/pallas_call | solution.py:309
  (6 shorter events, 0.0 us)
Async XLA Ops:
  8.1 30.8 %collective-permute-start = (f32[256,8192]{1,0:T(8,128)}, f32[256,8192]{1,0:T(8,128)S(1)}, u32[]{:S(2)}, u32[]{:S(2)}) collective-permute-start(f32[256,8192]{1,0:T(8,128)} %get-tuple-element.25), channel_id=1, source_target_pairs={{0,1},{1,0},{2,3},{3,2},{4,5},{5,4},{6,7},{7,6},{8,9},{9,8},{10,11... | collective-permute-start | bytes 25165832 | tf_op jit(solution)/shard_map/ppermute | solution.py:322
  21.8 66.2 %collective-permute-start.1 = (f32[256,8192]{1,0:T(8,128)}, f32[256,8192]{1,0:T(8,128)}, u32[]{:S(2)}, u32[]{:S(2)}) collective-permute-start(f32[256,8192]{1,0:T(8,128)} %sent_half.1), channel_id=1, source_target_pairs={{0,1},{1,0},{2,3},{3,2},{4,5},{5,4},{6,7},{7,6},{8,9},{9,8},{10,11... | collective-permute-start | bytes 25165832 | tf_op jit(solution)/shard_map/ppermute | solution.py:322
  38.9 3.4 %copy-start = (f32[256,8192]{1,0:T(8,128)}, f32[256,8192]{1,0:T(8,128)S(1)}, u32[]{:S(2)}) copy-start(f32[256,8192]{1,0:T(8,128)S(1)} %collective-permute-done.other_ref.other_x) | copy-start | bytes 25165828
  42.3 18.2 %all-to-all-start.1 = ((f32[16,32,256]{2,1,0:T(8,128)}), f32[16,32,256]{2,1,0:T(8,128)S(1)}, u32[]{:S(2)}, u32[]{:S(2)}) async-start(f32[16,32,256]{2,1,0:T(8,128)} %sum_shards.2), calls=%async_computation.1 | async-start | bytes 1048576 | tf_op jit(solution)/shard_map/all_to_all | solution.py:339
  46.0 3.4 %copy-start.1 = (f32[256,8192]{1,0:T(8,128)S(1)}, f32[256,8192]{1,0:T(8,128)}, u32[]{:S(2)}) copy-start(f32[256,8192]{1,0:T(8,128)} %copy-done) | copy-start | bytes 25165828
  88.0 3.4 %copy-start.2 = (f32[256,8192]{1,0:T(8,128)S(1)}, f32[256,8192]{1,0:T(8,128)}, u32[]{:S(2)}) copy-start(f32[256,8192]{1,0:T(8,128)} %copy-done) | copy-start | bytes 25165828
  98.3 22.0 %collective-permute-start.5 = (f32[256,2048]{1,0:T(8,128)S(1)}, f32[256,2048]{1,0:T(8,128)S(1)}, u32[]{:S(2)}, u32[]{:S(2)}) collective-permute-start(f32[256,2048]{1,0:T(8,128)S(1)} %get-tuple-element.43), channel_id=1, source_target_pairs={{0,1},{1,0},{2,3},{3,2},{4,5},{5,4},{6,7},{7,6},{8,9},{9,8},{10,11... | collective-permute-start | bytes 6291464 | tf_op jit(solution)/shard_map/ppermute | solution.py:322
  112.4 10.9 %collective-permute-start.3 = (f32[256,2048]{1,0:T(8,128)S(1)}, f32[256,2048]{1,0:T(8,128)S(1)}, u32[]{:S(2)}, u32[]{:S(2)}) collective-permute-start(f32[256,2048]{1,0:T(8,128)S(1)} %get-tuple-element.41), channel_id=1, source_target_pairs={{0,1},{1,0},{2,3},{3,2},{4,5},{5,4},{6,7},{7,6},{8,9},{9,8},{10,11... | collective-permute-start | bytes 6291464 | tf_op jit(solution)/shard_map/ppermute | solution.py:322
  112.8 8.9 %collective-permute-start.4 = (f32[256,2048]{1,0:T(8,128)}, f32[256,2048]{1,0:T(8,128)S(1)}, u32[]{:S(2)}, u32[]{:S(2)}) collective-permute-start(f32[256,2048]{1,0:T(8,128)} %get-tuple-element.42), channel_id=1, source_target_pairs={{0,1},{1,0},{2,3},{3,2},{4,5},{5,4},{6,7},{7,6},{8,9},{9,8},{10,11... | collective-permute-start | bytes 6291464 | tf_op jit(solution)/shard_map/ppermute | solution.py:322
  119.7 5.1 %collective-permute-start.2 = (f32[256,2048]{1,0:T(8,128)S(1)}, f32[256,2048]{1,0:T(8,128)S(1)}, u32[]{:S(2)}, u32[]{:S(2)}) collective-permute-start(f32[256,2048]{1,0:T(8,128)S(1)} %get-tuple-element.40), channel_id=1, source_target_pairs={{0,1},{1,0},{2,3},{3,2},{4,5},{5,4},{6,7},{7,6},{8,9},{9,8},{10,11... | collective-permute-start | bytes 6291464 | tf_op jit(solution)/shard_map/ppermute | solution.py:322

commit v5 on v3

--- a/solution.py
+++ b/solution.py
@@ -50,20 +50,34 @@
     return lax.broadcasted_iota(jnp.int32, (rows, rows), 0) == lax.broadcasted_iota(jnp.int32, (rows, rows), 1)
 
 
-def own_kernel(x_ref, out_ref, gram_ref, squares_ref):
+def strips(rows, columns):
+    for column in range(0, columns, 256):
+        for row in range(0, rows, 32):
+            yield slice(row, row + 32), slice(column, column + 256)
+
+
+def below(where, rows):
+    return slice(where.start + rows, where.stop + rows)
+
+
+def own_kernel(x_ref, out_ref, halves_ref, gram_ref, squares_ref):
+    rows, columns = x_ref.shape
+
     @pl.when(pl.program_id(0) == 0)
     def _():
         gram_ref[...] = jnp.zeros_like(gram_ref)
         squares_ref[...] = jnp.zeros_like(squares_ref)
 
-    x = x_ref[...]
-    hi, lo = split(x)
-    gram_ref[...] += nt_dot(jnp.concatenate([hi, lo], axis=0), hi)
-    squares_ref[...] += lane_sums(x * x)
+    for row, column in strips(rows, columns):
+        x = x_ref[row, column]
+        hi, lo = split(x)
+        halves_ref[row, column] = hi
+        halves_ref[below(row, rows), column] = lo
+        squares_ref[row, :] += lane_sums(x * x)
+    gram_ref[...] += nt_dot(halves_ref[...], halves_ref[:rows, :])
 
     @pl.when(pl.program_id(0) == pl.num_programs(0) - 1)
     def _():
-        rows = out_ref.shape[0]
         mixed = gram_ref[rows:, :]
         gram = gram_ref[:rows, :] + mixed + mixed.T
         norms = jnp.sum(squares_ref[...], axis=1, keepdims=True)
@@ -80,23 +94,31 @@
         in_specs=[pl.BlockSpec((rows, tile), lambda i: (0, i))],
         out_specs=whole(out),
         out_shape=out,
-        scratch_shapes=[pltpu.VMEM((2 * rows, rows), jnp.float32), pltpu.VMEM((rows, 128), jnp.float32)],
-        compiler_params=params(20),
+        scratch_shapes=[
+            pltpu.VMEM((2 * rows, tile), jnp.bfloat16),
+            pltpu.VMEM((2 * rows, rows), jnp.float32),
+            pltpu.VMEM((rows, 128), jnp.float32),
+        ],
+        compiler_params=params(52),
         cost_estimate=pl.CostEstimate(flops=4 * rows * rows * columns, bytes_accessed=4 * rows * columns, transcendentals=0),
         name="own_gram",
     )(particles)
 
 
-def pair_kernel(mine_ref, other_ref, gram_ref):
+def pair_kernel(mine_ref, other_ref, gram_ref, mine_halves, other_halves):
+    rows, columns = mine_ref.shape
+
     @pl.when(pl.program_id(0) == 0)
     def _():
         gram_ref[...] = jnp.zeros_like(gram_ref)
 
-    rows = gram_ref.shape[0]
-    my_hi, my_lo = split(mine_ref[...])
-    hi, lo = split(other_ref[...])
-    both = nt_dot(jnp.concatenate([my_hi, my_lo], axis=0), hi)
-    gram_ref[...] += both[:rows] + both[rows:] + nt_dot(my_hi, lo)
+    for source, halves_ref in ((mine_ref, mine_halves), (other_ref, other_halves)):
+        for row, column in strips(rows, columns):
+            hi, lo = split(source[row, column])
+            halves_ref[row, column] = hi
+            halves_ref[below(row, rows), column] = lo
+    both = nt_dot(mine_halves[...], other_halves[:rows, :])
+    gram_ref[...] += both[:rows] + both[rows:] + nt_dot(mine_halves[:rows, :], other_halves[rows:, :])
 
 
 def pair_part(particles, visitor):
@@ -110,7 +132,11 @@
         in_specs=[block, block],
         out_specs=whole(out),
         out_shape=out,
-        compiler_params=params(24),
+        scratch_shapes=[
+            pltpu.VMEM((2 * rows, tile), jnp.bfloat16),
+            pltpu.VMEM((2 * rows, tile), jnp.bfloat16),
+        ],
+        compiler_params=params(52),
         cost_estimate=pl.CostEstimate(flops=6 * rows * rows * columns, bytes_accessed=8 * rows * columns, transcendentals=0),
         name="pair_gram",
     )(particles, visitor)
@@ -149,7 +175,7 @@
     return pl.pallas_call(summary_kernel, out_shape=f32(8, own.shape[0]), compiler_params=params(8), name="summary")(own)
 
 
-def weights_kernel(scale_base, own_ref, summary_ref, other_ref, gram_ref, hi_ref, lo_ref, weight_ref, half_ref):
+def weights_kernel(scale_base, own_ref, summary_ref, other_ref, gram_ref, weights_ref, weight_ref, half_ref):
     own = own_ref[...]
     rows = own.shape[0]
     diagonal = on_diagonal(rows)
@@ -161,31 +187,40 @@
     own_weights = jnp.where(diagonal, 0.0, jnp.exp(own * inverse))
     pair_weights = jnp.exp(pair * inverse)
     weights = jnp.concatenate([own_weights, pair_weights], axis=1)
-    hi_ref[...], lo_ref[...] = split(weights)
+    hi, lo = split(weights)
+    weights_ref[...] = jnp.concatenate([hi, hi, lo], axis=1)
     weight_ref[...] = jnp.broadcast_to(jnp.sum(weights, axis=1, keepdims=True), weight_ref.shape)
     half_ref[...] = jnp.broadcast_to(0.5 * width, half_ref.shape)
 
 
 def weights_part(own, summary, other, gram, scale_base):
     rows = own.shape[0]
-    half = jax.ShapeDtypeStruct((rows, 2 * rows), jnp.bfloat16)
     return pl.pallas_call(
         functools.partial(weights_kernel, scale_base),
-        out_shape=[half, half, f32(rows, 128), f32(8, 128)],
+        out_shape=[jax.ShapeDtypeStruct((rows, 6 * rows), jnp.bfloat16), f32(rows, 128), f32(32, 256)],
         compiler_params=params(12),
         name="kernel_weights",
     )(own, summary, other, gram)
 
 
-def velocity_kernel(x_ref, s_ref, other_x, other_s, hi_ref, lo_ref, weight_ref, half_ref, out_ref):
-    half = half_ref[0:1, 0:1]
-    x = x_ref[...]
-    driven = half * s_ref[...]
-    moved_hi, moved_lo = split(jnp.concatenate([driven - x, half * other_s[...] - other_x[...]], axis=0))
-    hi = hi_ref[...]
-    left = jnp.concatenate([hi, hi, lo_ref[...]], axis=1)
-    right = jnp.concatenate([moved_hi, moved_lo, moved_hi], axis=0)
-    out_ref[...] = driven + weight_ref[:, 0:1] * x + nn_dot(left, right)
+def velocity_kernel(x_ref, s_ref, other_x, other_s, weights_ref, weight_ref, half_ref, out_ref, moved_ref):
+    rows, columns = x_ref.shape
+    half = half_ref[...]
+    for column in range(0, columns, 256):
+        column = slice(column, column + 256)
+        for offset, sources in ((0, (x_ref, s_ref)), (rows, (other_x, other_s))):
+            for row in range(0, rows, 32):
+                row = slice(row, row + 32)
+                hi, lo = split(half * sources[1][row, column] - sources[0][row, column])
+                moved_ref[below(row, offset), column] = hi
+                moved_ref[below(row, offset + 2 * rows), column] = lo
+                moved_ref[below(row, offset + 4 * rows), column] = hi
+        out_ref[:, column] = nn_dot(weights_ref[...], moved_ref[:, column])
+        for row in range(0, rows, 32):
+            row = slice(row, row + 32)
+            weight = weight_ref[row, :]
+            weight = jnp.concatenate([weight, weight], axis=1)
+            out_ref[row, column] += half * s_ref[row, column] + weight * x_ref[row, column]
 
 
 def velocity_part(particles, scores, visitor, visitor_scores, weights):
@@ -198,7 +233,8 @@
         in_specs=[block] * 4 + [whole(w) for w in weights],
         out_specs=block,
         out_shape=f32(rows, columns),
-        compiler_params=params(28),
+        scratch_shapes=[pltpu.VMEM((6 * rows, tile), jnp.bfloat16)],
+        compiler_params=params(52),
         cost_estimate=pl.CostEstimate(flops=12 * rows * rows * columns, bytes_accessed=20 * rows * columns, transcendentals=0),
         name="velocity",
     )(particles, scores, visitor, visitor_scores, *weights)

time: 117 us -> 111 us (0.949)
  local copies, waits for them, and re-layouts: 17.3 us -> 0 us
  Pallas kernels: 53.2 us -> 62.3 us
  starting transfers between devices: 7.68 us -> 9.04 us
    unnamed x6 -> x0, local copies, waits for them, and re-layouts: 17.3 us -> none
    pallas_call x1, Pallas kernels: 30.6 us -> 34.3 us  [velocity_part(): pl.pallas_call(velocity_kernel, grid=(columns // tile,), in_specs=[block]...]
    pallas_call x1, Pallas kernels: 7.88 us -> 10.9 us  [own_part(): pl.pallas_call(own_kernel, grid=(columns // tile,), in_specs=[pl.BlockSpe...]
    pallas_call x1, Pallas kernels: 12.5 us -> 14.8 us  [pair_part(): pl.pallas_call(pair_kernel, grid=(columns // tile,), in_specs=[block, blo...]
  transfers between devices with their start and end apart: 5 -> 5, of which waited for: 2 -> 2; matrix products, arithmetic and copies ran while one was open for 0% -> 0% of each run, Pallas kernels for 19% -> 25%
where the time goes in v5:
time: 111 us; the launch traced here: 110 us
  Pallas kernels  62.3 us (56%)
  blocking collectives  30.6 us (28%)
  starting transfers between devices  9.04 us (8%)
  waiting for transfers between devices  8.11 us (7%)
    pallas_call x1, Pallas kernels, velocity_part(): pl.pallas_call(velocity_kernel, grid=(columns // tile,), in_specs=[block]...  34.3 us
    all_to_all x2, blocking collectives, summed_shards(): lax.all_to_all(block.reshape(count, rows // count, columns), 'dim', 0, 0)  30.6 us
    pallas_call x1, Pallas kernels, pair_part(): pl.pallas_call(pair_kernel, grid=(columns // tile,), in_specs=[block, blo...  14.8 us
    pallas_call x1, Pallas kernels, own_part(): pl.pallas_call(own_kernel, grid=(columns // tile,), in_specs=[pl.BlockSpe...  10.9 us
    all_to_all x2, starting transfers between devices, gathered(): return lax.all_to_all(copies, 'dim', 0, 0).reshape(count * rows, columns)  8.03 us
    ppermute x1, waiting for transfers between devices, body(): other = lax.ppermute(summary, ('dim', 'blk'), across)  6.71 us
  transfers between devices with their start and end apart: 5, of which 2 were waited for; matrix products, arithmetic and copies ran while one was open for 0% of the time, Pallas kernels for 25%

profile of v5, /device:TPU:0, one launch (start us, length us, event | category | flops | bytes accessed | tf_op | source)
XLA Modules:
  0.0 110.1 jit_solution(15668601122434157773)
XLA Ops:
  0.0 0.5 collective-permute-start
  0.5 0.1 collective-permute-start.1
  0.5 10.9 %own_gram.1 = f32[256,256]{1,0:T(8,128)S(1)} custom-call(f32[256,16384]{1,0:T(8,128)} %x_ref.3), custom_call_target="tpu_custom_call" | custom-call | flops 4294967296 | bytes 16777216 | tf_op jit(solution)/shard_map/own_gram/pallas_call | solution.py:91
  11.4 16.2 %all_to_all.20.arrived_ref = f32[8,32,256]{2,1,0:T(8,128)S(1)} all-to-all(f32[8,32,256]{2,1,0:T(8,128)S(1)} %bitcast.7), channel_id=1, replica_groups=mesh['grp'=2,'dim'=8,'blk'=2] {'dim'}, dimensions={0} | all-to-all | bytes 524288 | tf_op jit(solution)/shard_map/all_to_all | solution.py:156
  27.6 0.7 sum_shards.2
  28.3 0.0 collective-permute-done.other_ref.other_x
  28.3 4.4 %all-to-all-start.1 = ((f32[8,32,256]{2,1,0:T(8,128)}), f32[8,32,256]{2,1,0:T(8,128)S(1)}, u32[]{:S(2)}, u32[]{:S(2)}) async-start(f32[8,32,256]{2,1,0:T(8,128)} %sum_shards.2), calls=%async_computation.1 | async-start | bytes 524288 | tf_op jit(solution)/shard_map/all_to_all | solution.py:162
  32.8 14.8 %pair_gram.1 = f32[256,256]{1,0:T(8,128)S(1)} custom-call(f32[256,16384]{1,0:T(8,128)} %x_ref.3, f32[256,16384]{1,0:T(8,128)} %collective-permute-done.other_ref.other_x), custom_call_target="tpu_custom_call" | custom-call | flops 6442450944 | bytes 33554432 | tf_op jit(solution)/shard_map/pair_gram/pallas_call | solution.py:129
  47.6 0.0 all-to-all-done.1
  47.6 0.2 summary.1.summary_ref
  47.8 14.5 %all_to_all.21.arrived_ref = f32[8,32,256]{2,1,0:T(8,128)S(1)} all-to-all(f32[8,32,256]{2,1,0:T(8,128)S(1)} %bitcast.6), channel_id=1, replica_groups=mesh['grp'=2,'dim'=8,'blk'=2] {'dim'}, dimensions={0} | all-to-all | bytes 524288 | tf_op jit(solution)/shard_map/all_to_all | solution.py:156
  62.3 0.7 sum_shards.3
  63.0 3.6 %all-to-all-start.3 = ((f32[8,32,256]{2,1,0:T(8,128)}), f32[8,32,256]{2,1,0:T(8,128)S(1)}, u32[]{:S(2)}, u32[]{:S(2)}) async-start(f32[8,32,256]{2,1,0:T(8,128)} %sum_shards.3), calls=%async_computation.3 | async-start | bytes 524288 | tf_op jit(solution)/shard_map/all_to_all | solution.py:162
  66.6 0.5 collective-permute-start.2
  67.1 6.7 %collective-permute-done.2.other_ref = f32[8,256]{1,0:T(8,128)S(1)} collective-permute-done((f32[8,256]{1,0:T(8,128)S(1)}, f32[8,256]{1,0:T(8,128)S(1)}, u32[]{:S(2)}, u32[]{:S(2)}) %collective-permute-start.2) | collective-permute-done | bytes 8224 | tf_op jit(solution)/shard_map/ppermute | solution.py:260
  73.8 1.4 %all-to-all-done.3 = f32[8,32,256]{2,1,0:T(8,128)S(1)} async-done(((f32[8,32,256]{2,1,0:T(8,128)}), f32[8,32,256]{2,1,0:T(8,128)S(1)}, u32[]{:S(2)}, u32[]{:S(2)}) %all-to-all-start.3) | async-done | bytes 262176 | tf_op jit(solution)/shard_map/all_to_all | solution.py:162
  75.2 0.6 kernel_weights.1
  75.8 0.0 collective-permute-done.1.other_s
  75.8 34.3 %velocity.1 = f32[256,16384]{1,0:T(8,128)} custom-call(f32[256,16384]{1,0:T(8,128)} %x_ref.3, f32[256,16384]{1,0:T(8,128)} %s_ref.1, f32[256,16384]{1,0:T(8,128)} %collective-permute-done.other_ref.other_x, f32[256,16384]{1,0:T(8,128)} %collective-permute-done.1.other_s, bf16[256,1536]{1,0:T(8,128)(2,1)S(1)} %get-tuple-element.16.weights_ref, ...), custom_call_target="tpu_custom_call" | custom-call | flops 12884901888 | bytes 83886080 | tf_op jit(solution)/shard_map/velocity/pallas_call | solution.py:230
Async XLA Ops:
  0.0 28.3 %collective-permute-start = (f32[256,16384]{1,0:T(8,128)}, f32[256,16384]{1,0:T(8,128)}, u32[]{:S(2)}, u32[]{:S(2)}) collective-permute-start(f32[256,16384]{1,0:T(8,128)} %x_ref.3), channel_id=1, source_target_pairs={{0,1},{1,0},{2,3},{3,2},{4,5},{5,4},{6,7},{7,6},{8,9},{9,8},{10,11... | collective-permute-start | bytes 50331656 | tf_op jit(solution)/shard_map/ppermute | solution.py:244
  0.5 75.3 %collective-permute-start.1 = (f32[256,16384]{1,0:T(8,128)}, f32[256,16384]{1,0:T(8,128)}, u32[]{:S(2)}, u32[]{:S(2)}) collective-permute-start(f32[256,16384]{1,0:T(8,128)} %s_ref.1), channel_id=1, source_target_pairs={{0,1},{1,0},{2,3},{3,2},{4,5},{5,4},{6,7},{7,6},{8,9},{9,8},{10,11... | collective-permute-start | bytes 50331656 | tf_op jit(solution)/shard_map/ppermute | solution.py:244
  28.3 19.3 %all-to-all-start.1 = ((f32[8,32,256]{2,1,0:T(8,128)}), f32[8,32,256]{2,1,0:T(8,128)S(1)}, u32[]{:S(2)}, u32[]{:S(2)}) async-start(f32[8,32,256]{2,1,0:T(8,128)} %sum_shards.2), calls=%async_computation.1 | async-start | bytes 524288 | tf_op jit(solution)/shard_map/all_to_all | solution.py:162
  63.0 12.2 %all-to-all-start.3 = ((f32[8,32,256]{2,1,0:T(8,128)}), f32[8,32,256]{2,1,0:T(8,128)S(1)}, u32[]{:S(2)}, u32[]{:S(2)}) async-start(f32[8,32,256]{2,1,0:T(8,128)} %sum_shards.3), calls=%async_computation.3 | async-start | bytes 524288 | tf_op jit(solution)/shard_map/all_to_all | solution.py:162
  66.6 7.2 %collective-permute-start.2 = (f32[8,256]{1,0:T(8,128)S(1)}, f32[8,256]{1,0:T(8,128)S(1)}, u32[]{:S(2)}, u32[]{:S(2)}) collective-permute-start(f32[8,256]{1,0:T(8,128)S(1)} %summary.1.summary_ref), channel_id=1, source_target_pairs={{0,3},{1,2},{2,5},{3,4},{4,7},{5,6},{6,9},{7,8},{8,11},{9,10},{10,... | collective-permute-start | bytes 24584 | tf_op jit(solution)/shard_map/ppermute | solution.py:260

commit v6 on v3

--- a/solution.py
+++ b/solution.py
@@ -81,7 +81,7 @@
         out_specs=whole(out),
         out_shape=out,
         scratch_shapes=[pltpu.VMEM((2 * rows, rows), jnp.float32), pltpu.VMEM((rows, 128), jnp.float32)],
-        compiler_params=params(20),
+        compiler_params=params(52),
         cost_estimate=pl.CostEstimate(flops=4 * rows * rows * columns, bytes_accessed=4 * rows * columns, transcendentals=0),
         name="own_gram",
     )(particles)
@@ -110,7 +110,7 @@
         in_specs=[block, block],
         out_specs=whole(out),
         out_shape=out,
-        compiler_params=params(24),
+        compiler_params=params(52),
         cost_estimate=pl.CostEstimate(flops=6 * rows * rows * columns, bytes_accessed=8 * rows * columns, transcendentals=0),
         name="pair_gram",
     )(particles, visitor)
@@ -124,10 +124,12 @@
         out_ref[step] = total
 
 
-def summed_shards(block):
+def summed_shards(block, beside=None):
     count = lax.axis_size("dim")
     rows, columns = block.shape
     arrived = lax.all_to_all(block.reshape(count, rows // count, columns), "dim", 0, 0)
+    if beside is not None:
+        arrived, _ = lax.optimization_barrier((arrived, beside))
     return pl.pallas_call(sum_kernel, out_shape=f32(*arrived.shape), compiler_params=params(8), name="sum_shards")(arrived)
 
 
@@ -178,14 +180,14 @@
 
 
 def velocity_kernel(x_ref, s_ref, other_x, other_s, hi_ref, lo_ref, weight_ref, half_ref, out_ref):
+    rows = out_ref.shape[0]
     half = half_ref[0:1, 0:1]
     x = x_ref[...]
     driven = half * s_ref[...]
     moved_hi, moved_lo = split(jnp.concatenate([driven - x, half * other_s[...] - other_x[...]], axis=0))
     hi = hi_ref[...]
-    left = jnp.concatenate([hi, hi, lo_ref[...]], axis=1)
-    right = jnp.concatenate([moved_hi, moved_lo, moved_hi], axis=0)
-    out_ref[...] = driven + weight_ref[:, 0:1] * x + nn_dot(left, right)
+    both = nn_dot(jnp.concatenate([hi, lo_ref[...]], axis=0), moved_hi)
+    out_ref[...] = driven + weight_ref[:, 0:1] * x + both[:rows] + both[rows:] + nn_dot(hi, moved_lo)
 
 
 def velocity_part(particles, scores, visitor, visitor_scores, weights):
@@ -198,7 +200,7 @@
         in_specs=[block] * 4 + [whole(w) for w in weights],
         out_specs=block,
         out_shape=f32(rows, columns),
-        compiler_params=params(28),
+        compiler_params=params(52),
         cost_estimate=pl.CostEstimate(flops=12 * rows * rows * columns, bytes_accessed=20 * rows * columns, transcendentals=0),
         name="velocity",
     )(particles, scores, visitor, visitor_scores, *weights)
@@ -216,16 +218,12 @@
     visitor = swap(particles)
     visitor_scores = swap(scores)
 
-    own_copies = summed_shards(own_part(particles))
-    visitor, own_copies = lax.optimization_barrier((visitor, own_copies))
-    own = gathered(own_copies)
+    own = gathered(summed_shards(own_part(particles)))
     summary = summary_part(own)
     across = [(d * 2 + b, (d + 1) % count * 2 + 1 - b) for d in range(count) for b in range(2)]
     other = lax.ppermute(summary, ("dim", "blk"), across)
 
-    gram = pair_part(particles, visitor)
-    gram, summary = lax.optimization_barrier((gram, summary))
-    gram = gathered(summed_shards(gram))
+    gram = gathered(summed_shards(pair_part(particles, visitor), other))
     weights = weights_part(own, summary, other, gram, scale_base)
     return velocity_part(particles, scores, visitor, visitor_scores, weights)
 

time: 117 us -> 109 us (0.932)
  local copies, waits for them, and re-layouts: 17.3 us -> 0 us
  Pallas kernels: 53.2 us -> 62.6 us
  starting transfers between devices: 7.68 us -> 10.2 us
  blocking collectives: 30.2 us -> 28.2 us
    unnamed x6 -> x0, local copies, waits for them, and re-layouts: 17.3 us -> none
    all_to_all x2 -> x1, blocking collectives: 30.2 us -> 16.2 us  [summed_shards(): lax.all_to_all(block.reshape(count, rows // count, columns), 'dim', 0, 0)]
    all_to_all x0 -> x1, blocking collectives: none -> 12 us  [gathered(): return lax.all_to_all(copies, 'dim', 0, 0).reshape(count * rows, columns)]
    all_to_all x0 -> x1, starting transfers between devices: none -> 6.01 us  [summed_shards(): lax.all_to_all(block.reshape(count, rows // count, columns), 'dim', 0, 0)]
    pallas_call x1, Pallas kernels: 30.6 us -> 34.5 us  [velocity_part(): pl.pallas_call(velocity_kernel, grid=(columns // tile,), in_specs=[block]...]
    all_to_all x2 -> x1, starting transfers between devices: 7 us -> 3.59 us  [gathered(): return lax.all_to_all(copies, 'dim', 0, 0).reshape(count * rows, columns)]
    pallas_call x1, Pallas kernels: 7.88 us -> 11.2 us  [own_part(): pl.pallas_call(own_kernel, grid=(columns // tile,), in_specs=[pl.BlockSpe...]
    pallas_call x1, Pallas kernels: 12.5 us -> 15.5 us  [pair_part(): pl.pallas_call(pair_kernel, grid=(columns // tile,), in_specs=[block, blo...]
  transfers between devices with their start and end apart: 5 -> 5, of which waited for: 2 -> 2; matrix products, arithmetic and copies ran while one was open for 0% -> 0% of each run, Pallas kernels for 19% -> 26%
where the time goes in v6:
time: 109 us
  Pallas kernels  62.6 us (57%)
  blocking collectives  28.2 us (26%)
  starting transfers between devices  10.2 us (9%)
  waiting for transfers between devices  7.95 us (7%)
    pallas_call x1, Pallas kernels, velocity_part(): pl.pallas_call(velocity_kernel, grid=(columns // tile,), in_specs=[block]...  34.5 us
    all_to_all x1, blocking collectives, summed_shards(): lax.all_to_all(block.reshape(count, rows // count, columns), 'dim', 0, 0)  16.2 us
    pallas_call x1, Pallas kernels, pair_part(): pl.pallas_call(pair_kernel, grid=(columns // tile,), in_specs=[block, blo...  15.5 us
    all_to_all x1, blocking collectives, gathered(): return lax.all_to_all(copies, 'dim', 0, 0).reshape(count * rows, columns)  12 us
    pallas_call x1, Pallas kernels, own_part(): pl.pallas_call(own_kernel, grid=(columns // tile,), in_specs=[pl.BlockSpe...  11.2 us
    ppermute x1, waiting for transfers between devices, body(): other = lax.ppermute(summary, ('dim', 'blk'), across)  6.04 us
    all_to_all x1, starting transfers between devices, summed_shards(): lax.all_to_all(block.reshape(count, rows // count, columns), 'dim', 0, 0)  6.01 us
    all_to_all x1, starting transfers between devices, gathered(): return lax.all_to_all(copies, 'dim', 0, 0).reshape(count * rows, columns)  3.59 us
  transfers between devices with their start and end apart: 5, of which 2 were waited for; matrix products, arithmetic and copies ran while one was open for 0% of the time, Pallas kernels for 26%

profile of v6, /device:TPU:0, one launch (start us, length us, event | category | flops | bytes accessed | tf_op | source)
XLA Modules:
  0.0 109.0 jit_solution(7242569625454298330)
XLA Ops:
  0.0 0.5 collective-permute-start
  0.5 0.1 collective-permute-start.1
  0.5 11.2 %own_gram.1 = f32[256,256]{1,0:T(8,128)S(1)} custom-call(f32[256,16384]{1,0:T(8,128)} %x_ref.3), custom_call_target="tpu_custom_call" | custom-call | flops 4294967296 | bytes 16777216 | tf_op jit(solution)/shard_map/own_gram/pallas_call | solution.py:77
  11.7 16.2 %all_to_all.20.arrived_ref = f32[8,32,256]{2,1,0:T(8,128)S(1)} all-to-all(f32[8,32,256]{2,1,0:T(8,128)S(1)} %bitcast.6), channel_id=1, replica_groups=mesh['grp'=2,'dim'=8,'blk'=2] {'dim'}, dimensions={0} | all-to-all | bytes 524288 | tf_op jit(solution)/shard_map/all_to_all | solution.py:130
  27.8 0.7 sum_shards.2
  28.6 3.6 %all-to-all-start.1 = ((f32[8,32,256]{2,1,0:T(8,128)}), f32[8,32,256]{2,1,0:T(8,128)S(1)}, u32[]{:S(2)}, u32[]{:S(2)}) async-start(f32[8,32,256]{2,1,0:T(8,128)} %sum_shards.2), calls=%async_computation.1 | async-start | bytes 524288 | tf_op jit(solution)/shard_map/all_to_all | solution.py:138
  32.2 0.0 collective-permute-done.other_ref.other_x
  32.2 15.5 %pair_gram.1 = f32[256,256]{1,0:T(8,128)} custom-call(f32[256,16384]{1,0:T(8,128)} %x_ref.3, f32[256,16384]{1,0:T(8,128)} %collective-permute-done.other_ref.other_x), custom_call_target="tpu_custom_call" | custom-call | flops 6442450944 | bytes 33554432 | tf_op jit(solution)/shard_map/pair_gram/pallas_call | solution.py:107
  47.7 0.0 all-to-all-done.1
  47.7 6.0 %all-to-all-start.2 = ((f32[8,32,256]{2,1,0:T(8,128)}), f32[8,32,256]{2,1,0:T(8,128)S(1)}, u32[]{:S(2)}, u32[]{:S(2)}) async-start(f32[8,32,256]{2,1,0:T(8,128)} %bitcast.2), calls=%async_computation.2 | async-start | bytes 524288 | tf_op jit(solution)/shard_map/all_to_all | solution.py:130
  53.7 0.2 summary.1.summary_ref
  53.9 0.1 collective-permute-start.2
  54.0 6.0 %collective-permute-done.2.other_ref = f32[8,256]{1,0:T(8,128)S(1)} collective-permute-done((f32[8,256]{1,0:T(8,128)S(1)}, f32[8,256]{1,0:T(8,128)S(1)}, u32[]{:S(2)}, u32[]{:S(2)}) %collective-permute-start.2) | collective-permute-done | bytes 8224 | tf_op jit(solution)/shard_map/ppermute | solution.py:224
  60.0 1.9 %all-to-all-done.2.arrived_ref = f32[8,32,256]{2,1,0:T(8,128)S(1)} async-done(((f32[8,32,256]{2,1,0:T(8,128)}), f32[8,32,256]{2,1,0:T(8,128)S(1)}, u32[]{:S(2)}, u32[]{:S(2)}) %all-to-all-start.2) | async-done | bytes 262176 | tf_op jit(solution)/shard_map/all_to_all | solution.py:130
  61.9 12.0 %all_to_all.21 = f32[8,32,256]{2,1,0:T(8,128)S(1)} all-to-all(f32[8,32,256]{2,1,0:T(8,128)S(1)} %sum_shards.3), channel_id=1, replica_groups=mesh['grp'=2,'dim'=8,'blk'=2] {'dim'}, dimensions={0} | all-to-all | bytes 524288 | tf_op jit(solution)/shard_map/all_to_all | solution.py:138
  74.0 0.6 kernel_weights.1
  74.5 0.0 collective-permute-done.1.other_s
  74.5 34.5 %velocity.1 = f32[256,16384]{1,0:T(8,128)} custom-call(f32[256,16384]{1,0:T(8,128)} %x_ref.3, f32[256,16384]{1,0:T(8,128)} %s_ref.1, f32[256,16384]{1,0:T(8,128)} %collective-permute-done.other_ref.other_x, f32[256,16384]{1,0:T(8,128)} %collective-permute-done.1.other_s, bf16[256,512]{1,0:T(8,128)(2,1)S(1)} %get-tuple-element.11.hi_ref, ...), custom_call_target="tpu_custom_call" | custom-call | flops 12884901888 | bytes 83886080 | tf_op jit(solution)/shard_map/velocity/pallas_call | solution.py:197
  (1 shorter events, 0.0 us)
Async XLA Ops:
  0.0 32.2 %collective-permute-start = (f32[256,16384]{1,0:T(8,128)}, f32[256,16384]{1,0:T(8,128)}, u32[]{:S(2)}, u32[]{:S(2)}) collective-permute-start(f32[256,16384]{1,0:T(8,128)} %x_ref.3), channel_id=1, source_target_pairs={{0,1},{1,0},{2,3},{3,2},{4,5},{5,4},{6,7},{7,6},{8,9},{9,8},{10,11... | collective-permute-start | bytes 50331656 | tf_op jit(solution)/shard_map/ppermute | solution.py:210
  0.5 74.1 %collective-permute-start.1 = (f32[256,16384]{1,0:T(8,128)}, f32[256,16384]{1,0:T(8,128)}, u32[]{:S(2)}, u32[]{:S(2)}) collective-permute-start(f32[256,16384]{1,0:T(8,128)} %s_ref.1), channel_id=1, source_target_pairs={{0,1},{1,0},{2,3},{3,2},{4,5},{5,4},{6,7},{7,6},{8,9},{9,8},{10,11... | collective-permute-start | bytes 50331656 | tf_op jit(solution)/shard_map/ppermute | solution.py:210
  28.6 19.1 %all-to-all-start.1 = ((f32[8,32,256]{2,1,0:T(8,128)}), f32[8,32,256]{2,1,0:T(8,128)S(1)}, u32[]{:S(2)}, u32[]{:S(2)}) async-start(f32[8,32,256]{2,1,0:T(8,128)} %sum_shards.2), calls=%async_computation.1 | async-start | bytes 524288 | tf_op jit(solution)/shard_map/all_to_all | solution.py:138
  47.7 14.2 %all-to-all-start.2 = ((f32[8,32,256]{2,1,0:T(8,128)}), f32[8,32,256]{2,1,0:T(8,128)S(1)}, u32[]{:S(2)}, u32[]{:S(2)}) async-start(f32[8,32,256]{2,1,0:T(8,128)} %bitcast.2), calls=%async_computation.2 | async-start | bytes 524288 | tf_op jit(solution)/shard_map/all_to_all | solution.py:130
  53.9 6.1 %collective-permute-start.2 = (f32[8,256]{1,0:T(8,128)S(1)}, f32[8,256]{1,0:T(8,128)S(1)}, u32[]{:S(2)}, u32[]{:S(2)}) collective-permute-start(f32[8,256]{1,0:T(8,128)S(1)} %summary.1.summary_ref), channel_id=1, source_target_pairs={{0,3},{1,2},{2,5},{3,4},{4,7},{5,6},{6,9},{7,8},{8,11},{9,10},{10,... | collective-permute-start | bytes 24584 | tf_op jit(solution)/shard_map/ppermute | solution.py:224

commit v7 on v6

--- a/solution.py
+++ b/solution.py
@@ -9,8 +9,9 @@
 from jax.sharding import PartitionSpec as P
 
 GRAM_TILE = 2048
-VELOCITY_TILE = 1024
+VELOCITY_TILE = 2048
 MIB = 1024 * 1024
+BOTH = ("dim", "blk")
 
 
 def params(limit):
@@ -87,7 +88,7 @@
     )(particles)
 
 
-def pair_kernel(mine_ref, other_ref, gram_ref):
+def pair_kernel(core_ref, mine_ref, other_ref, out_ref, gram_ref):
     @pl.when(pl.program_id(0) == 0)
     def _():
         gram_ref[...] = jnp.zeros_like(gram_ref)
@@ -98,22 +99,33 @@
     both = nt_dot(jnp.concatenate([my_hi, my_lo], axis=0), hi)
     gram_ref[...] += both[:rows] + both[rows:] + nt_dot(my_hi, lo)
 
-
-def pair_part(particles, visitor):
+    @pl.when(pl.program_id(0) == pl.num_programs(0) - 1)
+    def _():
+        gram = gram_ref[...]
+        out_ref[...] = jnp.where(core_ref[0] == 0, gram, gram.T)
+
+
+def pair_part(core, particles, visitor):
     rows, columns = particles.shape
-    tile = min(GRAM_TILE, columns)
+    width = columns // 2
+    tile = min(GRAM_TILE, width)
+    tiles = width // tile
     out = f32(rows, rows)
-    block = pl.BlockSpec((rows, tile), lambda i: (0, i))
+    block = pl.BlockSpec((rows, tile), lambda i, core: (0, core[0] * tiles + i))
     return pl.pallas_call(
         pair_kernel,
-        grid=(columns // tile,),
-        in_specs=[block, block],
-        out_specs=whole(out),
+        grid_spec=pltpu.PrefetchScalarGridSpec(
+            num_scalar_prefetch=1,
+            grid=(tiles,),
+            in_specs=[block, block],
+            out_specs=pl.BlockSpec(out.shape, lambda i, core: (0, 0)),
+            scratch_shapes=[pltpu.VMEM((rows, rows), jnp.float32)],
+        ),
         out_shape=out,
         compiler_params=params(52),
-        cost_estimate=pl.CostEstimate(flops=6 * rows * rows * columns, bytes_accessed=8 * rows * columns, transcendentals=0),
+        cost_estimate=pl.CostEstimate(flops=6 * rows * rows * width, bytes_accessed=8 * rows * width, transcendentals=0),
         name="pair_gram",
-    )(particles, visitor)
+    )(core, particles, visitor)
 
 
 def sum_kernel(arrived_ref, out_ref):
@@ -124,18 +136,18 @@
         out_ref[step] = total
 
 
-def summed_shards(block, beside=None):
-    count = lax.axis_size("dim")
+def summed_shards(block, axes, beside=None):
+    count = lax.axis_size(axes)
     rows, columns = block.shape
-    arrived = lax.all_to_all(block.reshape(count, rows // count, columns), "dim", 0, 0)
+    arrived = lax.all_to_all(block.reshape(count, rows // count, columns), axes, 0, 0)
     if beside is not None:
         arrived, _ = lax.optimization_barrier((arrived, beside))
     return pl.pallas_call(sum_kernel, out_shape=f32(*arrived.shape), compiler_params=params(8), name="sum_shards")(arrived)
 
 
-def gathered(copies):
+def gathered(copies, axes):
     count, rows, columns = copies.shape
-    return lax.all_to_all(copies, "dim", 0, 0).reshape(count * rows, columns)
+    return lax.all_to_all(copies, axes, 0, 0).reshape(count * rows, columns)
 
 
 def summary_kernel(own_ref, out_ref):
@@ -151,12 +163,13 @@
     return pl.pallas_call(summary_kernel, out_shape=f32(8, own.shape[0]), compiler_params=params(8), name="summary")(own)
 
 
-def weights_kernel(scale_base, own_ref, summary_ref, other_ref, gram_ref, hi_ref, lo_ref, weight_ref, half_ref):
+def weights_kernel(scale_base, core_ref, own_ref, summary_ref, other_ref, gram_ref, hi_ref, lo_ref, weight_ref, half_ref):
     own = own_ref[...]
     rows = own.shape[0]
     diagonal = on_diagonal(rows)
     norms = jnp.sum(jnp.where(diagonal, own, 0.0), axis=1, keepdims=True)
-    pair = norms + other_ref[0:1, :] - 2.0 * gram_ref[...]
+    gram = gram_ref[...]
+    pair = norms + other_ref[0:1, :] - 2.0 * jnp.where(core_ref[0] == 0, gram, gram.T)
     spread = summary_ref[1:2, 0:1] + other_ref[1:2, 0:1] + 2.0 * jnp.sum(pair)
     width = spread / scale_base
     inverse = -1.0 / width
@@ -168,15 +181,16 @@
     half_ref[...] = jnp.broadcast_to(0.5 * width, half_ref.shape)
 
 
-def weights_part(own, summary, other, gram, scale_base):
+def weights_part(core, own, summary, other, gram, scale_base):
     rows = own.shape[0]
     half = jax.ShapeDtypeStruct((rows, 2 * rows), jnp.bfloat16)
     return pl.pallas_call(
         functools.partial(weights_kernel, scale_base),
+        in_specs=[pl.BlockSpec(memory_space=pltpu.SMEM)] + [pl.BlockSpec(memory_space=pltpu.VMEM)] * 4,
         out_shape=[half, half, f32(rows, 128), f32(8, 128)],
         compiler_params=params(12),
         name="kernel_weights",
-    )(own, summary, other, gram)
+    )(core, own, summary, other, gram)
 
 
 def velocity_kernel(x_ref, s_ref, other_x, other_s, hi_ref, lo_ref, weight_ref, half_ref, out_ref):
@@ -215,16 +229,21 @@
     total_rows = particles.shape[0] * lax.axis_size("blk")
     scale_base = total_rows * total_rows * math.log(total_rows)
 
+    core = lax.axis_index("blk").reshape(1)
     visitor = swap(particles)
-    visitor_scores = swap(scores)
-
-    own = gathered(summed_shards(own_part(particles)))
+
+    own_copies = summed_shards(own_part(particles), "dim")
+    own = gathered(own_copies, "dim")
     summary = summary_part(own)
     across = [(d * 2 + b, (d + 1) % count * 2 + 1 - b) for d in range(count) for b in range(2)]
-    other = lax.ppermute(summary, ("dim", "blk"), across)
-
-    gram = gathered(summed_shards(pair_part(particles, visitor), other))
-    weights = weights_part(own, summary, other, gram, scale_base)
+    other = lax.ppermute(summary, BOTH, across)
+
+    visitor, _ = lax.optimization_barrier((visitor, own_copies))
+    gram = pair_part(core, particles, visitor)
+    scores_late, gram = lax.optimization_barrier((scores, gram))
+    visitor_scores = swap(scores_late)
+    gram = gathered(summed_shards(gram, BOTH, other), BOTH)
+    weights = weights_part(core, own, summary, other, gram, scale_base)
     return velocity_part(particles, scores, visitor, visitor_scores, weights)
 
 

time: 109 us -> 109 us (level)
  Pallas kernels: 62.6 us -> 52.4 us
  waiting for transfers between devices: 7.95 us -> 17.8 us
  starting transfers between devices: 10.2 us -> 12.7 us
  blocking collectives: 28.2 us -> 26.1 us
    all_to_all x2, waiting for transfers between devices: 1.9 us -> 9.99 us  [summed_shards(): lax.all_to_all(block.reshape(count, rows // count, columns), axes, 0, 0)]
    pallas_call x2, Pallas kernels: 16.1 us -> 9.44 us  [the longest x1 8.79 us: pair_part(): pl.pallas_call(pair_kernel, grid_spec=pltpu.PrefetchScalarGridSpec(num_sc...]
    pallas_call x1, Pallas kernels: 34.5 us -> 30.8 us  [velocity_part(): pl.pallas_call(velocity_kernel, grid=(columns // tile,), in_specs=[block]...]
    all_to_all x2, blocking collectives: 28.2 us -> 26.1 us  [gathered(): return lax.all_to_all(copies, axes, 0, 0).reshape(count * rows, columns)]
    ppermute x1, waiting for transfers between devices: 6.04 us -> 7.8 us  [body(): other = lax.ppermute(summary, BOTH, across)]
    ppermute x1, starting transfers between devices: 0.06 us -> 1.73 us  [body(): other = lax.ppermute(summary, BOTH, across)]
  transfers between devices with their start and end apart: 5 -> 5, of which waited for: 2 -> 3; matrix products, arithmetic and copies ran while one was open for 0% -> 0% of each run, Pallas kernels for 26% -> 12%
where the time goes in v7:
time: 109 us
  Pallas kernels  52.4 us (48%)
  blocking collectives  26.1 us (24%)
  waiting for transfers between devices  17.8 us (16%)
  starting transfers between devices  12.7 us (12%)
    pallas_call x1, Pallas kernels, velocity_part(): pl.pallas_call(velocity_kernel, grid=(columns // tile,), in_specs=[block]...  30.8 us
    all_to_all x2, blocking collectives, gathered(): return lax.all_to_all(copies, axes, 0, 0).reshape(count * rows, columns)  26.1 us
    pallas_call x1, Pallas kernels, own_part(): pl.pallas_call(own_kernel, grid=(columns // tile,), in_specs=[pl.BlockSpe...  11.8 us
    all_to_all x2, starting transfers between devices, summed_shards(): lax.all_to_all(block.reshape(count, rows // count, columns), axes, 0, 0)  10.5 us
    all_to_all x2, waiting for transfers between devices, summed_shards(): lax.all_to_all(block.reshape(count, rows // count, columns), axes, 0, 0)  9.99 us
    pallas_call x1, Pallas kernels, pair_part(): pl.pallas_call(pair_kernel, grid_spec=pltpu.PrefetchScalarGridSpec(num_sc...  8.79 us
    ppermute x1, waiting for transfers between devices, body(): other = lax.ppermute(summary, BOTH, across)  7.8 us
  transfers between devices with their start and end apart: 5, of which 3 were waited for; matrix products, arithmetic and copies ran while one was open for 0% of the time, Pallas kernels for 12%

profile of v7, /device:TPU:0, one launch (start us, length us, event | category | flops | bytes accessed | tf_op | source)
XLA Modules:
  0.0 109.0 jit_solution(18192247420405167578)
XLA Ops:
  0.0 0.5 collective-permute-start
  0.5 11.8 %own_gram.1 = f32[256,256]{1,0:T(8,128)} custom-call(f32[256,16384]{1,0:T(8,128)} %x_ref.3), custom_call_target="tpu_custom_call" | custom-call | flops 4294967296 | bytes 16777216 | tf_op jit(solution)/shard_map/own_gram/pallas_call | solution.py:78
  12.3 6.8 %all-to-all-start = ((f32[8,32,256]{2,1,0:T(8,128)}), f32[8,32,256]{2,1,0:T(8,128)S(1)}, u32[]{:S(2)}, u32[]{:S(2)}) async-start(f32[8,32,256]{2,1,0:T(8,128)} %bitcast), calls=%async_computation | async-start | bytes 524288 | tf_op jit(solution)/shard_map/all_to_all | solution.py:142
  19.1 9.6 %all-to-all-done.arrived_ref = f32[8,32,256]{2,1,0:T(8,128)S(1)} async-done(((f32[8,32,256]{2,1,0:T(8,128)}), f32[8,32,256]{2,1,0:T(8,128)S(1)}, u32[]{:S(2)}, u32[]{:S(2)}) %all-to-all-start) | async-done | bytes 262176 | tf_op jit(solution)/shard_map/all_to_all | solution.py:142
  28.8 0.0 collective-permute-done.other_ref.other_x
  28.8 8.8 %pair_gram.1 = f32[256,256]{1,0:T(8,128)} custom-call(s32[1]{0:T(128)} %bitcast.1.core_ref, f32[256,16384]{1,0:T(8,128)} %x_ref.3, f32[256,16384]{1,0:T(8,128)} %collective-permute-done.other_ref.other_x), custom_call_target="tpu_custom_call" | custom-call | flops 3221225472 | bytes 16777216 | tf_op jit(solution)/shard_map/pair_gram/pallas_call | solution.py:115
  37.6 0.0 collective-permute-start.1
  37.6 13.4 %all_to_all.20 = f32[8,32,256]{2,1,0:T(8,128)S(1)} all-to-all(f32[8,32,256]{2,1,0:T(8,128)S(1)} %sum_shards.2), channel_id=1, replica_groups=mesh['grp'=2,'dim'=8,'blk'=2] {'dim'}, dimensions={0} | all-to-all | bytes 524288 | tf_op jit(solution)/shard_map/all_to_all | solution.py:150
  50.9 3.7 %all-to-all-start.2 = ((f32[16,16,256]{2,1,0:T(8,128)}), f32[16,16,256]{2,1,0:T(8,128)S(1)}, u32[]{:S(2)}, u32[]{:S(2)}) async-start(f32[16,16,256]{2,1,0:T(8,128)} %bitcast.3), calls=%async_computation.2 | async-start | bytes 524288 | tf_op jit(solution)/shard_map/all_to_all | solution.py:142
  54.6 0.2 summary.1.summary_ref
  54.9 1.7 %collective-permute-start.2 = (f32[8,256]{1,0:T(8,128)S(1)}, f32[8,256]{1,0:T(8,128)S(1)}, u32[]{:S(2)}, u32[]{:S(2)}) collective-permute-start(f32[8,256]{1,0:T(8,128)S(1)} %summary.1.summary_ref), channel_id=1, source_target_pairs={{0,3},{1,2},{2,5},{3,4},{4,7},{5,6},{6,9},{7,8},{8,11},{9,10},{10,... | collective-permute-start | bytes 24584 | tf_op jit(solution)/shard_map/ppermute | solution.py:239
  56.6 7.8 %collective-permute-done.2.other_ref = f32[8,256]{1,0:T(8,128)S(1)} collective-permute-done((f32[8,256]{1,0:T(8,128)S(1)}, f32[8,256]{1,0:T(8,128)S(1)}, u32[]{:S(2)}, u32[]{:S(2)}) %collective-permute-start.2) | collective-permute-done | bytes 8224 | tf_op jit(solution)/shard_map/ppermute | solution.py:239
  64.4 0.4 all-to-all-done.2.arrived_ref
  64.8 12.7 %all_to_all.21 = f32[16,16,256]{2,1,0:T(8,128)S(1)} all-to-all(f32[16,16,256]{2,1,0:T(8,128)S(1)} %sum_shards.3), channel_id=1, replica_groups=mesh['grp'=2,'dim'=8,'blk'=2] {'dim','blk'}, dimensions={0} | all-to-all | bytes 524288 | tf_op jit(solution)/shard_map/all_to_all | solution.py:150
  77.6 0.6 kernel_weights.1
  78.2 0.0 collective-permute-done.1.other_s
  78.2 30.8 %velocity.1 = f32[256,16384]{1,0:T(8,128)} custom-call(f32[256,16384]{1,0:T(8,128)} %x_ref.3, f32[256,16384]{1,0:T(8,128)} %s_ref.1, f32[256,16384]{1,0:T(8,128)} %collective-permute-done.other_ref.other_x, f32[256,16384]{1,0:T(8,128)} %collective-permute-done.1.other_s, bf16[256,512]{1,0:T(8,128)(2,1)S(1)} %get-tuple-element.17.hi_ref, ...), custom_call_target="tpu_custom_call" | custom-call | flops 12884901888 | bytes 83886080 | tf_op jit(solution)/shard_map/velocity/pallas_call | solution.py:211
  (2 shorter events, 0.1 us)
Async XLA Ops:
  0.0 28.8 %collective-permute-start = (f32[256,16384]{1,0:T(8,128)}, f32[256,16384]{1,0:T(8,128)}, u32[]{:S(2)}, u32[]{:S(2)}) collective-permute-start(f32[256,16384]{1,0:T(8,128)} %x_ref.3), channel_id=1, source_target_pairs={{0,1},{1,0},{2,3},{3,2},{4,5},{5,4},{6,7},{7,6},{8,9},{9,8},{10,11... | collective-permute-start | bytes 50331656 | tf_op jit(solution)/shard_map/ppermute | solution.py:224
  12.3 16.4 %all-to-all-start = ((f32[8,32,256]{2,1,0:T(8,128)}), f32[8,32,256]{2,1,0:T(8,128)S(1)}, u32[]{:S(2)}, u32[]{:S(2)}) async-start(f32[8,32,256]{2,1,0:T(8,128)} %bitcast), calls=%async_computation | async-start | bytes 524288 | tf_op jit(solution)/shard_map/all_to_all | solution.py:142
  37.6 40.6 %collective-permute-start.1 = (f32[256,16384]{1,0:T(8,128)}, f32[256,16384]{1,0:T(8,128)}, u32[]{:S(2)}, u32[]{:S(2)}) collective-permute-start(f32[256,16384]{1,0:T(8,128)} %s_ref.1), channel_id=1, source_target_pairs={{0,1},{1,0},{2,3},{3,2},{4,5},{5,4},{6,7},{7,6},{8,9},{9,8},{10,11... | collective-permute-start | bytes 50331656 | tf_op jit(solution)/shard_map/ppermute | solution.py:224
  50.9 13.8 %all-to-all-start.2 = ((f32[16,16,256]{2,1,0:T(8,128)}), f32[16,16,256]{2,1,0:T(8,128)S(1)}, u32[]{:S(2)}, u32[]{:S(2)}) async-start(f32[16,16,256]{2,1,0:T(8,128)} %bitcast.3), calls=%async_computation.2 | async-start | bytes 524288 | tf_op jit(solution)/shard_map/all_to_all | solution.py:142
  54.9 9.5 %collective-permute-start.2 = (f32[8,256]{1,0:T(8,128)S(1)}, f32[8,256]{1,0:T(8,128)S(1)}, u32[]{:S(2)}, u32[]{:S(2)}) collective-permute-start(f32[8,256]{1,0:T(8,128)S(1)} %summary.1.summary_ref), channel_id=1, source_target_pairs={{0,3},{1,2},{2,5},{3,4},{4,7},{5,6},{6,9},{7,8},{8,11},{9,10},{10,... | collective-permute-start | bytes 24584 | tf_op jit(solution)/shard_map/ppermute | solution.py:239

commit v8 on v7

--- a/solution.py
+++ b/solution.py
@@ -231,18 +231,15 @@
 
     core = lax.axis_index("blk").reshape(1)
     visitor = swap(particles)
-
-    own_copies = summed_shards(own_part(particles), "dim")
-    own = gathered(own_copies, "dim")
+    visitor_scores = swap(scores)
+
+    own = gathered(summed_shards(own_part(particles), "dim"), "dim")
     summary = summary_part(own)
     across = [(d * 2 + b, (d + 1) % count * 2 + 1 - b) for d in range(count) for b in range(2)]
     other = lax.ppermute(summary, BOTH, across)
 
-    visitor, _ = lax.optimization_barrier((visitor, own_copies))
-    gram = pair_part(core, particles, visitor)
-    scores_late, gram = lax.optimization_barrier((scores, gram))
-    visitor_scores = swap(scores_late)
-    gram = gathered(summed_shards(gram, BOTH, other), BOTH)
+    gram = summed_shards(pair_part(core, particles, visitor), BOTH, other)
+    gram = gathered(gram, BOTH)
     weights = weights_part(core, own, summary, other, gram, scale_base)
     return velocity_part(particles, scores, visitor, visitor_scores, weights)
 

time: 109 us -> 102 us (0.936)
  waiting for transfers between devices: 17.8 us -> 8.19 us
  blocking collectives: 26.1 us -> 28.9 us
    all_to_all x0 -> x1, blocking collectives: none -> 16.2 us  [summed_shards(): lax.all_to_all(block.reshape(count, rows // count, columns), axes, 0, 0)]
    all_to_all x2 -> x1, blocking collectives: 26.1 us -> 12.7 us  [gathered(): return lax.all_to_all(copies, axes, 0, 0).reshape(count * rows, columns)]
    all_to_all x2 -> x1, waiting for transfers between devices: 9.99 us -> 0.39 us  [summed_shards(): lax.all_to_all(block.reshape(count, rows // count, columns), axes, 0, 0)]
    all_to_all x2 -> x1, starting transfers between devices: 10.5 us -> 6.09 us  [summed_shards(): lax.all_to_all(block.reshape(count, rows // count, columns), axes, 0, 0)]
    all_to_all x0 -> x1, starting transfers between devices: none -> 3.59 us  [gathered(): return lax.all_to_all(copies, axes, 0, 0).reshape(count * rows, columns)]
  transfers between devices with their start and end apart: 5 -> 5, of which waited for: 3 -> 2; matrix products, arithmetic and copies ran while one was open for 0% -> 0% of each run, Pallas kernels for 12% -> 21%
where the time goes in v8:
time: 102 us; the launch traced here: 101 us
  Pallas kernels  52.4 us (51%)
  blocking collectives  28.9 us (28%)
  starting transfers between devices  11.9 us (12%)
  waiting for transfers between devices  8.19 us (8%)
    pallas_call x1, Pallas kernels, velocity_part(): pl.pallas_call(velocity_kernel, grid=(columns // tile,), in_specs=[block]...  30.8 us
    all_to_all x1, blocking collectives, summed_shards(): lax.all_to_all(block.reshape(count, rows // count, columns), axes, 0, 0)  16.2 us
    all_to_all x1, blocking collectives, gathered(): return lax.all_to_all(copies, axes, 0, 0).reshape(count * rows, columns)  12.7 us
    pallas_call x1, Pallas kernels, own_part(): pl.pallas_call(own_kernel, grid=(columns // tile,), in_specs=[pl.BlockSpe...  11.2 us
    pallas_call x1, Pallas kernels, pair_part(): pl.pallas_call(pair_kernel, grid_spec=pltpu.PrefetchScalarGridSpec(num_sc...  8.79 us
    ppermute x1, waiting for transfers between devices, body(): other = lax.ppermute(summary, BOTH, across)  7.8 us
    all_to_all x1, starting transfers between devices, summed_shards(): lax.all_to_all(block.reshape(count, rows // count, columns), axes, 0, 0)  6.09 us
    all_to_all x1, starting transfers between devices, gathered(): return lax.all_to_all(copies, axes, 0, 0).reshape(count * rows, columns)  3.59 us
  transfers between devices with their start and end apart: 5, of which 2 were waited for; matrix products, arithmetic and copies ran while one was open for 0% of the time, Pallas kernels for 21%

profile of v8, /device:TPU:0, one launch (start us, length us, event | category | flops | bytes accessed | tf_op | source)
XLA Modules:
  0.0 101.4 jit_solution(11939453014580742639)
XLA Ops:
  0.0 0.5 collective-permute-start
  0.5 0.1 collective-permute-start.1
  0.5 11.2 %own_gram.1 = f32[256,256]{1,0:T(8,128)S(1)} custom-call(f32[256,16384]{1,0:T(8,128)} %x_ref.3), custom_call_target="tpu_custom_call" | custom-call | flops 4294967296 | bytes 16777216 | tf_op jit(solution)/shard_map/own_gram/pallas_call | solution.py:78
  11.7 16.2 %all_to_all.20.arrived_ref = f32[8,32,256]{2,1,0:T(8,128)S(1)} all-to-all(f32[8,32,256]{2,1,0:T(8,128)S(1)} %bitcast.7), channel_id=1, replica_groups=mesh['grp'=2,'dim'=8,'blk'=2] {'dim'}, dimensions={0} | all-to-all | bytes 524288 | tf_op jit(solution)/shard_map/all_to_all | solution.py:142
  27.8 0.7 sum_shards.2
  28.6 3.6 %all-to-all-start.1 = ((f32[8,32,256]{2,1,0:T(8,128)}), f32[8,32,256]{2,1,0:T(8,128)S(1)}, u32[]{:S(2)}, u32[]{:S(2)}) async-start(f32[8,32,256]{2,1,0:T(8,128)} %sum_shards.2), calls=%async_computation.1 | async-start | bytes 524288 | tf_op jit(solution)/shard_map/all_to_all | solution.py:150
  32.2 0.0 collective-permute-done.other_ref.other_x
  32.2 8.8 %pair_gram.1 = f32[256,256]{1,0:T(8,128)} custom-call(s32[1]{0:T(128)} %bitcast.core_ref, f32[256,16384]{1,0:T(8,128)} %x_ref.3, f32[256,16384]{1,0:T(8,128)} %collective-permute-done.other_ref.other_x), custom_call_target="tpu_custom_call" | custom-call | flops 3221225472 | bytes 16777216 | tf_op jit(solution)/shard_map/pair_gram/pallas_call | solution.py:115
  40.9 0.0 all-to-all-done.1
  41.0 6.1 %all-to-all-start.2 = ((f32[16,16,256]{2,1,0:T(8,128)}), f32[16,16,256]{2,1,0:T(8,128)S(1)}, u32[]{:S(2)}, u32[]{:S(2)}) async-start(f32[16,16,256]{2,1,0:T(8,128)} %bitcast.3), calls=%async_computation.2 | async-start | bytes 524288 | tf_op jit(solution)/shard_map/all_to_all | solution.py:142
  47.0 0.2 summary.1.summary_ref
  47.3 1.7 %collective-permute-start.2 = (f32[8,256]{1,0:T(8,128)S(1)}, f32[8,256]{1,0:T(8,128)S(1)}, u32[]{:S(2)}, u32[]{:S(2)}) collective-permute-start(f32[8,256]{1,0:T(8,128)S(1)} %summary.1.summary_ref), channel_id=1, source_target_pairs={{0,3},{1,2},{2,5},{3,4},{4,7},{5,6},{6,9},{7,8},{8,11},{9,10},{10,... | collective-permute-start | bytes 24584 | tf_op jit(solution)/shard_map/ppermute | solution.py:239
  49.0 7.8 %collective-permute-done.2.other_ref = f32[8,256]{1,0:T(8,128)S(1)} collective-permute-done((f32[8,256]{1,0:T(8,128)S(1)}, f32[8,256]{1,0:T(8,128)S(1)}, u32[]{:S(2)}, u32[]{:S(2)}) %collective-permute-start.2) | collective-permute-done | bytes 8224 | tf_op jit(solution)/shard_map/ppermute | solution.py:239
  56.8 0.4 all-to-all-done.2.arrived_ref
  57.2 12.7 %all_to_all.21 = f32[16,16,256]{2,1,0:T(8,128)S(1)} all-to-all(f32[16,16,256]{2,1,0:T(8,128)S(1)} %sum_shards.3), channel_id=1, replica_groups=mesh['grp'=2,'dim'=8,'blk'=2] {'dim','blk'}, dimensions={0} | all-to-all | bytes 524288 | tf_op jit(solution)/shard_map/all_to_all | solution.py:150
  70.0 0.6 kernel_weights.1
  70.6 0.0 collective-permute-done.1.other_s
  70.6 30.8 %velocity.1 = f32[256,16384]{1,0:T(8,128)} custom-call(f32[256,16384]{1,0:T(8,128)} %x_ref.3, f32[256,16384]{1,0:T(8,128)} %s_ref.1, f32[256,16384]{1,0:T(8,128)} %collective-permute-done.other_ref.other_x, f32[256,16384]{1,0:T(8,128)} %collective-permute-done.1.other_s, bf16[256,512]{1,0:T(8,128)(2,1)S(1)} %get-tuple-element.11.hi_ref, ...), custom_call_target="tpu_custom_call" | custom-call | flops 12884901888 | bytes 83886080 | tf_op jit(solution)/shard_map/velocity/pallas_call | solution.py:211
  (1 shorter events, 0.0 us)
Async XLA Ops:
  0.0 32.2 %collective-permute-start = (f32[256,16384]{1,0:T(8,128)}, f32[256,16384]{1,0:T(8,128)}, u32[]{:S(2)}, u32[]{:S(2)}) collective-permute-start(f32[256,16384]{1,0:T(8,128)} %x_ref.3), channel_id=1, source_target_pairs={{0,1},{1,0},{2,3},{3,2},{4,5},{5,4},{6,7},{7,6},{8,9},{9,8},{10,11... | collective-permute-start | bytes 50331656 | tf_op jit(solution)/shard_map/ppermute | solution.py:224
  0.5 70.2 %collective-permute-start.1 = (f32[256,16384]{1,0:T(8,128)}, f32[256,16384]{1,0:T(8,128)}, u32[]{:S(2)}, u32[]{:S(2)}) collective-permute-start(f32[256,16384]{1,0:T(8,128)} %s_ref.1), channel_id=1, source_target_pairs={{0,1},{1,0},{2,3},{3,2},{4,5},{5,4},{6,7},{7,6},{8,9},{9,8},{10,11... | collective-permute-start | bytes 50331656 | tf_op jit(solution)/shard_map/ppermute | solution.py:224
  28.6 12.4 %all-to-all-start.1 = ((f32[8,32,256]{2,1,0:T(8,128)}), f32[8,32,256]{2,1,0:T(8,128)S(1)}, u32[]{:S(2)}, u32[]{:S(2)}) async-start(f32[8,32,256]{2,1,0:T(8,128)} %sum_shards.2), calls=%async_computation.1 | async-start | bytes 524288 | tf_op jit(solution)/shard_map/all_to_all | solution.py:150
  41.0 16.2 %all-to-all-start.2 = ((f32[16,16,256]{2,1,0:T(8,128)}), f32[16,16,256]{2,1,0:T(8,128)S(1)}, u32[]{:S(2)}, u32[]{:S(2)}) async-start(f32[16,16,256]{2,1,0:T(8,128)} %bitcast.3), calls=%async_computation.2 | async-start | bytes 524288 | tf_op jit(solution)/shard_map/all_to_all | solution.py:142
  47.3 9.5 %collective-permute-start.2 = (f32[8,256]{1,0:T(8,128)S(1)}, f32[8,256]{1,0:T(8,128)S(1)}, u32[]{:S(2)}, u32[]{:S(2)}) collective-permute-start(f32[8,256]{1,0:T(8,128)S(1)} %summary.1.summary_ref), channel_id=1, source_target_pairs={{0,3},{1,2},{2,5},{3,4},{4,7},{5,6},{6,9},{7,8},{8,11},{9,10},{10,... | collective-permute-start | bytes 24584 | tf_op jit(solution)/shard_map/ppermute | solution.py:239

commit v9 on v8

--- a/solution.py
+++ b/solution.py
@@ -8,8 +8,9 @@
 from jax.experimental.pallas import tpu as pltpu
 from jax.sharding import PartitionSpec as P
 
-GRAM_TILE = 2048
-VELOCITY_TILE = 2048
+GRAM_TILE = 1024
+VELOCITY_TILE = 1024
+DEPTH = 4
 MIB = 1024 * 1024
 BOTH = ("dim", "blk")
 
@@ -39,6 +40,43 @@
     return total
 
 
+def fetch(sources, buffers, sems, first=0):
+    step, steps = pl.program_id(0), pl.num_programs(0)
+    depth, _, tile = buffers[0].shape
+
+    def copies(at):
+        columns = pl.ds(pl.multiple_of((first + at) * tile, tile), tile)
+        slot = lax.rem(at, depth)
+        return [
+            pltpu.make_async_copy(source.at[:, columns], buffer.at[slot], sems.at[n, slot])
+            for n, (source, buffer) in enumerate(zip(sources, buffers))
+        ]
+
+    def start(at):
+        @pl.when(at < steps)
+        def _():
+            for copy in copies(at):
+                copy.start()
+
+    @pl.when(step == 0)
+    def _():
+        for ahead in range(depth - 1):
+            start(ahead)
+
+    start(step + depth - 1)
+    for copy in copies(step):
+        copy.wait()
+    return [buffer[lax.rem(step, depth)] for buffer in buffers]
+
+
+def slots(count, rows, tile):
+    return [pltpu.VMEM((DEPTH, rows, tile), jnp.float32)] * count + [pltpu.SemaphoreType.DMA((count, DEPTH))]
+
+
+def in_hbm():
+    return pl.BlockSpec(memory_space=pl.ANY)
+
+
 def whole(array):
     return pl.BlockSpec(array.shape, lambda i: (0,) * len(array.shape))
 
@@ -51,13 +89,13 @@
     return lax.broadcasted_iota(jnp.int32, (rows, rows), 0) == lax.broadcasted_iota(jnp.int32, (rows, rows), 1)
 
 
-def own_kernel(x_ref, out_ref, gram_ref, squares_ref):
+def own_kernel(x_ref, out_ref, gram_ref, squares_ref, buffer, sems):
     @pl.when(pl.program_id(0) == 0)
     def _():
         gram_ref[...] = jnp.zeros_like(gram_ref)
         squares_ref[...] = jnp.zeros_like(squares_ref)
 
-    x = x_ref[...]
+    (x,) = fetch([x_ref], [buffer], sems)
     hi, lo = split(x)
     gram_ref[...] += nt_dot(jnp.concatenate([hi, lo], axis=0), hi)
     squares_ref[...] += lane_sums(x * x)
@@ -78,24 +116,29 @@
     return pl.pallas_call(
         own_kernel,
         grid=(columns // tile,),
-        in_specs=[pl.BlockSpec((rows, tile), lambda i: (0, i))],
+        in_specs=[in_hbm()],
         out_specs=whole(out),
         out_shape=out,
-        scratch_shapes=[pltpu.VMEM((2 * rows, rows), jnp.float32), pltpu.VMEM((rows, 128), jnp.float32)],
+        scratch_shapes=[
+            pltpu.VMEM((2 * rows, rows), jnp.float32),
+            pltpu.VMEM((rows, 128), jnp.float32),
+            *slots(1, rows, tile),
+        ],
         compiler_params=params(52),
         cost_estimate=pl.CostEstimate(flops=4 * rows * rows * columns, bytes_accessed=4 * rows * columns, transcendentals=0),
         name="own_gram",
     )(particles)
 
 
-def pair_kernel(core_ref, mine_ref, other_ref, out_ref, gram_ref):
+def pair_kernel(core_ref, mine_ref, other_ref, out_ref, gram_ref, my_buffer, buffer, sems):
     @pl.when(pl.program_id(0) == 0)
     def _():
         gram_ref[...] = jnp.zeros_like(gram_ref)
 
     rows = gram_ref.shape[0]
-    my_hi, my_lo = split(mine_ref[...])
-    hi, lo = split(other_ref[...])
+    mine, other = fetch([mine_ref, other_ref], [my_buffer, buffer], sems, core_ref[0] * pl.num_programs(0))
+    my_hi, my_lo = split(mine)
+    hi, lo = split(other)
     both = nt_dot(jnp.concatenate([my_hi, my_lo], axis=0), hi)
     gram_ref[...] += both[:rows] + both[rows:] + nt_dot(my_hi, lo)
 
@@ -111,15 +154,14 @@
     tile = min(GRAM_TILE, width)
     tiles = width // tile
     out = f32(rows, rows)
-    block = pl.BlockSpec((rows, tile), lambda i, core: (0, core[0] * tiles + i))
     return pl.pallas_call(
         pair_kernel,
         grid_spec=pltpu.PrefetchScalarGridSpec(
             num_scalar_prefetch=1,
             grid=(tiles,),
-            in_specs=[block, block],
+            in_specs=[in_hbm(), in_hbm()],
             out_specs=pl.BlockSpec(out.shape, lambda i, core: (0, 0)),
-            scratch_shapes=[pltpu.VMEM((rows, rows), jnp.float32)],
+            scratch_shapes=[pltpu.VMEM((rows, rows), jnp.float32), *slots(2, rows, tile)],
         ),
         out_shape=out,
         compiler_params=params(52),
@@ -193,12 +235,14 @@
     )(core, own, summary, other, gram)
 
 
-def velocity_kernel(x_ref, s_ref, other_x, other_s, hi_ref, lo_ref, weight_ref, half_ref, out_ref):
+def velocity_kernel(
+    x_ref, s_ref, other_x_ref, other_s_ref, hi_ref, lo_ref, weight_ref, half_ref, out_ref, *scratch
+):
     rows = out_ref.shape[0]
     half = half_ref[0:1, 0:1]
-    x = x_ref[...]
-    driven = half * s_ref[...]
-    moved_hi, moved_lo = split(jnp.concatenate([driven - x, half * other_s[...] - other_x[...]], axis=0))
+    x, s, other_x, other_s = fetch([x_ref, s_ref, other_x_ref, other_s_ref], scratch[:4], scratch[4])
+    driven = half * s
+    moved_hi, moved_lo = split(jnp.concatenate([driven - x, half * other_s - other_x], axis=0))
     hi = hi_ref[...]
     both = nn_dot(jnp.concatenate([hi, lo_ref[...]], axis=0), moved_hi)
     out_ref[...] = driven + weight_ref[:, 0:1] * x + both[:rows] + both[rows:] + nn_dot(hi, moved_lo)
@@ -211,9 +255,10 @@
     return pl.pallas_call(
         velocity_kernel,
         grid=(columns // tile,),
-        in_specs=[block] * 4 + [whole(w) for w in weights],
+        in_specs=[in_hbm()] * 4 + [whole(w) for w in weights],
         out_specs=block,
         out_shape=f32(rows, columns),
+        scratch_shapes=slots(4, rows, tile),
         compiler_params=params(52),
         cost_estimate=pl.CostEstimate(flops=12 * rows * rows * columns, bytes_accessed=20 * rows * columns, transcendentals=0),
         name="velocity",

time: 102 us -> 96.4 us (0.945)
  Pallas kernels: 52.4 us -> 46.9 us
    pallas_call x2, Pallas kernels: 42 us -> 37.5 us  [the longest x1 28 us: velocity_part(): pl.pallas_call(velocity_kernel, grid=(columns // tile,), in_specs=[in_hbm...]
    pallas_call x1, Pallas kernels: 8.79 us -> 7.73 us  [pair_part(): pl.pallas_call(pair_kernel, grid_spec=pltpu.PrefetchScalarGridSpec(num_sc...]
  transfers between devices with their start and end apart: 5 -> 5, of which waited for: 2 -> 3; matrix products, arithmetic and copies ran while one was open for 0% -> 0% of each run, Pallas kernels for 21% -> 20%
where the time goes in v9:
time: 96.4 us; the launch traced here: 96 us
  Pallas kernels  46.9 us (49%)
  blocking collectives  28.9 us (30%)
  starting transfers between devices  11.1 us (12%)
  waiting for transfers between devices  9.01 us (9%)
    pallas_call x1, Pallas kernels, velocity_part(): pl.pallas_call(velocity_kernel, grid=(columns // tile,), in_specs=[in_hbm...  28 us
    all_to_all x1, blocking collectives, summed_shards(): lax.all_to_all(block.reshape(count, rows // count, columns), axes, 0, 0)  16.2 us
    all_to_all x1, blocking collectives, gathered(): return lax.all_to_all(copies, axes, 0, 0).reshape(count * rows, columns)  12.7 us
    pallas_call x1, Pallas kernels, own_part(): pl.pallas_call(own_kernel, grid=(columns // tile,), in_specs=[in_hbm()],...  9.52 us
    ppermute x1, waiting for transfers between devices, body(): other = lax.ppermute(summary, BOTH, across)  7.8 us
    pallas_call x1, Pallas kernels, pair_part(): pl.pallas_call(pair_kernel, grid_spec=pltpu.PrefetchScalarGridSpec(num_sc...  7.73 us
    all_to_all x1, starting transfers between devices, summed_shards(): lax.all_to_all(block.reshape(count, rows // count, columns), axes, 0, 0)  5.29 us
    all_to_all x1, starting transfers between devices, gathered(): return lax.all_to_all(copies, axes, 0, 0).reshape(count * rows, columns)  3.59 us
  transfers between devices with their start and end apart: 5, of which 3 were waited for; matrix products, arithmetic and copies ran while one was open for 0% of the time, Pallas kernels for 20%

profile of v9, /device:TPU:0, one launch (start us, length us, event | category | flops | bytes accessed | tf_op | source)
XLA Modules:
  0.0 96.0 jit_solution(7126319835995207812)
XLA Ops:
  0.0 0.5 collective-permute-start
  0.5 0.1 collective-permute-start.1
  0.5 9.5 %own_gram.1 = f32[256,256]{1,0:T(8,128)S(1)} custom-call(f32[256,16384]{1,0:T(8,128)} %x_ref.3), custom_call_target="tpu_custom_call" | custom-call | flops 4294967296 | bytes 16777216 | tf_op jit(solution)/shard_map/own_gram/pallas_call | solution.py:116
  10.0 16.2 %all_to_all.20.arrived_ref = f32[8,32,256]{2,1,0:T(8,128)S(1)} all-to-all(f32[8,32,256]{2,1,0:T(8,128)S(1)} %bitcast.7), channel_id=1, replica_groups=mesh['grp'=2,'dim'=8,'blk'=2] {'dim'}, dimensions={0} | all-to-all | bytes 524288 | tf_op jit(solution)/shard_map/all_to_all | solution.py:184
  26.3 0.7 sum_shards.2
  27.0 3.6 %all-to-all-start.1 = ((f32[8,32,256]{2,1,0:T(8,128)}), f32[8,32,256]{2,1,0:T(8,128)S(1)}, u32[]{:S(2)}, u32[]{:S(2)}) async-start(f32[8,32,256]{2,1,0:T(8,128)} %sum_shards.2), calls=%async_computation.1 | async-start | bytes 524288 | tf_op jit(solution)/shard_map/all_to_all | solution.py:192
  30.6 0.0 collective-permute-done.other_ref.other_x_ref
  30.6 7.7 %pair_gram.1 = f32[256,256]{1,0:T(8,128)} custom-call(s32[1]{0:T(128)} %bitcast.core_ref, f32[256,16384]{1,0:T(8,128)} %x_ref.3, f32[256,16384]{1,0:T(8,128)} %collective-permute-done.other_ref.other_x_ref), custom_call_target="tpu_custom_call" | custom-call | flops 3221225472 | bytes 16777216 | tf_op jit(solution)/shard_map/pair_gram/pallas_call | solution.py:157
  38.3 0.8 all-to-all-done.1
  39.1 5.3 %all-to-all-start.2 = ((f32[16,16,256]{2,1,0:T(8,128)}), f32[16,16,256]{2,1,0:T(8,128)S(1)}, u32[]{:S(2)}, u32[]{:S(2)}) async-start(f32[16,16,256]{2,1,0:T(8,128)} %bitcast.3), calls=%async_computation.2 | async-start | bytes 524288 | tf_op jit(solution)/shard_map/all_to_all | solution.py:184
  44.4 0.2 summary.1.summary_ref
  44.7 1.7 %collective-permute-start.2 = (f32[8,256]{1,0:T(8,128)S(1)}, f32[8,256]{1,0:T(8,128)S(1)}, u32[]{:S(2)}, u32[]{:S(2)}) collective-permute-start(f32[8,256]{1,0:T(8,128)S(1)} %summary.1.summary_ref), channel_id=1, source_target_pairs={{0,3},{1,2},{2,5},{3,4},{4,7},{5,6},{6,9},{7,8},{8,11},{9,10},{10,... | collective-permute-start | bytes 24584 | tf_op jit(solution)/shard_map/ppermute | solution.py:284
  46.4 7.8 %collective-permute-done.2.other_ref = f32[8,256]{1,0:T(8,128)S(1)} collective-permute-done((f32[8,256]{1,0:T(8,128)S(1)}, f32[8,256]{1,0:T(8,128)S(1)}, u32[]{:S(2)}, u32[]{:S(2)}) %collective-permute-start.2) | collective-permute-done | bytes 8224 | tf_op jit(solution)/shard_map/ppermute | solution.py:284
  54.2 0.4 all-to-all-done.2.arrived_ref
  54.6 12.7 %all_to_all.21 = f32[16,16,256]{2,1,0:T(8,128)S(1)} all-to-all(f32[16,16,256]{2,1,0:T(8,128)S(1)} %sum_shards.3), channel_id=1, replica_groups=mesh['grp'=2,'dim'=8,'blk'=2] {'dim','blk'}, dimensions={0} | all-to-all | bytes 524288 | tf_op jit(solution)/shard_map/all_to_all | solution.py:192
  67.3 0.6 kernel_weights.1
  68.0 0.0 collective-permute-done.1.other_s_ref
  68.0 28.0 %velocity.1 = f32[256,16384]{1,0:T(8,128)} custom-call(f32[256,16384]{1,0:T(8,128)} %x_ref.3, f32[256,16384]{1,0:T(8,128)} %s_ref.1, f32[256,16384]{1,0:T(8,128)} %collective-permute-done.other_ref.other_x_ref, f32[256,16384]{1,0:T(8,128)} %collective-permute-done.1.other_s_ref, bf16[256,512]{1,0:T(8,128)(2,1)S(1)} %get-tuple-element.11.hi_ref, ...), custom_call_target="tpu_custom_call" | custom-call | flops 12884901888 | bytes 83886080 | tf_op jit(solution)/shard_map/velocity/pallas_call | solution.py:255
  (1 shorter events, 0.0 us)
Async XLA Ops:
  0.0 30.6 %collective-permute-start = (f32[256,16384]{1,0:T(8,128)}, f32[256,16384]{1,0:T(8,128)}, u32[]{:S(2)}, u32[]{:S(2)}) collective-permute-start(f32[256,16384]{1,0:T(8,128)} %x_ref.3), channel_id=1, source_target_pairs={{0,1},{1,0},{2,3},{3,2},{4,5},{5,4},{6,7},{7,6},{8,9},{9,8},{10,11... | collective-permute-start | bytes 50331656 | tf_op jit(solution)/shard_map/ppermute | solution.py:269
  0.5 67.5 %collective-permute-start.1 = (f32[256,16384]{1,0:T(8,128)}, f32[256,16384]{1,0:T(8,128)}, u32[]{:S(2)}, u32[]{:S(2)}) collective-permute-start(f32[256,16384]{1,0:T(8,128)} %s_ref.1), channel_id=1, source_target_pairs={{0,1},{1,0},{2,3},{3,2},{4,5},{5,4},{6,7},{7,6},{8,9},{9,8},{10,11... | collective-permute-start | bytes 50331656 | tf_op jit(solution)/shard_map/ppermute | solution.py:269
  27.0 12.2 %all-to-all-start.1 = ((f32[8,32,256]{2,1,0:T(8,128)}), f32[8,32,256]{2,1,0:T(8,128)S(1)}, u32[]{:S(2)}, u32[]{:S(2)}) async-start(f32[8,32,256]{2,1,0:T(8,128)} %sum_shards.2), calls=%async_computation.1 | async-start | bytes 524288 | tf_op jit(solution)/shard_map/all_to_all | solution.py:192
  39.1 15.4 %all-to-all-start.2 = ((f32[16,16,256]{2,1,0:T(8,128)}), f32[16,16,256]{2,1,0:T(8,128)S(1)}, u32[]{:S(2)}, u32[]{:S(2)}) async-start(f32[16,16,256]{2,1,0:T(8,128)} %bitcast.3), calls=%async_computation.2 | async-start | bytes 524288 | tf_op jit(solution)/shard_map/all_to_all | solution.py:184
  44.7 9.5 %collective-permute-start.2 = (f32[8,256]{1,0:T(8,128)S(1)}, f32[8,256]{1,0:T(8,128)S(1)}, u32[]{:S(2)}, u32[]{:S(2)}) collective-permute-start(f32[8,256]{1,0:T(8,128)S(1)} %summary.1.summary_ref), channel_id=1, source_target_pairs={{0,3},{1,2},{2,5},{3,4},{4,7},{5,6},{6,9},{7,8},{8,11},{9,10},{10,... | collective-permute-start | bytes 24584 | tf_op jit(solution)/shard_map/ppermute | solution.py:284

commit v10 on v9

--- a/solution.py
+++ b/solution.py
@@ -40,7 +40,7 @@
     return total
 
 
-def fetch(sources, buffers, sems, first=0):
+def fetch(sources, buffers, sems, first=0, meanwhile=None):
     step, steps = pl.program_id(0), pl.num_programs(0)
     depth, _, tile = buffers[0].shape
 
@@ -62,6 +62,8 @@
     def _():
         for ahead in range(depth - 1):
             start(ahead)
+        if meanwhile is not None:
+            meanwhile()
 
     start(step + depth - 1)
     for copy in copies(step):
@@ -205,64 +207,68 @@
     return pl.pallas_call(summary_kernel, out_shape=f32(8, own.shape[0]), compiler_params=params(8), name="summary")(own)
 
 
-def weights_kernel(scale_base, core_ref, own_ref, summary_ref, other_ref, gram_ref, hi_ref, lo_ref, weight_ref, half_ref):
+def form_weights(scale_base, core, own_ref, summary_ref, other_ref, gram_ref, weights_ref, weight_ref, half_ref):
     own = own_ref[...]
     rows = own.shape[0]
     diagonal = on_diagonal(rows)
     norms = jnp.sum(jnp.where(diagonal, own, 0.0), axis=1, keepdims=True)
     gram = gram_ref[...]
-    pair = norms + other_ref[0:1, :] - 2.0 * jnp.where(core_ref[0] == 0, gram, gram.T)
+    pair = norms + other_ref[0:1, :] - 2.0 * jnp.where(core == 0, gram, gram.T)
     spread = summary_ref[1:2, 0:1] + other_ref[1:2, 0:1] + 2.0 * jnp.sum(pair)
     width = spread / scale_base
     inverse = -1.0 / width
     own_weights = jnp.where(diagonal, 0.0, jnp.exp(own * inverse))
     pair_weights = jnp.exp(pair * inverse)
     weights = jnp.concatenate([own_weights, pair_weights], axis=1)
-    hi_ref[...], lo_ref[...] = split(weights)
+    weights_ref[:rows, :], weights_ref[rows:, :] = split(weights)
     weight_ref[...] = jnp.broadcast_to(jnp.sum(weights, axis=1, keepdims=True), weight_ref.shape)
     half_ref[...] = jnp.broadcast_to(0.5 * width, half_ref.shape)
 
 
-def weights_part(core, own, summary, other, gram, scale_base):
-    rows = own.shape[0]
-    half = jax.ShapeDtypeStruct((rows, 2 * rows), jnp.bfloat16)
-    return pl.pallas_call(
-        functools.partial(weights_kernel, scale_base),
-        in_specs=[pl.BlockSpec(memory_space=pltpu.SMEM)] + [pl.BlockSpec(memory_space=pltpu.VMEM)] * 4,
-        out_shape=[half, half, f32(rows, 128), f32(8, 128)],
-        compiler_params=params(12),
-        name="kernel_weights",
-    )(core, own, summary, other, gram)
-
-
 def velocity_kernel(
-    x_ref, s_ref, other_x_ref, other_s_ref, hi_ref, lo_ref, weight_ref, half_ref, out_ref, *scratch
+    scale_base, core_ref, x_ref, s_ref, other_x_ref, other_s_ref, own_ref, summary_ref, other_ref, gram_ref, out_ref, *scratch
 ):
     rows = out_ref.shape[0]
+    weights_ref, weight_ref, half_ref = scratch[5:]
+
+    def meanwhile():
+        form_weights(
+            scale_base, core_ref[0], own_ref, summary_ref, other_ref, gram_ref, weights_ref, weight_ref, half_ref
+        )
+
+    x, s, other_x, other_s = fetch(
+        [x_ref, s_ref, other_x_ref, other_s_ref], scratch[:4], scratch[4], meanwhile=meanwhile
+    )
     half = half_ref[0:1, 0:1]
-    x, s, other_x, other_s = fetch([x_ref, s_ref, other_x_ref, other_s_ref], scratch[:4], scratch[4])
     driven = half * s
     moved_hi, moved_lo = split(jnp.concatenate([driven - x, half * other_s - other_x], axis=0))
-    hi = hi_ref[...]
-    both = nn_dot(jnp.concatenate([hi, lo_ref[...]], axis=0), moved_hi)
-    out_ref[...] = driven + weight_ref[:, 0:1] * x + both[:rows] + both[rows:] + nn_dot(hi, moved_lo)
-
-
-def velocity_part(particles, scores, visitor, visitor_scores, weights):
+    both = nn_dot(weights_ref[...], moved_hi)
+    out_ref[...] = driven + weight_ref[:, 0:1] * x + both[:rows] + both[rows:] + nn_dot(weights_ref[:rows, :], moved_lo)
+
+
+def velocity_part(core, particles, scores, visitor, visitor_scores, own, summary, other, gram, scale_base):
     rows, columns = particles.shape
     tile = min(VELOCITY_TILE, columns)
-    block = pl.BlockSpec((rows, tile), lambda i: (0, i))
+    small = [own, summary, other, gram]
     return pl.pallas_call(
-        velocity_kernel,
-        grid=(columns // tile,),
-        in_specs=[in_hbm()] * 4 + [whole(w) for w in weights],
-        out_specs=block,
+        functools.partial(velocity_kernel, scale_base),
+        grid_spec=pltpu.PrefetchScalarGridSpec(
+            num_scalar_prefetch=1,
+            grid=(columns // tile,),
+            in_specs=[in_hbm()] * 4 + [pl.BlockSpec(a.shape, lambda i, core: (0, 0)) for a in small],
+            out_specs=pl.BlockSpec((rows, tile), lambda i, core: (0, i)),
+            scratch_shapes=[
+                *slots(4, rows, tile),
+                pltpu.VMEM((2 * rows, 2 * rows), jnp.bfloat16),
+                pltpu.VMEM((rows, 128), jnp.float32),
+                pltpu.VMEM((8, 128), jnp.float32),
+            ],
+        ),
         out_shape=f32(rows, columns),
-        scratch_shapes=slots(4, rows, tile),
         compiler_params=params(52),
         cost_estimate=pl.CostEstimate(flops=12 * rows * rows * columns, bytes_accessed=20 * rows * columns, transcendentals=0),
         name="velocity",
-    )(particles, scores, visitor, visitor_scores, *weights)
+    )(core, particles, scores, visitor, visitor_scores, *small)
 
 
 def swap(array):
@@ -285,8 +291,7 @@
 
     gram = summed_shards(pair_part(core, particles, visitor), BOTH, other)
     gram = gathered(gram, BOTH)
-    weights = weights_part(core, own, summary, other, gram, scale_base)
-    return velocity_part(particles, scores, visitor, visitor_scores, weights)
+    return velocity_part(core, particles, scores, visitor, visitor_scores, own, summary, other, gram, scale_base)
 
 
 def solution(mesh):

time: 96.4 us -> 97.6 us (1.012)
  blocking collectives: 28.9 us -> 16.2 us
  waiting for transfers between devices: 9.01 us -> 19 us
  starting transfers between devices: 11.1 us -> 14.7 us
    all_to_all x1 -> x0, blocking collectives: 12.7 us -> none  [gathered(): return lax.all_to_all(copies, axes, 0, 0).reshape(count * rows, columns)]
    all_to_all x1 -> x2, waiting for transfers between devices: 0.82 us -> 10.8 us  [gathered(): return lax.all_to_all(copies, axes, 0, 0).reshape(count * rows, columns)]
    all_to_all x1 -> x2, starting transfers between devices: 3.59 us -> 7.12 us  [gathered(): return lax.all_to_all(copies, axes, 0, 0).reshape(count * rows, columns)]
    pallas_call x2 -> x1, Pallas kernels: 28.6 us -> 28.3 us  [velocity_part(): pl.pallas_call(functools.partial(velocity_kernel, scale_base), grid_spec=...]
  transfers between devices with their start and end apart: 5 -> 6, of which waited for: 3 -> 4; matrix products, arithmetic and copies ran while one was open for 0% -> 0% of each run, Pallas kernels for 20% -> 19%
where the time goes in v10:
time: 97.6 us; the launch traced here: 97.2 us
  Pallas kernels  47.3 us (48%)
  waiting for transfers between devices  19 us (19%)
  blocking collectives  16.2 us (17%)
  starting transfers between devices  14.7 us (15%)
    pallas_call x1, Pallas kernels, velocity_part(): pl.pallas_call(functools.partial(velocity_kernel, scale_base), grid_spec=...  28.3 us
    all_to_all x1, blocking collectives, summed_shards(): lax.all_to_all(block.reshape(count, rows // count, columns), axes, 0, 0)  16.2 us
    all_to_all x2, waiting for transfers between devices, gathered(): return lax.all_to_all(copies, axes, 0, 0).reshape(count * rows, columns)  10.8 us
    pallas_call x1, Pallas kernels, own_part(): pl.pallas_call(own_kernel, grid=(columns // tile,), in_specs=[in_hbm()],...  9.52 us
    ppermute x1, waiting for transfers between devices, body(): other = lax.ppermute(summary, BOTH, across)  7.8 us
    pallas_call x1, Pallas kernels, pair_part(): pl.pallas_call(pair_kernel, grid_spec=pltpu.PrefetchScalarGridSpec(num_sc...  7.73 us
    all_to_all x2, starting transfers between devices, gathered(): return lax.all_to_all(copies, axes, 0, 0).reshape(count * rows, columns)  7.12 us
    all_to_all x1, starting transfers between devices, summed_shards(): lax.all_to_all(block.reshape(count, rows // count, columns), axes, 0, 0)  5.29 us
  transfers between devices with their start and end apart: 6, of which 4 were waited for; matrix products, arithmetic and copies ran while one was open for 0% of the time, Pallas kernels for 19%

profile of v10, /device:TPU:0, one launch (start us, length us, event | category | flops | bytes accessed | tf_op | source)
XLA Modules:
  0.0 97.2 jit_solution(1913183079267560240)
XLA Ops:
  0.0 0.5 collective-permute-start
  0.5 0.1 collective-permute-start.1
  0.5 9.5 %own_gram.1 = f32[256,256]{1,0:T(8,128)S(1)} custom-call(f32[256,16384]{1,0:T(8,128)} %x_ref.3), custom_call_target="tpu_custom_call" | custom-call | flops 4294967296 | bytes 16777216 | tf_op jit(solution)/shard_map/own_gram/pallas_call | solution.py:118
  10.0 16.2 %all_to_all.20.arrived_ref = f32[8,32,256]{2,1,0:T(8,128)S(1)} all-to-all(f32[8,32,256]{2,1,0:T(8,128)S(1)} %bitcast.7), channel_id=1, replica_groups=mesh['grp'=2,'dim'=8,'blk'=2] {'dim'}, dimensions={0} | all-to-all | bytes 524288 | tf_op jit(solution)/shard_map/all_to_all | solution.py:186
  26.3 0.7 sum_shards.2
  27.0 3.6 %all-to-all-start.1 = ((f32[8,32,256]{2,1,0:T(8,128)}), f32[8,32,256]{2,1,0:T(8,128)S(1)}, u32[]{:S(2)}, u32[]{:S(2)}) async-start(f32[8,32,256]{2,1,0:T(8,128)} %sum_shards.2), calls=%async_computation.1 | async-start | bytes 524288 | tf_op jit(solution)/shard_map/all_to_all | solution.py:194
  30.6 0.0 collective-permute-done.other_ref.other_x_ref
  30.6 7.7 %pair_gram.1 = f32[256,256]{1,0:T(8,128)} custom-call(s32[1]{0:T(128)} %bitcast.core_ref, f32[256,16384]{1,0:T(8,128)} %x_ref.3, f32[256,16384]{1,0:T(8,128)} %collective-permute-done.other_ref.other_x_ref), custom_call_target="tpu_custom_call" | custom-call | flops 3221225472 | bytes 16777216 | tf_op jit(solution)/shard_map/pair_gram/pallas_call | solution.py:159
  38.3 0.8 all-to-all-done.1
  39.1 5.3 %all-to-all-start.2 = ((f32[16,16,256]{2,1,0:T(8,128)}), f32[16,16,256]{2,1,0:T(8,128)S(1)}, u32[]{:S(2)}, u32[]{:S(2)}) async-start(f32[16,16,256]{2,1,0:T(8,128)} %bitcast.3), calls=%async_computation.2 | async-start | bytes 524288 | tf_op jit(solution)/shard_map/all_to_all | solution.py:186
  44.4 0.2 summary.1.summary_ref
  44.7 1.7 %collective-permute-start.2 = (f32[8,256]{1,0:T(8,128)S(1)}, f32[8,256]{1,0:T(8,128)S(1)}, u32[]{:S(2)}, u32[]{:S(2)}) collective-permute-start(f32[8,256]{1,0:T(8,128)S(1)} %summary.1.summary_ref), channel_id=1, source_target_pairs={{0,3},{1,2},{2,5},{3,4},{4,7},{5,6},{6,9},{7,8},{8,11},{9,10},{10,... | collective-permute-start | bytes 24584 | tf_op jit(solution)/shard_map/ppermute | solution.py:290
  46.4 7.8 %collective-permute-done.2.other_ref = f32[8,256]{1,0:T(8,128)S(1)} collective-permute-done((f32[8,256]{1,0:T(8,128)S(1)}, f32[8,256]{1,0:T(8,128)S(1)}, u32[]{:S(2)}, u32[]{:S(2)}) %collective-permute-start.2) | collective-permute-done | bytes 8224 | tf_op jit(solution)/shard_map/ppermute | solution.py:290
  54.2 0.4 all-to-all-done.2.arrived_ref
  54.6 0.7 sum_shards.3
  55.3 3.5 %all-to-all-start.3 = ((f32[16,16,256]{2,1,0:T(8,128)}), f32[16,16,256]{2,1,0:T(8,128)S(1)}, u32[]{:S(2)}, u32[]{:S(2)}) async-start(f32[16,16,256]{2,1,0:T(8,128)} %sum_shards.3), calls=%async_computation.3 | async-start | bytes 524288 | tf_op jit(solution)/shard_map/all_to_all | solution.py:194
  58.9 0.0 collective-permute-done.1.other_s_ref
  58.9 10.0 %all-to-all-done.3 = f32[16,16,256]{2,1,0:T(8,128)S(1)} async-done(((f32[16,16,256]{2,1,0:T(8,128)}), f32[16,16,256]{2,1,0:T(8,128)S(1)}, u32[]{:S(2)}, u32[]{:S(2)}) %all-to-all-start.3) | async-done | bytes 262176 | tf_op jit(solution)/shard_map/all_to_all | solution.py:194
  68.9 28.3 %velocity.1 = f32[256,16384]{1,0:T(8,128)} custom-call(s32[1]{0:T(128)} %bitcast.core_ref, f32[256,16384]{1,0:T(8,128)} %x_ref.3, f32[256,16384]{1,0:T(8,128)} %s_ref.1, f32[256,16384]{1,0:T(8,128)} %collective-permute-done.other_ref.other_x_ref, f32[256,16384]{1,0:T(8,128)} %collective-permute-done.1.other_s_ref, f32[256,256]{1,0:T(8,128)S(1)} %bitcast.6, ...), custom_call_target="tpu_custom_call" | custom-call | flops 12884901888 | bytes 83886080 | tf_op jit(solution)/shard_map/velocity/pallas_call | solution.py:253
Async XLA Ops:
  0.0 30.6 %collective-permute-start = (f32[256,16384]{1,0:T(8,128)}, f32[256,16384]{1,0:T(8,128)}, u32[]{:S(2)}, u32[]{:S(2)}) collective-permute-start(f32[256,16384]{1,0:T(8,128)} %x_ref.3), channel_id=1, source_target_pairs={{0,1},{1,0},{2,3},{3,2},{4,5},{5,4},{6,7},{7,6},{8,9},{9,8},{10,11... | collective-permute-start | bytes 50331656 | tf_op jit(solution)/shard_map/ppermute | solution.py:275
  0.5 58.4 %collective-permute-start.1 = (f32[256,16384]{1,0:T(8,128)}, f32[256,16384]{1,0:T(8,128)}, u32[]{:S(2)}, u32[]{:S(2)}) collective-permute-start(f32[256,16384]{1,0:T(8,128)} %s_ref.1), channel_id=1, source_target_pairs={{0,1},{1,0},{2,3},{3,2},{4,5},{5,4},{6,7},{7,6},{8,9},{9,8},{10,11... | collective-permute-start | bytes 50331656 | tf_op jit(solution)/shard_map/ppermute | solution.py:275
  27.0 12.2 %all-to-all-start.1 = ((f32[8,32,256]{2,1,0:T(8,128)}), f32[8,32,256]{2,1,0:T(8,128)S(1)}, u32[]{:S(2)}, u32[]{:S(2)}) async-start(f32[8,32,256]{2,1,0:T(8,128)} %sum_shards.2), calls=%async_computation.1 | async-start | bytes 524288 | tf_op jit(solution)/shard_map/all_to_all | solution.py:194
  39.1 15.4 %all-to-all-start.2 = ((f32[16,16,256]{2,1,0:T(8,128)}), f32[16,16,256]{2,1,0:T(8,128)S(1)}, u32[]{:S(2)}, u32[]{:S(2)}) async-start(f32[16,16,256]{2,1,0:T(8,128)} %bitcast.3), calls=%async_computation.2 | async-start | bytes 524288 | tf_op jit(solution)/shard_map/all_to_all | solution.py:186
  44.7 9.5 %collective-permute-start.2 = (f32[8,256]{1,0:T(8,128)S(1)}, f32[8,256]{1,0:T(8,128)S(1)}, u32[]{:S(2)}, u32[]{:S(2)}) collective-permute-start(f32[8,256]{1,0:T(8,128)S(1)} %summary.1.summary_ref), channel_id=1, source_target_pairs={{0,3},{1,2},{2,5},{3,4},{4,7},{5,6},{6,9},{7,8},{8,11},{9,10},{10,... | collective-permute-start | bytes 24584 | tf_op jit(solution)/shard_map/ppermute | solution.py:290
  55.3 13.5 %all-to-all-start.3 = ((f32[16,16,256]{2,1,0:T(8,128)}), f32[16,16,256]{2,1,0:T(8,128)S(1)}, u32[]{:S(2)}, u32[]{:S(2)}) async-start(f32[16,16,256]{2,1,0:T(8,128)} %sum_shards.3), calls=%async_computation.3 | async-start | bytes 524288 | tf_op jit(solution)/shard_map/all_to_all | solution.py:194

commit v11 on v9

--- a/solution.py
+++ b/solution.py
@@ -9,8 +9,9 @@
 from jax.sharding import PartitionSpec as P
 
 GRAM_TILE = 1024
-VELOCITY_TILE = 1024
-DEPTH = 4
+VELOCITY_TILE = 2048
+GRAM_DEPTH = 4
+VELOCITY_DEPTH = 3
 MIB = 1024 * 1024
 BOTH = ("dim", "blk")
 
@@ -69,8 +70,8 @@
     return [buffer[lax.rem(step, depth)] for buffer in buffers]
 
 
-def slots(count, rows, tile):
-    return [pltpu.VMEM((DEPTH, rows, tile), jnp.float32)] * count + [pltpu.SemaphoreType.DMA((count, DEPTH))]
+def slots(depth, count, rows, tile):
+    return [pltpu.VMEM((depth, rows, tile), jnp.float32)] * count + [pltpu.SemaphoreType.DMA((count, depth))]
 
 
 def in_hbm():
@@ -122,7 +123,7 @@
         scratch_shapes=[
             pltpu.VMEM((2 * rows, rows), jnp.float32),
             pltpu.VMEM((rows, 128), jnp.float32),
-            *slots(1, rows, tile),
+            *slots(GRAM_DEPTH, 1, rows, tile),
         ],
         compiler_params=params(52),
         cost_estimate=pl.CostEstimate(flops=4 * rows * rows * columns, bytes_accessed=4 * rows * columns, transcendentals=0),
@@ -161,7 +162,7 @@
             grid=(tiles,),
             in_specs=[in_hbm(), in_hbm()],
             out_specs=pl.BlockSpec(out.shape, lambda i, core: (0, 0)),
-            scratch_shapes=[pltpu.VMEM((rows, rows), jnp.float32), *slots(2, rows, tile)],
+            scratch_shapes=[pltpu.VMEM((rows, rows), jnp.float32), *slots(GRAM_DEPTH, 2, rows, tile)],
         ),
         out_shape=out,
         compiler_params=params(52),
@@ -258,7 +259,7 @@
         in_specs=[in_hbm()] * 4 + [whole(w) for w in weights],
         out_specs=block,
         out_shape=f32(rows, columns),
-        scratch_shapes=slots(4, rows, tile),
+        scratch_shapes=slots(VELOCITY_DEPTH, 4, rows, tile),
         compiler_params=params(52),
         cost_estimate=pl.CostEstimate(flops=12 * rows * rows * columns, bytes_accessed=20 * rows * columns, transcendentals=0),
         name="velocity",

time: 96.4 us -> 96.9 us (level)
  no operation moved by 1% of the time
where the time goes in v11:
time: 96.9 us; the launch traced here: 96.5 us
  Pallas kernels  47.4 us (49%)
  blocking collectives  28.9 us (30%)
  starting transfers between devices  11.1 us (11%)
  waiting for transfers between devices  9.01 us (9%)
    pallas_call x1, Pallas kernels, velocity_part(): pl.pallas_call(velocity_kernel, grid=(columns // tile,), in_specs=[in_hbm...  28.5 us
    all_to_all x1, blocking collectives, summed_shards(): lax.all_to_all(block.reshape(count, rows // count, columns), axes, 0, 0)  16.2 us
    all_to_all x1, blocking collectives, gathered(): return lax.all_to_all(copies, axes, 0, 0).reshape(count * rows, columns)  12.7 us
    pallas_call x1, Pallas kernels, own_part(): pl.pallas_call(own_kernel, grid=(columns // tile,), in_specs=[in_hbm()],...  9.52 us
    ppermute x1, waiting for transfers between devices, body(): other = lax.ppermute(summary, BOTH, across)  7.8 us
    pallas_call x1, Pallas kernels, pair_part(): pl.pallas_call(pair_kernel, grid_spec=pltpu.PrefetchScalarGridSpec(num_sc...  7.73 us
    all_to_all x1, starting transfers between devices, summed_shards(): lax.all_to_all(block.reshape(count, rows // count, columns), axes, 0, 0)  5.29 us
    all_to_all x1, starting transfers between devices, gathered(): return lax.all_to_all(copies, axes, 0, 0).reshape(count * rows, columns)  3.59 us
  transfers between devices with their start and end apart: 5, of which 3 were waited for; matrix products, arithmetic and copies ran while one was open for 0% of the time, Pallas kernels for 20%

profile of v11, /device:TPU:0, one launch (start us, length us, event | category | flops | bytes accessed | tf_op | source)
XLA Modules:
  0.0 96.5 jit_solution(13211806335955758403)
XLA Ops:
  0.0 0.5 collective-permute-start
  0.5 0.1 collective-permute-start.1
  0.5 9.5 %own_gram.1 = f32[256,256]{1,0:T(8,128)S(1)} custom-call(f32[256,16384]{1,0:T(8,128)} %x_ref.3), custom_call_target="tpu_custom_call" | custom-call | flops 4294967296 | bytes 16777216 | tf_op jit(solution)/shard_map/own_gram/pallas_call | solution.py:117
  10.0 16.2 %all_to_all.20.arrived_ref = f32[8,32,256]{2,1,0:T(8,128)S(1)} all-to-all(f32[8,32,256]{2,1,0:T(8,128)S(1)} %bitcast.7), channel_id=1, replica_groups=mesh['grp'=2,'dim'=8,'blk'=2] {'dim'}, dimensions={0} | all-to-all | bytes 524288 | tf_op jit(solution)/shard_map/all_to_all | solution.py:185
  26.3 0.7 sum_shards.2
  27.0 3.6 %all-to-all-start.1 = ((f32[8,32,256]{2,1,0:T(8,128)}), f32[8,32,256]{2,1,0:T(8,128)S(1)}, u32[]{:S(2)}, u32[]{:S(2)}) async-start(f32[8,32,256]{2,1,0:T(8,128)} %sum_shards.2), calls=%async_computation.1 | async-start | bytes 524288 | tf_op jit(solution)/shard_map/all_to_all | solution.py:193
  30.6 0.0 collective-permute-done.other_ref.other_x_ref
  30.6 7.7 %pair_gram.1 = f32[256,256]{1,0:T(8,128)} custom-call(s32[1]{0:T(128)} %bitcast.core_ref, f32[256,16384]{1,0:T(8,128)} %x_ref.3, f32[256,16384]{1,0:T(8,128)} %collective-permute-done.other_ref.other_x_ref), custom_call_target="tpu_custom_call" | custom-call | flops 3221225472 | bytes 16777216 | tf_op jit(solution)/shard_map/pair_gram/pallas_call | solution.py:158
  38.3 0.8 all-to-all-done.1
  39.1 5.3 %all-to-all-start.2 = ((f32[16,16,256]{2,1,0:T(8,128)}), f32[16,16,256]{2,1,0:T(8,128)S(1)}, u32[]{:S(2)}, u32[]{:S(2)}) async-start(f32[16,16,256]{2,1,0:T(8,128)} %bitcast.3), calls=%async_computation.2 | async-start | bytes 524288 | tf_op jit(solution)/shard_map/all_to_all | solution.py:185
  44.4 0.2 summary.1.summary_ref
  44.7 1.7 %collective-permute-start.2 = (f32[8,256]{1,0:T(8,128)S(1)}, f32[8,256]{1,0:T(8,128)S(1)}, u32[]{:S(2)}, u32[]{:S(2)}) collective-permute-start(f32[8,256]{1,0:T(8,128)S(1)} %summary.1.summary_ref), channel_id=1, source_target_pairs={{0,3},{1,2},{2,5},{3,4},{4,7},{5,6},{6,9},{7,8},{8,11},{9,10},{10,... | collective-permute-start | bytes 24584 | tf_op jit(solution)/shard_map/ppermute | solution.py:285
  46.4 7.8 %collective-permute-done.2.other_ref = f32[8,256]{1,0:T(8,128)S(1)} collective-permute-done((f32[8,256]{1,0:T(8,128)S(1)}, f32[8,256]{1,0:T(8,128)S(1)}, u32[]{:S(2)}, u32[]{:S(2)}) %collective-permute-start.2) | collective-permute-done | bytes 8224 | tf_op jit(solution)/shard_map/ppermute | solution.py:285
  54.2 0.4 all-to-all-done.2.arrived_ref
  54.6 12.7 %all_to_all.21 = f32[16,16,256]{2,1,0:T(8,128)S(1)} all-to-all(f32[16,16,256]{2,1,0:T(8,128)S(1)} %sum_shards.3), channel_id=1, replica_groups=mesh['grp'=2,'dim'=8,'blk'=2] {'dim','blk'}, dimensions={0} | all-to-all | bytes 524288 | tf_op jit(solution)/shard_map/all_to_all | solution.py:193
  67.3 0.6 kernel_weights.1
  68.0 0.0 collective-permute-done.1.other_s_ref
  68.0 28.5 %velocity.1 = f32[256,16384]{1,0:T(8,128)} custom-call(f32[256,16384]{1,0:T(8,128)} %x_ref.3, f32[256,16384]{1,0:T(8,128)} %s_ref.1, f32[256,16384]{1,0:T(8,128)} %collective-permute-done.other_ref.other_x_ref, f32[256,16384]{1,0:T(8,128)} %collective-permute-done.1.other_s_ref, bf16[256,512]{1,0:T(8,128)(2,1)S(1)} %get-tuple-element.11.hi_ref, ...), custom_call_target="tpu_custom_call" | custom-call | flops 12884901888 | bytes 83886080 | tf_op jit(solution)/shard_map/velocity/pallas_call | solution.py:256
  (1 shorter events, 0.0 us)
Async XLA Ops:
  0.0 30.6 %collective-permute-start = (f32[256,16384]{1,0:T(8,128)}, f32[256,16384]{1,0:T(8,128)}, u32[]{:S(2)}, u32[]{:S(2)}) collective-permute-start(f32[256,16384]{1,0:T(8,128)} %x_ref.3), channel_id=1, source_target_pairs={{0,1},{1,0},{2,3},{3,2},{4,5},{5,4},{6,7},{7,6},{8,9},{9,8},{10,11... | collective-permute-start | bytes 50331656 | tf_op jit(solution)/shard_map/ppermute | solution.py:270
  0.5 67.5 %collective-permute-start.1 = (f32[256,16384]{1,0:T(8,128)}, f32[256,16384]{1,0:T(8,128)}, u32[]{:S(2)}, u32[]{:S(2)}) collective-permute-start(f32[256,16384]{1,0:T(8,128)} %s_ref.1), channel_id=1, source_target_pairs={{0,1},{1,0},{2,3},{3,2},{4,5},{5,4},{6,7},{7,6},{8,9},{9,8},{10,11... | collective-permute-start | bytes 50331656 | tf_op jit(solution)/shard_map/ppermute | solution.py:270
  27.0 12.2 %all-to-all-start.1 = ((f32[8,32,256]{2,1,0:T(8,128)}), f32[8,32,256]{2,1,0:T(8,128)S(1)}, u32[]{:S(2)}, u32[]{:S(2)}) async-start(f32[8,32,256]{2,1,0:T(8,128)} %sum_shards.2), calls=%async_computation.1 | async-start | bytes 524288 | tf_op jit(solution)/shard_map/all_to_all | solution.py:193
  39.1 15.4 %all-to-all-start.2 = ((f32[16,16,256]{2,1,0:T(8,128)}), f32[16,16,256]{2,1,0:T(8,128)S(1)}, u32[]{:S(2)}, u32[]{:S(2)}) async-start(f32[16,16,256]{2,1,0:T(8,128)} %bitcast.3), calls=%async_computation.2 | async-start | bytes 524288 | tf_op jit(solution)/shard_map/all_to_all | solution.py:185
  44.7 9.5 %collective-permute-start.2 = (f32[8,256]{1,0:T(8,128)S(1)}, f32[8,256]{1,0:T(8,128)S(1)}, u32[]{:S(2)}, u32[]{:S(2)}) collective-permute-start(f32[8,256]{1,0:T(8,128)S(1)} %summary.1.summary_ref), channel_id=1, source_target_pairs={{0,3},{1,2},{2,5},{3,4},{4,7},{5,6},{6,9},{7,8},{8,11},{9,10},{10,... | collective-permute-start | bytes 24584 | tf_op jit(solution)/shard_map/ppermute | solution.py:285

commit v12 on v9

--- a/solution.py
+++ b/solution.py
@@ -66,7 +66,7 @@
     start(step + depth - 1)
     for copy in copies(step):
         copy.wait()
-    return [buffer[lax.rem(step, depth)] for buffer in buffers]
+    return [buffer.at[lax.rem(step, depth)] for buffer in buffers]
 
 
 def slots(count, rows, tile):
@@ -89,30 +89,48 @@
     return lax.broadcasted_iota(jnp.int32, (rows, rows), 0) == lax.broadcasted_iota(jnp.int32, (rows, rows), 1)
 
 
-def own_kernel(x_ref, out_ref, gram_ref, squares_ref, buffer, sems):
+def strips(rows, columns):
+    for column in range(0, columns, 256):
+        for row in range(0, rows, 32):
+            yield slice(row, row + 32), slice(column, column + 256)
+
+
+def below(where, rows):
+    return slice(where.start + rows, where.stop + rows)
+
+
+def own_kernel(x_ref, out_ref, gram_ref, squares_ref, halves_ref, buffer, sems):
     @pl.when(pl.program_id(0) == 0)
     def _():
         gram_ref[...] = jnp.zeros_like(gram_ref)
         squares_ref[...] = jnp.zeros_like(squares_ref)
 
     (x,) = fetch([x_ref], [buffer], sems)
-    hi, lo = split(x)
-    gram_ref[...] += nt_dot(jnp.concatenate([hi, lo], axis=0), hi)
-    squares_ref[...] += lane_sums(x * x)
+    rows = x.shape[0]
+    for row, column in strips(*x.shape):
+        part = x[row, column]
+        hi, lo = split(part)
+        halves_ref[row, column] = hi
+        halves_ref[below(row, rows), column] = lo
+        squares_ref[row, :] += lane_sums(part * part)
+    gram_ref[...] += nt_dot(halves_ref[...], halves_ref[:rows, :])
 
     @pl.when(pl.program_id(0) == pl.num_programs(0) - 1)
     def _():
-        rows = out_ref.shape[0]
         mixed = gram_ref[rows:, :]
         gram = gram_ref[:rows, :] + mixed + mixed.T
         norms = jnp.sum(squares_ref[...], axis=1, keepdims=True)
-        out_ref[...] = jnp.where(on_diagonal(rows), norms, norms + norms.T - 2.0 * gram)
+        distance = jnp.where(on_diagonal(rows), norms, norms + norms.T - 2.0 * gram)
+        half, quarter = rows // 2, rows // 4
+        out_ref[:half, :] = distance[:half, :]
+        out_ref[half:, :half] = distance[half:half + quarter, half:]
+        out_ref[half:, half:] = distance[half + quarter:, half:]
 
 
 def own_part(particles):
     rows, columns = particles.shape
     tile = min(GRAM_TILE, columns)
-    out = f32(rows, rows)
+    out = f32(rows * 3 // 4, rows)
     return pl.pallas_call(
         own_kernel,
         grid=(columns // tile,),
@@ -122,6 +140,7 @@
         scratch_shapes=[
             pltpu.VMEM((2 * rows, rows), jnp.float32),
             pltpu.VMEM((rows, 128), jnp.float32),
+            pltpu.VMEM((2 * rows, tile), jnp.bfloat16),
             *slots(1, rows, tile),
         ],
         compiler_params=params(52),
@@ -130,17 +149,20 @@
     )(particles)
 
 
-def pair_kernel(core_ref, mine_ref, other_ref, out_ref, gram_ref, my_buffer, buffer, sems):
+def pair_kernel(core_ref, mine_ref, other_ref, out_ref, gram_ref, my_halves, halves, my_buffer, buffer, sems):
     @pl.when(pl.program_id(0) == 0)
     def _():
         gram_ref[...] = jnp.zeros_like(gram_ref)
 
     rows = gram_ref.shape[0]
     mine, other = fetch([mine_ref, other_ref], [my_buffer, buffer], sems, core_ref[0] * pl.num_programs(0))
-    my_hi, my_lo = split(mine)
-    hi, lo = split(other)
-    both = nt_dot(jnp.concatenate([my_hi, my_lo], axis=0), hi)
-    gram_ref[...] += both[:rows] + both[rows:] + nt_dot(my_hi, lo)
+    for source, halves_ref in ((mine, my_halves), (other, halves)):
+        for row, column in strips(*source.shape):
+            hi, lo = split(source[row, column])
+            halves_ref[row, column] = hi
+            halves_ref[below(row, rows), column] = lo
+    both = nt_dot(my_halves[...], halves[:rows, :])
+    gram_ref[...] += both[:rows] + both[rows:] + nt_dot(my_halves[:rows, :], halves[rows:, :])
 
     @pl.when(pl.program_id(0) == pl.num_programs(0) - 1)
     def _():
@@ -161,7 +183,12 @@
             grid=(tiles,),
             in_specs=[in_hbm(), in_hbm()],
             out_specs=pl.BlockSpec(out.shape, lambda i, core: (0, 0)),
-            scratch_shapes=[pltpu.VMEM((rows, rows), jnp.float32), *slots(2, rows, tile)],
+            scratch_shapes=[
+                pltpu.VMEM((rows, rows), jnp.float32),
+                pltpu.VMEM((2 * rows, tile), jnp.bfloat16),
+                pltpu.VMEM((2 * rows, tile), jnp.bfloat16),
+                *slots(2, rows, tile),
+            ],
         ),
         out_shape=out,
         compiler_params=params(52),
@@ -192,17 +219,26 @@
     return lax.all_to_all(copies, axes, 0, 0).reshape(count * rows, columns)
 
 
-def summary_kernel(own_ref, out_ref):
+def summary_kernel(packed_ref, own_ref, out_ref):
+    rows = own_ref.shape[0]
+    half = rows // 2
+    upper = packed_ref[:half, :]
+    own_ref[:half, :] = upper
+    own_ref[half:, :half] = upper[:, half:].T
+    own_ref[half:half + half // 2, half:] = packed_ref[half:, :half]
+    own_ref[half + half // 2:, half:] = packed_ref[half:, half:]
     own = own_ref[...]
-    rows = own.shape[0]
     diagonal = on_diagonal(rows)
     norms = jnp.sum(jnp.where(diagonal, own, 0.0), axis=0, keepdims=True)
     total = jnp.sum(jnp.where(diagonal, 0.0, own))
     out_ref[...] = jnp.concatenate([norms, jnp.full((7, rows), total)], axis=0)
 
 
-def summary_part(own):
-    return pl.pallas_call(summary_kernel, out_shape=f32(8, own.shape[0]), compiler_params=params(8), name="summary")(own)
+def summary_part(packed):
+    rows = packed.shape[1]
+    return pl.pallas_call(
+        summary_kernel, out_shape=[f32(rows, rows), f32(8, rows)], compiler_params=params(8), name="summary"
+    )(packed)
 
 
 def weights_kernel(scale_base, core_ref, own_ref, summary_ref, other_ref, gram_ref, hi_ref, lo_ref, weight_ref, half_ref):
@@ -229,23 +265,36 @@
     return pl.pallas_call(
         functools.partial(weights_kernel, scale_base),
         in_specs=[pl.BlockSpec(memory_space=pltpu.SMEM)] + [pl.BlockSpec(memory_space=pltpu.VMEM)] * 4,
-        out_shape=[half, half, f32(rows, 128), f32(8, 128)],
+        out_shape=[half, half, f32(rows, 128), f32(32, 256)],
         compiler_params=params(12),
         name="kernel_weights",
     )(core, own, summary, other, gram)
 
 
 def velocity_kernel(
-    x_ref, s_ref, other_x_ref, other_s_ref, hi_ref, lo_ref, weight_ref, half_ref, out_ref, *scratch
+    x_ref, s_ref, other_x_ref, other_s_ref, hi_ref, lo_ref, weight_ref, half_ref, out_ref, moved_ref, *scratch
 ):
-    rows = out_ref.shape[0]
-    half = half_ref[0:1, 0:1]
+    rows, columns = out_ref.shape
+    half = half_ref[...]
+    weights = jnp.concatenate([hi_ref[...], lo_ref[...]], axis=0)
     x, s, other_x, other_s = fetch([x_ref, s_ref, other_x_ref, other_s_ref], scratch[:4], scratch[4])
-    driven = half * s
-    moved_hi, moved_lo = split(jnp.concatenate([driven - x, half * other_s - other_x], axis=0))
-    hi = hi_ref[...]
-    both = nn_dot(jnp.concatenate([hi, lo_ref[...]], axis=0), moved_hi)
-    out_ref[...] = driven + weight_ref[:, 0:1] * x + both[:rows] + both[rows:] + nn_dot(hi, moved_lo)
+    for start in range(0, columns, 256):
+        column = slice(start, start + 256)
+        for offset, points, slopes in ((0, x, s), (rows, other_x, other_s)):
+            for start_row in range(0, rows, 32):
+                row = slice(start_row, start_row + 32)
+                hi, lo = split(half * slopes[row, column] - points[row, column])
+                moved_ref[below(row, offset), column] = hi
+                moved_ref[below(row, offset + 2 * rows), column] = lo
+        both = nn_dot(weights, moved_ref[:2 * rows, column])
+        rest = nn_dot(hi_ref[...], moved_ref[2 * rows:, column])
+        for start_row in range(0, rows, 32):
+            row = slice(start_row, start_row + 32)
+            weight = weight_ref[row, :]
+            weight = jnp.concatenate([weight, weight], axis=1)
+            out_ref[row, column] = (
+                half * s[row, column] + weight * x[row, column] + both[row] + both[below(row, rows)] + rest[row]
+            )
 
 
 def velocity_part(particles, scores, visitor, visitor_scores, weights):
@@ -258,7 +307,7 @@
         in_specs=[in_hbm()] * 4 + [whole(w) for w in weights],
         out_specs=block,
         out_shape=f32(rows, columns),
-        scratch_shapes=slots(4, rows, tile),
+        scratch_shapes=[pltpu.VMEM((4 * rows, tile), jnp.bfloat16), *slots(4, rows, tile)],
         compiler_params=params(52),
         cost_estimate=pl.CostEstimate(flops=12 * rows * rows * columns, bytes_accessed=20 * rows * columns, transcendentals=0),
         name="velocity",
@@ -279,7 +328,7 @@
     visitor_scores = swap(scores)
 
     own = gathered(summed_shards(own_part(particles), "dim"), "dim")
-    summary = summary_part(own)
+    own, summary = summary_part(own)
     across = [(d * 2 + b, (d + 1) % count * 2 + 1 - b) for d in range(count) for b in range(2)]
     other = lax.ppermute(summary, BOTH, across)
 

time: 96.4 us -> 95.6 us (level)
  transfers between devices with their start and end apart: 5 -> 5, of which waited for: 3 -> 2; matrix products, arithmetic and copies ran while one was open for 0% -> 0% of each run, Pallas kernels for 20% -> 20%
where the time goes in v12:
time: 95.6 us; the launch traced here: 95.3 us
  Pallas kernels  46.7 us (49%)
  blocking collectives  28.7 us (30%)
  starting transfers between devices  11.7 us (12%)
  waiting for transfers between devices  8.18 us (9%)
    pallas_call x1, Pallas kernels, velocity_part(): pl.pallas_call(velocity_kernel, grid=(columns // tile,), in_specs=[in_hbm...  28 us
    all_to_all x1, blocking collectives, summed_shards(): lax.all_to_all(block.reshape(count, rows // count, columns), axes, 0, 0)  15.3 us
    all_to_all x1, blocking collectives, gathered(): return lax.all_to_all(copies, axes, 0, 0).reshape(count * rows, columns)  13.3 us
    pallas_call x1, Pallas kernels, own_part(): pl.pallas_call(own_kernel, grid=(columns // tile,), in_specs=[in_hbm()],...  9.41 us
    ppermute x1, waiting for transfers between devices, body(): other = lax.ppermute(summary, BOTH, across)  7.79 us
    pallas_call x1, Pallas kernels, pair_part(): pl.pallas_call(pair_kernel, grid_spec=pltpu.PrefetchScalarGridSpec(num_sc...  7.74 us
    all_to_all x1, starting transfers between devices, summed_shards(): lax.all_to_all(block.reshape(count, rows // count, columns), axes, 0, 0)  6.03 us
    all_to_all x1, starting transfers between devices, gathered(): return lax.all_to_all(copies, axes, 0, 0).reshape(count * rows, columns)  3.39 us
  transfers between devices with their start and end apart: 5, of which 2 were waited for; matrix products, arithmetic and copies ran while one was open for 0% of the time, Pallas kernels for 20%

profile of v12, /device:TPU:0, one launch (start us, length us, event | category | flops | bytes accessed | tf_op | source)
XLA Modules:
  0.0 95.3 jit_solution(11295178877139183351)
XLA Ops:
  0.0 0.5 collective-permute-start
  0.5 0.1 collective-permute-start.1
  0.5 9.4 %own_gram.1 = f32[192,256]{1,0:T(8,128)S(1)} custom-call(f32[256,16384]{1,0:T(8,128)} %x_ref.3), custom_call_target="tpu_custom_call" | custom-call | flops 4294967296 | bytes 16777216 | tf_op jit(solution)/shard_map/own_gram/pallas_call | solution.py:134
  9.9 15.3 %all_to_all.20.arrived_ref = f32[8,24,256]{2,1,0:T(8,128)S(1)} all-to-all(f32[8,24,256]{2,1,0:T(8,128)S(1)} %bitcast.6), channel_id=1, replica_groups=mesh['grp'=2,'dim'=8,'blk'=2] {'dim'}, dimensions={0} | all-to-all | bytes 393216 | tf_op jit(solution)/shard_map/all_to_all | solution.py:211
  25.3 0.7 sum_shards.2
  26.0 3.4 %all-to-all-start.1 = ((f32[8,24,256]{2,1,0:T(8,128)}), f32[8,24,256]{2,1,0:T(8,128)S(1)}, u32[]{:S(2)}, u32[]{:S(2)}) async-start(f32[8,24,256]{2,1,0:T(8,128)} %sum_shards.2), calls=%async_computation.1 | async-start | bytes 393216 | tf_op jit(solution)/shard_map/all_to_all | solution.py:219
  29.4 0.0 collective-permute-done.other_ref.other_x_ref
  29.4 7.7 %pair_gram.1 = f32[256,256]{1,0:T(8,128)} custom-call(s32[1]{0:T(128)} %bitcast.core_ref, f32[256,16384]{1,0:T(8,128)} %x_ref.3, f32[256,16384]{1,0:T(8,128)} %collective-permute-done.other_ref.other_x_ref), custom_call_target="tpu_custom_call" | custom-call | flops 3221225472 | bytes 16777216 | tf_op jit(solution)/shard_map/pair_gram/pallas_call | solution.py:179
  37.1 0.0 all-to-all-done.1
  37.1 6.0 %all-to-all-start.2 = ((f32[16,16,256]{2,1,0:T(8,128)}), f32[16,16,256]{2,1,0:T(8,128)S(1)}, u32[]{:S(2)}, u32[]{:S(2)}) async-start(f32[16,16,256]{2,1,0:T(8,128)} %bitcast.3), calls=%async_computation.2 | async-start | bytes 524288 | tf_op jit(solution)/shard_map/all_to_all | solution.py:211
  43.2 0.2 summary.1
  43.4 1.7 %collective-permute-start.2 = (f32[8,256]{1,0:T(8,128)S(1)}, f32[8,256]{1,0:T(8,128)S(1)}, u32[]{:S(2)}, u32[]{:S(2)}) collective-permute-start(f32[8,256]{1,0:T(8,128)S(1)} %get-tuple-element.13.summary_ref), channel_id=1, source_target_pairs={{0,3},{1,2},{2,5},{3,4},{4,7},{5,6},{6,9},{7,8},{8,11},{9,10},{10,... | collective-permute-start | bytes 24584 | tf_op jit(solution)/shard_map/ppermute | solution.py:333
  45.1 7.8 %collective-permute-done.2.other_ref = f32[8,256]{1,0:T(8,128)S(1)} collective-permute-done((f32[8,256]{1,0:T(8,128)S(1)}, f32[8,256]{1,0:T(8,128)S(1)}, u32[]{:S(2)}, u32[]{:S(2)}) %collective-permute-start.2) | collective-permute-done | bytes 8224 | tf_op jit(solution)/shard_map/ppermute | solution.py:333
  52.9 0.4 all-to-all-done.2.arrived_ref
  53.3 13.3 %all_to_all.21 = f32[16,16,256]{2,1,0:T(8,128)S(1)} all-to-all(f32[16,16,256]{2,1,0:T(8,128)S(1)} %sum_shards.3), channel_id=1, replica_groups=mesh['grp'=2,'dim'=8,'blk'=2] {'dim','blk'}, dimensions={0} | all-to-all | bytes 524288 | tf_op jit(solution)/shard_map/all_to_all | solution.py:219
  66.7 0.6 kernel_weights.1
  67.3 0.0 collective-permute-done.1.other_s_ref
  67.3 28.0 %velocity.1 = f32[256,16384]{1,0:T(8,128)} custom-call(f32[256,16384]{1,0:T(8,128)} %x_ref.3, f32[256,16384]{1,0:T(8,128)} %s_ref.1, f32[256,16384]{1,0:T(8,128)} %collective-permute-done.other_ref.other_x_ref, f32[256,16384]{1,0:T(8,128)} %collective-permute-done.1.other_s_ref, bf16[256,512]{1,0:T(8,128)(2,1)S(1)} %get-tuple-element.15.hi_ref, ...), custom_call_target="tpu_custom_call" | custom-call | flops 12884901888 | bytes 83886080 | tf_op jit(solution)/shard_map/velocity/pallas_call | solution.py:304
  (1 shorter events, 0.0 us)
Async XLA Ops:
  0.0 29.4 %collective-permute-start = (f32[256,16384]{1,0:T(8,128)}, f32[256,16384]{1,0:T(8,128)}, u32[]{:S(2)}, u32[]{:S(2)}) collective-permute-start(f32[256,16384]{1,0:T(8,128)} %x_ref.3), channel_id=1, source_target_pairs={{0,1},{1,0},{2,3},{3,2},{4,5},{5,4},{6,7},{7,6},{8,9},{9,8},{10,11... | collective-permute-start | bytes 50331656 | tf_op jit(solution)/shard_map/ppermute | solution.py:318
  0.5 66.9 %collective-permute-start.1 = (f32[256,16384]{1,0:T(8,128)}, f32[256,16384]{1,0:T(8,128)}, u32[]{:S(2)}, u32[]{:S(2)}) collective-permute-start(f32[256,16384]{1,0:T(8,128)} %s_ref.1), channel_id=1, source_target_pairs={{0,1},{1,0},{2,3},{3,2},{4,5},{5,4},{6,7},{7,6},{8,9},{9,8},{10,11... | collective-permute-start | bytes 50331656 | tf_op jit(solution)/shard_map/ppermute | solution.py:318
  26.0 11.2 %all-to-all-start.1 = ((f32[8,24,256]{2,1,0:T(8,128)}), f32[8,24,256]{2,1,0:T(8,128)S(1)}, u32[]{:S(2)}, u32[]{:S(2)}) async-start(f32[8,24,256]{2,1,0:T(8,128)} %sum_shards.2), calls=%async_computation.1 | async-start | bytes 393216 | tf_op jit(solution)/shard_map/all_to_all | solution.py:219
  37.1 16.2 %all-to-all-start.2 = ((f32[16,16,256]{2,1,0:T(8,128)}), f32[16,16,256]{2,1,0:T(8,128)S(1)}, u32[]{:S(2)}, u32[]{:S(2)}) async-start(f32[16,16,256]{2,1,0:T(8,128)} %bitcast.3), calls=%async_computation.2 | async-start | bytes 524288 | tf_op jit(solution)/shard_map/all_to_all | solution.py:211
  43.4 9.5 %collective-permute-start.2 = (f32[8,256]{1,0:T(8,128)S(1)}, f32[8,256]{1,0:T(8,128)S(1)}, u32[]{:S(2)}, u32[]{:S(2)}) collective-permute-start(f32[8,256]{1,0:T(8,128)S(1)} %get-tuple-element.13.summary_ref), channel_id=1, source_target_pairs={{0,3},{1,2},{2,5},{3,4},{4,7},{5,6},{6,9},{7,8},{8,11},{9,10},{10,... | collective-permute-start | bytes 24584 | tf_op jit(solution)/shard_map/ppermute | solution.py:333

commit v13 on v2

v13 whole, which is shorter than its diff:
```python
import functools
import math

import jax
import jax.numpy as jnp
from jax import lax
from jax.experimental import pallas as pl
from jax.experimental.pallas import tpu as pltpu
from jax.sharding import PartitionSpec as P

GRAM_TILE = 1024
VELOCITY_TILE = 1024
GRAM_DEPTH = 4
VELOCITY_DEPTH = 4
MIB = 1024 * 1024
BOTH = ("dim", "blk")


def params(limit):
    return pltpu.CompilerParams(vmem_limit_bytes=limit * MIB)


def split(x):
    hi = x.astype(jnp.bfloat16)
    lo = (x - hi.astype(jnp.float32)).astype(jnp.bfloat16)
    return hi, lo


def nt_dot(left, right):
    return lax.dot_general(left, right, (((1,), (1,)), ((), ())), preferred_element_type=jnp.float32)


def nn_dot(left, right):
    return jnp.dot(left, right, preferred_element_type=jnp.float32)


def lane_sums(values):
    total = values[:, :128]
    for start in range(128, values.shape[1], 128):
        total = total + values[:, start:start + 128]
    return total


def fetch(sources, buffers, sems, first=0):
    step, steps = pl.program_id(0), pl.num_programs(0)
    depth, _, tile = buffers[0].shape

    def each(at, act):
        slot = lax.rem(at, depth)
        for n, (source, buffer) in enumerate(zip(sources, buffers)):

            def one(source, block):
                columns = pl.ds(pl.multiple_of(block * tile, tile), tile)
                act(pltpu.make_async_copy(source.at[:, columns], buffer.at[slot], sems.at[n, slot]))

            if isinstance(source, tuple):
                pl.when(at < steps // 2)(functools.partial(one, source[0], at))
                pl.when(at >= steps // 2)(functools.partial(one, source[1], at - steps // 2))
            else:
                one(source, lax.rem(first + at, source.shape[1] // tile))

    def start(at):
        @pl.when(at < steps)
        def _():
            each(at, lambda copy: copy.start())

    @pl.when(step == 0)
    def _():
        for ahead in range(depth - 1):
            start(ahead)

    start(step + depth - 1)
    each(step, lambda copy: copy.wait())
    return [buffer.at[lax.rem(step, depth)] for buffer in buffers]


def slots(depth, count, rows, tile):
    return [pltpu.VMEM((depth, rows, tile), jnp.float32)] * count + [pltpu.SemaphoreType.DMA((count, depth))]


def in_hbm():
    return pl.BlockSpec(memory_space=pl.ANY)


def whole(array):
    return pl.BlockSpec(array.shape, lambda i, core: (0,) * len(array.shape))


def f32(*shape):
    return jax.ShapeDtypeStruct(shape, jnp.float32)


def on_diagonal(rows):
    return lax.broadcasted_iota(jnp.int32, (rows, rows), 0) == lax.broadcasted_iota(jnp.int32, (rows, rows), 1)


def strips(rows, columns):
    for column in range(0, columns, 256):
        for row in range(0, rows, 32):
            yield slice(row, row + 32), slice(column, column + 256)


def below(where, rows):
    return slice(where.start + rows, where.stop + rows)


def call(kernel, name, steps, in_specs, out_specs, out_shape, scratch, limit):
    return pl.pallas_call(
        kernel,
        grid_spec=pltpu.PrefetchScalarGridSpec(
            num_scalar_prefetch=1, grid=(steps,), in_specs=in_specs, out_specs=out_specs, scratch_shapes=scratch
        ),
        out_shape=out_shape,
        compiler_params=params(limit),
        cost_estimate=pl.CostEstimate(flops=1024, bytes_accessed=1024, transcendentals=0),
        name=name,
    )


def add_own(x, halves_ref, gram_ref, squares_ref):
    rows = x.shape[0]
    for row, column in strips(*x.shape):
        part = x[row, column]
        hi, lo = split(part)
        halves_ref[row, column] = hi
        halves_ref[below(row, rows), column] = lo
        squares_ref[row, :] += lane_sums(part * part)
    gram_ref[...] += nt_dot(halves_ref[...], halves_ref[:rows, :])


def sent_kernel(core_ref, x_ref, copy_ref, gram_ref, squares_ref, halves_ref, buffer, sems):
    steps = pl.num_programs(0)

    @pl.when(pl.program_id(0) == 0)
    def _():
        gram_ref[...] = jnp.zeros_like(gram_ref)
        squares_ref[...] = jnp.zeros_like(squares_ref)

    (x,) = fetch([x_ref], [buffer], sems, (1 - core_ref[0]) * steps)
    copy_ref[...] = x[...]
    add_own(x, halves_ref, gram_ref, squares_ref)


def kept_kernel(core_ref, x_ref, gram_in, squares_in, copy_ref, out_ref, gram_ref, squares_ref, halves_ref, buffer, sems):
    steps = pl.num_programs(0)

    @pl.when(pl.program_id(0) == 0)
    def _():
        gram_ref[...] = gram_in[...]
        squares_ref[...] = squares_in[...]

    (x,) = fetch([x_ref], [buffer], sems, core_ref[0] * steps)
    copy_ref[...] = x[...]
    add_own(x, halves_ref, gram_ref, squares_ref)

    @pl.when(pl.program_id(0) == steps - 1)
    def _():
        rows = x.shape[0]
        half = rows // 2
        mixed = gram_ref[rows:, :]
        gram = gram_ref[:rows, :] + mixed + mixed.T
        norms = jnp.sum(squares_ref[...], axis=1, keepdims=True)
        distance = norms + norms.T - 2.0 * gram
        down = lax.broadcasted_iota(jnp.int32, (half, half), 0)
        across = lax.broadcasted_iota(jnp.int32, (half, half), 1)
        square = jnp.where(across > down, distance[:half, :half], distance[half:, half:])
        out_ref[:, :half] = jnp.where(across == down, 0.0, square)
        out_ref[:, half:] = distance[:half, half:]


def own_parts(core, particles):
    rows, columns = particles.shape
    width = columns // 2
    tile = min(GRAM_TILE, width)
    block = pl.BlockSpec((rows, tile), lambda i, core: (0, i))
    sums = [f32(2 * rows, rows), f32(rows, 128)]
    scratch = [pltpu.VMEM((2 * rows, tile), jnp.bfloat16), *slots(GRAM_DEPTH, 1, rows, tile)]
    sent, *partial = call(
        sent_kernel, "own_gram_sent", width // tile, [in_hbm()], [block] + [whole(o) for o in sums],
        [f32(rows, width)] + sums, scratch, 56,
    )(core, particles)
    packed = f32(rows // 2, rows)
    kept, packed = call(
        kept_kernel, "own_gram_kept", width // tile, [in_hbm()] + [whole(o) for o in sums], [block, whole(packed)],
        [f32(rows, width), packed], [pltpu.VMEM(o.shape, jnp.float32) for o in sums] + scratch, 56,
    )(core, particles, *partial)
    return sent, kept, packed


def pair_kernel(core_ref, mine_ref, other_ref, packed_ref, out_ref, gram_ref, squares_ref, my_halves, halves, *scratch):
    my_buffer, buffer, sems = scratch
    steps = pl.num_programs(0)
    rows = gram_ref.shape[0]

    @pl.when(pl.program_id(0) == 0)
    def _():
        gram_ref[...] = jnp.zeros_like(gram_ref)
        squares_ref[...] = jnp.zeros_like(squares_ref)

    mine, other = fetch([mine_ref, other_ref], [my_buffer, buffer], sems, core_ref[0] * steps)
    for offset, source, halves_ref in ((0, mine, my_halves), (rows, other, halves)):
        for row, column in strips(*source.shape):
            part = source[row, column]
            hi, lo = split(part)
            halves_ref[row, column] = hi
            halves_ref[below(row, rows), column] = lo
            squares_ref[below(row, offset), :] += lane_sums(part * part)
    both = nt_dot(my_halves[...], halves[:rows, :])
    gram_ref[...] += both[:rows] + both[rows:] + nt_dot(my_halves[:rows, :], halves[rows:, :])

    @pl.when(pl.program_id(0) == steps - 1)
    def _():
        norms = jnp.sum(squares_ref[:rows, :], axis=1, keepdims=True)
        others = jnp.sum(squares_ref[rows:, :], axis=1, keepdims=True)
        pair = norms + others.T - 2.0 * gram_ref[...]
        gram_ref[...] = jnp.where(core_ref[0] == 0, pair, pair.T)
        count = out_ref.shape[0]
        depth, few = rows // count, rows // 2 // count
        for shard in range(count):
            out_ref[shard, :depth, :] = gram_ref[shard * depth:(shard + 1) * depth, :]
            out_ref[shard, depth:, :] = packed_ref[shard * few:(shard + 1) * few, :]


def pair_part(core, particles, visitor, packed, count):
    rows, width = visitor.shape
    tile = min(GRAM_TILE, width)
    out = f32(count, rows * 3 // 2 // count, rows)
    return call(
        pair_kernel, "pair_gram", width // tile, [in_hbm(), in_hbm(), whole(packed)], whole(out), out,
        [
            pltpu.VMEM((rows, rows), jnp.float32),
            pltpu.VMEM((2 * rows, 128), jnp.float32),
            pltpu.VMEM((2 * rows, tile), jnp.bfloat16),
            pltpu.VMEM((2 * rows, tile), jnp.bfloat16),
            *slots(GRAM_DEPTH, 2, rows, tile),
        ],
        56,
    )(core, particles, visitor, packed)


def sum_kernel(place_ref, arrived_ref, out_ref):
    count, height, rows = arrived_ref.shape
    depth = rows // count
    few = height - depth
    pair = arrived_ref[0, :depth, :]
    for source in range(1, count):
        pair = pair + arrived_ref[source, :depth, :]
    own = []
    for core in range(2):
        total = arrived_ref[core, depth:, :]
        for source in range(core + 2, count, 2):
            total = total + arrived_ref[source, depth:, :]
        own.append(total)
    down = lax.broadcasted_iota(jnp.int32, (few, rows), 0) + place_ref[0] * few
    free = down == lax.broadcasted_iota(jnp.int32, (few, rows), 1)
    for core in range(2):
        elsewhere = jnp.sum(jnp.where(free, 0.0, own[1 - core]), keepdims=True)
        shard = jnp.where(free, elsewhere * (2.0 / few), own[core])
        for target in range(core, count, 2):
            out_ref[target, :depth, :] = pair
            out_ref[target, depth:, :] = shard


def summed_shards(place, arrived):
    return pl.pallas_call(
        sum_kernel,
        in_specs=[pl.BlockSpec(memory_space=pltpu.SMEM), pl.BlockSpec(memory_space=pltpu.VMEM)],
        out_shape=f32(*arrived.shape),
        compiler_params=params(12),
        name="sum_shards",
    )(place, arrived)


def weights_kernel(scale_base, core_ref, shards_ref, hi_ref, lo_ref, weight_ref, half_ref, pair_ref, packed_ref):
    count, height, rows = shards_ref.shape
    depth, half = rows // count, rows // 2
    few = height - depth
    for shard in range(count):
        pair_ref[shard * depth:(shard + 1) * depth, :] = shards_ref[shard, :depth, :]
        packed_ref[shard * few:(shard + 1) * few, :] = shards_ref[shard, depth:, :]
    pair = pair_ref[...]
    pair = jnp.where(core_ref[0] == 0, pair, pair.T)
    square, corner = packed_ref[:, :half], packed_ref[:, half:]
    down = lax.broadcasted_iota(jnp.int32, (half, half), 0)
    across = lax.broadcasted_iota(jnp.int32, (half, half), 1)
    elsewhere = jnp.sum(jnp.where(across == down, square, 0.0), keepdims=True)
    upper = jnp.where(across == down, 0.0, jnp.where(across > down, square, square.T))
    lower = jnp.where(across == down, 0.0, jnp.where(across < down, square, square.T))
    own = jnp.concatenate(
        [jnp.concatenate([upper, corner], axis=1), jnp.concatenate([corner.T, lower], axis=1)], axis=0
    )
    spread = elsewhere + jnp.sum(own, keepdims=True) + 2.0 * jnp.sum(pair, keepdims=True)
    width = spread / scale_base
    inverse = -1.0 / width
    own_weights = jnp.where(on_diagonal(rows), 0.0, jnp.exp(own * inverse))
    pair_weights = jnp.exp(pair * inverse)
    weights = jnp.concatenate([own_weights, pair_weights], axis=1)
    hi_ref[...], lo_ref[...] = split(weights)
    weight_ref[...] = jnp.broadcast_to(jnp.sum(weights, axis=1, keepdims=True), weight_ref.shape)
    half_ref[...] = jnp.broadcast_to(0.5 * width, half_ref.shape)


def weights_part(core, shards, scale_base):
    rows = shards.shape[2]
    bf16 = jax.ShapeDtypeStruct((rows, 2 * rows), jnp.bfloat16)
    return pl.pallas_call(
        functools.partial(weights_kernel, scale_base),
        in_specs=[pl.BlockSpec(memory_space=pltpu.SMEM), pl.BlockSpec(memory_space=pltpu.VMEM)],
        out_shape=[bf16, bf16, f32(rows, 128), f32(32, 256)],
        scratch_shapes=[pltpu.VMEM((rows, rows), jnp.float32), pltpu.VMEM((rows // 2, rows), jnp.float32)],
        compiler_params=params(16),
        name="kernel_weights",
    )(core, shards)


def velocity_kernel(
    core_ref, x_ref, s_ref, first_x_ref, second_x_ref, other_s_ref, hi_ref, lo_ref, weight_ref, half_ref, out_ref, moved_ref, *scratch
):
    rows, columns = out_ref.shape
    half = half_ref[...]
    weights = jnp.concatenate([hi_ref[...], lo_ref[...]], axis=0)
    x, s, other_x, other_s = fetch(
        [x_ref, s_ref, (first_x_ref, second_x_ref), other_s_ref],
        scratch[:4],
        scratch[4],
        core_ref[0] * (pl.num_programs(0) // 2),
    )
    for start in range(0, columns, 256):
        column = slice(start, start + 256)
        for offset, points, slopes in ((0, x, s), (rows, other_x, other_s)):
            for start_row in range(0, rows, 32):
                row = slice(start_row, start_row + 32)
                hi, lo = split(half * slopes[row, column] - points[row, column])
                moved_ref[below(row, offset), column] = hi
                moved_ref[below(row, offset + 2 * rows), column] = lo
        both = nn_dot(weights, moved_ref[:2 * rows, column])
        rest = nn_dot(hi_ref[...], moved_ref[2 * rows:, column])
        for start_row in range(0, rows, 32):
            row = slice(start_row, start_row + 32)
            weight = weight_ref[row, :]
            weight = jnp.concatenate([weight, weight], axis=1)
            out_ref[row, column] = (
                half * s[row, column] + weight * x[row, column] + both[row] + both[below(row, rows)] + rest[row]
            )


def velocity_part(core, particles, scores, visitors, visitor_scores, weights):
    rows, columns = particles.shape
    tile = min(VELOCITY_TILE, columns // 2)
    steps = columns // tile
    return call(
        velocity_kernel, "velocity", steps, [in_hbm()] * 5 + [whole(w) for w in weights],
        pl.BlockSpec((rows, tile), lambda i, core: (0, lax.rem(core[0] * (steps // 2) + i, steps))),
        f32(rows, columns), [pltpu.VMEM((4 * rows, tile), jnp.bfloat16), *slots(VELOCITY_DEPTH, 4, rows, tile)],
        52,
    )(core, particles, scores, *visitors, visitor_scores, *weights)


def swap(array):
    return lax.ppermute(array, "blk", [(0, 1), (1, 0)])


def body(particles, scores):
    total_rows = particles.shape[0] * lax.axis_size("blk")
    scale_base = total_rows * total_rows * math.log(total_rows)
    core = lax.axis_index("blk").reshape(1)
    place = lax.axis_index("dim").reshape(1) * 2 + core

    sent, kept, packed = own_parts(core, particles)
    visitor = swap(sent)
    kept, scores_late, _ = lax.optimization_barrier((kept, scores, visitor))
    visitors = [visitor, swap(kept)]
    visitor_scores = swap(scores_late)

    shards = pair_part(core, particles, visitor, packed, lax.axis_size(BOTH))
    shards = summed_shards(place, lax.all_to_all(shards, BOTH, 0, 0))
    weights = weights_part(core, lax.all_to_all(shards, BOTH, 0, 0), scale_base)
    return velocity_part(core, particles, scores, visitors, visitor_scores, weights)


def solution(mesh):
    return jax.shard_map(
        body,
        mesh=mesh,
        in_specs=(P(("grp", "blk"), "dim"), P(("grp", "blk"), "dim")),
        out_specs=P(("grp", "blk"), "dim"),
        check_vma=False,
    )
```

time: 174 us -> 95.2 us (0.55)
  matrix products: 69.6 us -> 0 us
  Pallas kernels: 0 us -> 54.7 us
  other arithmetic: 44.5 us -> 0 us
  blocking collectives: 26.8 us -> 15.7 us
  waiting for transfers between devices: 20.3 us -> 16.1 us
  local copies, waits for them, and re-layouts: 2.9 us -> 0 us
  between operations: 2.02 us -> 0.07 us
    dot_general x3 -> x0, matrix products: 69.6 us -> none  [dot3(): jnp.dot(left, right, precision=lax.Precision.HIGH, preferred_element_type...]
    pallas_call x0 -> x6, Pallas kernels: none -> 54.7 us  [the longest x1 28 us: velocity_part(): call(velocity_kernel, 'velocity', steps, [in_hbm()] * 5 + [whole(w) for w...]
    sub x2 -> x0, other arithmetic: 35.5 us -> none  [the longest x1 17.7 us: body(): half * visitor_scores - visitor]
    all_to_all x2 -> x1, blocking collectives: 26.8 us -> 15.7 us  [body(): weights = weights_part(core, lax.all_to_all(shards, BOTH, 0, 0), scale_base)]
    reduce_sum x5 -> x0, other arithmetic: 8.15 us -> none  [the longest x1 7 us: body(): norms = jnp.sum(particles * particles, axis=1)]
    ppermute x1 -> x0, waiting for transfers between devices: 5.69 us -> none  [body(): other = lax.ppermute(summary, ('dim', 'blk'), across)]
    ppermute x2 -> x3, waiting for transfers between devices: 0.01 us -> 3.87 us  [swap(): return lax.ppermute(array, 'blk', [(0, 1), (1, 0)])]
    all_to_all x2 -> x1, waiting for transfers between devices: 14.6 us -> 12.2 us  [body(): shards = summed_shards(place, lax.all_to_all(shards, BOTH, 0, 0))]
  transfers between devices with their start and end apart: 5 -> 4, of which waited for: 3 -> 2; matrix products, arithmetic and copies ran while one was open for 39% -> 0% of each run, Pallas kernels for 0% -> 20%
where the time goes in v13:
time: 95.2 us; the launch traced here: 94.9 us
  Pallas kernels  54.7 us (57%)
  waiting for transfers between devices  16.1 us (17%)
  blocking collectives  15.7 us (16%)
  starting transfers between devices  8.36 us (9%)
    pallas_call x1, Pallas kernels, velocity_part(): call(velocity_kernel, 'velocity', steps, [in_hbm()] * 5 + [whole(w) for w...  28 us
    all_to_all x1, blocking collectives, body(): weights = weights_part(core, lax.all_to_all(shards, BOTH, 0, 0), scale_base)  15.7 us
    all_to_all x1, waiting for transfers between devices, body(): shards = summed_shards(place, lax.all_to_all(shards, BOTH, 0, 0))  12.2 us
    pallas_call x1, Pallas kernels, own_parts(): call(kept_kernel, 'own_gram_kept', width // tile, [in_hbm()] + [whole(o)...  9.26 us
    pallas_call x1, Pallas kernels, pair_part(): call(pair_kernel, 'pair_gram', width // tile, [in_hbm(), in_hbm(), whole(...  8.98 us
    pallas_call x1, Pallas kernels, own_parts(): call(sent_kernel, 'own_gram_sent', width // tile, [in_hbm()], [block] + [...  7.8 us
    all_to_all x1, starting transfers between devices, body(): shards = summed_shards(place, lax.all_to_all(shards, BOTH, 0, 0))  7.32 us
    ppermute x3, waiting for transfers between devices, swap(): return lax.ppermute(array, 'blk', [(0, 1), (1, 0)])  3.87 us
  transfers between devices with their start and end apart: 4, of which 2 were waited for; matrix products, arithmetic and copies ran while one was open for 0% of the time, Pallas kernels for 20%

profile of v13, /device:TPU:0, one launch (start us, length us, event | category | flops | bytes accessed | tf_op | source)
XLA Modules:
  0.0 94.9 jit_solution(8067612548473763842)
XLA Ops:
  0.0 7.8 %own_gram_sent.1 = (f32[256,8192]{1,0:T(8,128)}, f32[512,256]{1,0:T(8,128)}, f32[256,128]{1,0:T(8,128)}) custom-call(s32[1]{0:T(128)} %bitcast.core_ref, f32[256,16384]{1,0:T(8,128)} %x_ref.5), custom_call_target="tpu_custom_call" | custom-call | flops 1024 | bytes 1024 | tf_op jit(solution)/shard_map/own_gram_sent/pallas_call | solution.py:178
  7.8 0.5 collective-permute-start
  8.3 9.3 %own_gram_kept.1 = (f32[256,8192]{1,0:T(8,128)}, f32[128,256]{1,0:T(8,128)}) custom-call(s32[1]{0:T(128)} %bitcast.core_ref, f32[256,16384]{1,0:T(8,128)} %x_ref.5, f32[512,256]{1,0:T(8,128)} %get-tuple-element.17.gram_in, f32[256,128]{1,0:T(8,128)} %get-tuple-element.18.squares_in), custom_call_target="tpu_custom_call" | custom-call | flops 1024 | bytes 1024 | tf_op jit(solution)/shard_map/own_gram_kept/pallas_call | solution.py:183
  17.6 3.9 %collective-permute-done.other_ref.first_x_ref = f32[256,8192]{1,0:T(8,128)} collective-permute-done((f32[256,8192]{1,0:T(8,128)}, f32[256,8192]{1,0:T(8,128)}, u32[]{:S(2)}, u32[]{:S(2)}) %collective-permute-start) | collective-permute-done | bytes 8388640 | tf_op jit(solution)/shard_map/ppermute | solution.py:360
  21.5 0.4 collective-permute-start.2
  21.8 0.1 collective-permute-start.1
  22.0 9.0 %pair_gram.1 = f32[16,24,256]{2,1,0:T(8,128)} custom-call(s32[1]{0:T(128)} %bitcast.core_ref, f32[256,16384]{1,0:T(8,128)} %x_ref.5, f32[256,8192]{1,0:T(8,128)} %collective-permute-done.other_ref.first_x_ref, f32[128,256]{1,0:T(8,128)} %get-tuple-element.22.packed_ref), custom_call_target="tpu_custom_call" | custom-call | flops 1024 | bytes 1024 | tf_op jit(solution)/shard_map/pair_gram/pallas_call | solution.py:228
  31.0 7.3 %all-to-all-start = ((f32[16,24,256]{2,1,0:T(8,128)}), f32[16,24,256]{2,1,0:T(8,128)S(1)}, u32[]{:S(2)}, u32[]{:S(2)}) async-start(f32[16,24,256]{2,1,0:T(8,128)} %pair_gram.1), calls=%async_computation | async-start | bytes 786432 | tf_op jit(solution)/shard_map/all_to_all | solution.py:376
  38.3 12.2 %all-to-all-done.arrived_ref = f32[16,24,256]{2,1,0:T(8,128)S(1)} async-done(((f32[16,24,256]{2,1,0:T(8,128)}), f32[16,24,256]{2,1,0:T(8,128)S(1)}, u32[]{:S(2)}, u32[]{:S(2)}) %all-to-all-start) | async-done | bytes 393248 | tf_op jit(solution)/shard_map/all_to_all | solution.py:376
  50.5 0.1 sum_shards.1
  50.6 15.7 %all_to_all.10.shards_ref = f32[16,24,256]{2,1,0:T(8,128)S(1)} all-to-all(f32[16,24,256]{2,1,0:T(8,128)S(1)} %sum_shards.1), channel_id=1, replica_groups=mesh['grp'=2,'dim'=8,'blk'=2] {'dim','blk'}, dimensions={0} | all-to-all | bytes 786432 | tf_op jit(solution)/shard_map/all_to_all | solution.py:377
  66.4 0.5 kernel_weights.1
  66.9 0.0 collective-permute-done.1.second_x_ref
  66.9 0.0 collective-permute-done.2.other_s_ref
  66.9 28.0 %velocity.1 = f32[256,16384]{1,0:T(8,128)} custom-call(s32[1]{0:T(128)} %bitcast.core_ref, f32[256,16384]{1,0:T(8,128)} %x_ref.5, f32[256,16384]{1,0:T(8,128)} %s_ref.1, f32[256,8192]{1,0:T(8,128)} %collective-permute-done.other_ref.first_x_ref, f32[256,8192]{1,0:T(8,128)} %collective-permute-done.1.second_x_ref, ...), custom_call_target="tpu_custom_call" | custom-call | flops 1024 | bytes 1024 | tf_op jit(solution)/shard_map/velocity/pallas_call | solution.py:351
Async XLA Ops:
  7.8 13.7 %collective-permute-start = (f32[256,8192]{1,0:T(8,128)}, f32[256,8192]{1,0:T(8,128)}, u32[]{:S(2)}, u32[]{:S(2)}) collective-permute-start(f32[256,8192]{1,0:T(8,128)} %get-tuple-element.16), channel_id=1, source_target_pairs={{0,1},{1,0},{2,3},{3,2},{4,5},{5,4},{6,7},{7,6},{8,9},{9,8},{10,11... | collective-permute-start | bytes 25165832 | tf_op jit(solution)/shard_map/ppermute | solution.py:360
  21.5 45.4 %collective-permute-start.2 = (f32[256,16384]{1,0:T(8,128)}, f32[256,16384]{1,0:T(8,128)}, u32[]{:S(2)}, u32[]{:S(2)}) collective-permute-start(f32[256,16384]{1,0:T(8,128)} %s_ref.1), channel_id=1, source_target_pairs={{0,1},{1,0},{2,3},{3,2},{4,5},{5,4},{6,7},{7,6},{8,9},{9,8},{10,11... | collective-permute-start | bytes 50331656 | tf_op jit(solution)/shard_map/ppermute | solution.py:360
  21.8 45.0 %collective-permute-start.1 = (f32[256,8192]{1,0:T(8,128)}, f32[256,8192]{1,0:T(8,128)}, u32[]{:S(2)}, u32[]{:S(2)}) collective-permute-start(f32[256,8192]{1,0:T(8,128)} %get-tuple-element.20), channel_id=1, source_target_pairs={{0,1},{1,0},{2,3},{3,2},{4,5},{5,4},{6,7},{7,6},{8,9},{9,8},{10,11... | collective-permute-start | bytes 25165832 | tf_op jit(solution)/shard_map/ppermute | solution.py:360
  31.0 19.5 %all-to-all-start = ((f32[16,24,256]{2,1,0:T(8,128)}), f32[16,24,256]{2,1,0:T(8,128)S(1)}, u32[]{:S(2)}, u32[]{:S(2)}) async-start(f32[16,24,256]{2,1,0:T(8,128)} %pair_gram.1), calls=%async_computation | async-start | bytes 786432 | tf_op jit(solution)/shard_map/all_to_all | solution.py:376

commit v14 on v13

--- a/solution.py
+++ b/solution.py
@@ -54,8 +54,11 @@
                 act(pltpu.make_async_copy(source.at[:, columns], buffer.at[slot], sems.at[n, slot]))
 
             if isinstance(source, tuple):
-                pl.when(at < steps // 2)(functools.partial(one, source[0], at))
-                pl.when(at >= steps // 2)(functools.partial(one, source[1], at - steps // 2))
+                begin = 0
+                for piece in source:
+                    end = begin + piece.shape[1] // tile
+                    pl.when((at >= begin) & (at < end))(functools.partial(one, piece, at - begin))
+                    begin = end
             else:
                 one(source, lax.rem(first + at, source.shape[1] // tile))
 
@@ -128,7 +131,49 @@
     gram_ref[...] += nt_dot(halves_ref[...], halves_ref[:rows, :])
 
 
-def sent_kernel(core_ref, x_ref, copy_ref, gram_ref, squares_ref, halves_ref, buffer, sems):
+def cut_kernel(begin, of_other, core_ref, x_ref, out_ref, buffer, in_sems, out_sems):
+    columns = out_ref.shape[1]
+    half = x_ref.shape[1] // 2
+    side = 1 - core_ref[0] if of_other else core_ref[0]
+    step = columns // in_sems.shape[0]
+    start = pl.multiple_of(side * half + begin, step)
+    ins, outs = [], []
+    for n in range(in_sems.shape[0]):
+        there = pl.ds(n * step, step)
+        here = pl.ds(pl.multiple_of(start + n * step, step), step)
+        ins.append(pltpu.make_async_copy(x_ref.at[:, here], buffer.at[:, there], in_sems.at[n]))
+        outs.append(pltpu.make_async_copy(buffer.at[:, there], out_ref.at[:, there], out_sems.at[n]))
+    for copy in ins:
+        copy.start()
+    for arriving, leaving in zip(ins, outs):
+        arriving.wait()
+        leaving.start()
+    for copy in outs:
+        copy.wait()
+
+
+def cut(core, array, begin, width, of_other):
+    rows = array.shape[0]
+    pieces = max(1, width // 512)
+    return pl.pallas_call(
+        functools.partial(cut_kernel, begin, of_other),
+        in_specs=[pl.BlockSpec(memory_space=pltpu.SMEM), in_hbm()],
+        out_specs=in_hbm(),
+        out_shape=f32(rows, width),
+        scratch_shapes=[
+            pltpu.VMEM((rows, width), jnp.float32),
+            pltpu.SemaphoreType.DMA((pieces,)),
+            pltpu.SemaphoreType.DMA((pieces,)),
+        ],
+        compiler_params=params(56),
+        cost_estimate=pl.CostEstimate(
+            flops=0, bytes_accessed=1024 if of_other else 8 * rows * width, transcendentals=0
+        ),
+        name="cut_positions",
+    )(core, array)
+
+
+def own_kernel(core_ref, x_ref, out_ref, gram_ref, squares_ref, halves_ref, buffer, sems):
     steps = pl.num_programs(0)
 
     @pl.when(pl.program_id(0) == 0)
@@ -136,21 +181,7 @@
         gram_ref[...] = jnp.zeros_like(gram_ref)
         squares_ref[...] = jnp.zeros_like(squares_ref)
 
-    (x,) = fetch([x_ref], [buffer], sems, (1 - core_ref[0]) * steps)
-    copy_ref[...] = x[...]
-    add_own(x, halves_ref, gram_ref, squares_ref)
-
-
-def kept_kernel(core_ref, x_ref, gram_in, squares_in, copy_ref, out_ref, gram_ref, squares_ref, halves_ref, buffer, sems):
-    steps = pl.num_programs(0)
-
-    @pl.when(pl.program_id(0) == 0)
-    def _():
-        gram_ref[...] = gram_in[...]
-        squares_ref[...] = squares_in[...]
-
-    (x,) = fetch([x_ref], [buffer], sems, core_ref[0] * steps)
-    copy_ref[...] = x[...]
+    (x,) = fetch([x_ref], [buffer], sems)
     add_own(x, halves_ref, gram_ref, squares_ref)
 
     @pl.when(pl.program_id(0) == steps - 1)
@@ -168,26 +199,25 @@
         out_ref[:, half:] = distance[:half, half:]
 
 
-def own_parts(core, particles):
+def own_part(core, particles):
     rows, columns = particles.shape
-    width = columns // 2
-    tile = min(GRAM_TILE, width)
-    block = pl.BlockSpec((rows, tile), lambda i, core: (0, i))
-    sums = [f32(2 * rows, rows), f32(rows, 128)]
-    scratch = [pltpu.VMEM((2 * rows, tile), jnp.bfloat16), *slots(GRAM_DEPTH, 1, rows, tile)]
-    sent, *partial = call(
-        sent_kernel, "own_gram_sent", width // tile, [in_hbm()], [block] + [whole(o) for o in sums],
-        [f32(rows, width)] + sums, scratch, 56,
+    tile = min(GRAM_TILE, columns)
+    packed = f32(rows // 2, rows)
+    return call(
+        own_kernel, "own_gram", columns // tile, [in_hbm()], whole(packed), packed,
+        [
+            pltpu.VMEM((2 * rows, rows), jnp.float32),
+            pltpu.VMEM((rows, 128), jnp.float32),
+            pltpu.VMEM((2 * rows, tile), jnp.bfloat16),
+            *slots(GRAM_DEPTH, 1, rows, tile),
+        ],
+        56,
     )(core, particles)
-    packed = f32(rows // 2, rows)
-    kept, packed = call(
-        kept_kernel, "own_gram_kept", width // tile, [in_hbm()] + [whole(o) for o in sums], [block, whole(packed)],
-        [f32(rows, width), packed], [pltpu.VMEM(o.shape, jnp.float32) for o in sums] + scratch, 56,
-    )(core, particles, *partial)
-    return sent, kept, packed
-
-
-def pair_kernel(core_ref, mine_ref, other_ref, packed_ref, out_ref, gram_ref, squares_ref, my_halves, halves, *scratch):
+
+
+def pair_kernel(
+    core_ref, mine_ref, other_ref, packed_ref, out_ref, gram_ref, squares_ref, my_halves, halves, *scratch
+):
     my_buffer, buffer, sems = scratch
     steps = pl.num_programs(0)
     rows = gram_ref.shape[0]
@@ -221,12 +251,12 @@
             out_ref[shard, depth:, :] = packed_ref[shard * few:(shard + 1) * few, :]
 
 
-def pair_part(core, particles, visitor, packed, count):
-    rows, width = visitor.shape
+def pair_part(core, particles, visitors, packed, count):
+    rows, width = particles.shape[0], particles.shape[1] // 2
     tile = min(GRAM_TILE, width)
     out = f32(count, rows * 3 // 2 // count, rows)
     return call(
-        pair_kernel, "pair_gram", width // tile, [in_hbm(), in_hbm(), whole(packed)], whole(out), out,
+        pair_kernel, "pair_gram", width // tile, [in_hbm()] * 2 + [whole(packed)], whole(out), out,
         [
             pltpu.VMEM((rows, rows), jnp.float32),
             pltpu.VMEM((2 * rows, 128), jnp.float32),
@@ -235,7 +265,7 @@
             *slots(GRAM_DEPTH, 2, rows, tile),
         ],
         56,
-    )(core, particles, visitor, packed)
+    )(core, particles, *visitors, packed)
 
 
 def sum_kernel(place_ref, arrived_ref, out_ref):
@@ -266,7 +296,7 @@
         sum_kernel,
         in_specs=[pl.BlockSpec(memory_space=pltpu.SMEM), pl.BlockSpec(memory_space=pltpu.VMEM)],
         out_shape=f32(*arrived.shape),
-        compiler_params=params(12),
+        compiler_params=params(58),
         name="sum_shards",
     )(place, arrived)
 
@@ -314,13 +344,13 @@
 
 
 def velocity_kernel(
-    core_ref, x_ref, s_ref, first_x_ref, second_x_ref, other_s_ref, hi_ref, lo_ref, weight_ref, half_ref, out_ref, moved_ref, *scratch
+    core_ref, x_ref, s_ref, first_x_ref, last_x_ref, other_s_ref, hi_ref, lo_ref, weight_ref, half_ref, out_ref, moved_ref, *scratch
 ):
     rows, columns = out_ref.shape
     half = half_ref[...]
     weights = jnp.concatenate([hi_ref[...], lo_ref[...]], axis=0)
     x, s, other_x, other_s = fetch(
-        [x_ref, s_ref, (first_x_ref, second_x_ref), other_s_ref],
+        [x_ref, s_ref, (first_x_ref, last_x_ref), other_s_ref],
         scratch[:4],
         scratch[4],
         core_ref[0] * (pl.num_programs(0) // 2),
@@ -366,13 +396,17 @@
     core = lax.axis_index("blk").reshape(1)
     place = lax.axis_index("dim").reshape(1) * 2 + core
 
-    sent, kept, packed = own_parts(core, particles)
-    visitor = swap(sent)
-    kept, scores_late, _ = lax.optimization_barrier((kept, scores, visitor))
-    visitors = [visitor, swap(kept)]
+    width = particles.shape[1] // 2
+    sent = cut(core, particles, 0, width, True)
+    visitors = [swap(sent)]
+    particles_next, _ = lax.optimization_barrier((particles, sent))
+    packed = own_part(core, particles_next)
+    scores_late, *_ = lax.optimization_barrier((scores, visitors[0], packed))
     visitor_scores = swap(scores_late)
 
-    shards = pair_part(core, particles, visitor, packed, lax.axis_size(BOTH))
+    shards = pair_part(core, particles, visitors, packed, lax.axis_size(BOTH))
+    particles_next, _ = lax.optimization_barrier((particles, shards))
+    visitors.append(swap(cut(core, particles_next, 0, width, False)))
     shards = summed_shards(place, lax.all_to_all(shards, BOTH, 0, 0))
     weights = weights_part(core, lax.all_to_all(shards, BOTH, 0, 0), scale_base)
     return velocity_part(core, particles, scores, visitors, visitor_scores, weights)

time: 95.2 us -> 103 us (1.082)
  Pallas kernels: 54.7 us -> 62.8 us
    pallas_call x3 -> x4, Pallas kernels: 26 us -> 32.4 us  [the longest x2 13.3 us: cut(): pl.pallas_call(functools.partial(cut_kernel, begin, of_other), in_specs=[...]
    pallas_call x1, Pallas kernels: 0.14 us -> 1.89 us  [summed_shards(): pl.pallas_call(sum_kernel, in_specs=[pl.BlockSpec(memory_space=pltpu.SMEM...]
  transfers between devices with their start and end apart: 4 -> 4, of which waited for: 2 -> 2; matrix products, arithmetic and copies ran while one was open for 0% -> 0% of each run, Pallas kernels for 20% -> 27%
where the time goes in v14:
time: 103 us
  Pallas kernels  62.8 us (61%)
  blocking collectives  15.7 us (15%)
  waiting for transfers between devices  15.1 us (15%)
  starting transfers between devices  8.41 us (8%)
    pallas_call x1, Pallas kernels, velocity_part(): call(velocity_kernel, 'velocity', steps, [in_hbm()] * 5 + [whole(w) for w...  28 us
    all_to_all x1, blocking collectives, body(): weights = weights_part(core, lax.all_to_all(shards, BOTH, 0, 0), scale_base)  15.7 us
    pallas_call x2, Pallas kernels, cut(): pl.pallas_call(functools.partial(cut_kernel, begin, of_other), in_specs=[...  13.3 us
    all_to_all x1, waiting for transfers between devices, body(): shards = summed_shards(place, lax.all_to_all(shards, BOTH, 0, 0))  12.2 us
    pallas_call x1, Pallas kernels, own_part(): call(own_kernel, 'own_gram', columns // tile, [in_hbm()], whole(packed),...  10.2 us
    pallas_call x1, Pallas kernels, pair_part(): call(pair_kernel, 'pair_gram', width // tile, [in_hbm()] * 2 + [whole(pac...  8.99 us
    all_to_all x1, starting transfers between devices, body(): shards = summed_shards(place, lax.all_to_all(shards, BOTH, 0, 0))  7.32 us
    ppermute x3, waiting for transfers between devices, swap(): return lax.ppermute(array, 'blk', [(0, 1), (1, 0)])  2.94 us
  transfers between devices with their start and end apart: 4, of which 2 were waited for; matrix products, arithmetic and copies ran while one was open for 0% of the time, Pallas kernels for 27%

profile of v14, /device:TPU:0, one launch (start us, length us, event | category | flops | bytes accessed | tf_op | source)
XLA Modules:
  0.0 102.9 jit_solution(16319609895350181506)
XLA Ops:
  0.0 6.6 %cut_positions.2 = f32[256,8192]{1,0:T(8,128)} custom-call(s32[1]{0:T(128)} %bitcast.core_ref, f32[256,16384]{1,0:T(8,128)} %x_ref.5), custom_call_target="tpu_custom_call" | custom-call | bytes 1024 | tf_op jit(solution)/shard_map/cut_positions/pallas_call | solution.py:158
  6.6 0.5 collective-permute-start
  7.1 10.2 %own_gram.1.packed_ref = f32[128,256]{1,0:T(8,128)} custom-call(s32[1]{0:T(128)} %bitcast.core_ref, f32[256,16384]{1,0:T(8,128)} %x_ref.5), custom_call_target="tpu_custom_call" | custom-call | flops 1024 | bytes 1024 | tf_op jit(solution)/shard_map/own_gram/pallas_call | solution.py:206
  17.3 2.9 %collective-permute-done.other_ref.first_x_ref = f32[256,8192]{1,0:T(8,128)} collective-permute-done((f32[256,8192]{1,0:T(8,128)}, f32[256,8192]{1,0:T(8,128)}, u32[]{:S(2)}, u32[]{:S(2)}) %collective-permute-start) | collective-permute-done | bytes 8388640 | tf_op jit(solution)/shard_map/ppermute | solution.py:390
  20.3 0.4 collective-permute-start.2
  20.6 9.0 %pair_gram.1 = f32[16,24,256]{2,1,0:T(8,128)} custom-call(s32[1]{0:T(128)} %bitcast.core_ref, f32[256,16384]{1,0:T(8,128)} %x_ref.5, f32[256,8192]{1,0:T(8,128)} %collective-permute-done.other_ref.first_x_ref, f32[128,256]{1,0:T(8,128)} %own_gram.1.packed_ref), custom_call_target="tpu_custom_call" | custom-call | flops 1024 | bytes 1024 | tf_op jit(solution)/shard_map/pair_gram/pallas_call | solution.py:258
  29.7 6.6 %cut_positions.3 = f32[256,8192]{1,0:T(8,128)} custom-call(s32[1]{0:T(128)} %bitcast.core_ref, f32[256,16384]{1,0:T(8,128)} %x_ref.5), custom_call_target="tpu_custom_call" | custom-call | bytes 16777216 | tf_op jit(solution)/shard_map/cut_positions/pallas_call | solution.py:158
  36.3 0.2 collective-permute-start.1
  36.5 7.3 %all-to-all-start = ((f32[16,24,256]{2,1,0:T(8,128)}), f32[16,24,256]{2,1,0:T(8,128)S(1)}, u32[]{:S(2)}, u32[]{:S(2)}) async-start(f32[16,24,256]{2,1,0:T(8,128)} %pair_gram.1), calls=%async_computation | async-start | bytes 786432 | tf_op jit(solution)/shard_map/all_to_all | solution.py:410
  43.8 12.2 %all-to-all-done.arrived_ref = f32[16,24,256]{2,1,0:T(8,128)S(1)} async-done(((f32[16,24,256]{2,1,0:T(8,128)}), f32[16,24,256]{2,1,0:T(8,128)S(1)}, u32[]{:S(2)}, u32[]{:S(2)}) %all-to-all-start) | async-done | bytes 393248 | tf_op jit(solution)/shard_map/all_to_all | solution.py:410
  56.0 0.0 copy-start
  56.0 0.8 copy-done
  56.8 1.9 %sum_shards.1 = f32[16,24,256]{2,1,0:T(8,128)} custom-call(s32[1]{0:T(128)S(6)} %add.3.place_ref, f32[16,24,256]{2,1,0:T(8,128)} %copy-done), custom_call_target="tpu_custom_call" | custom-call | tf_op jit(solution)/shard_map/sum_shards/pallas_call | solution.py:295
  58.7 15.7 %all_to_all.10.shards_ref = f32[16,24,256]{2,1,0:T(8,128)S(1)} all-to-all(f32[16,24,256]{2,1,0:T(8,128)} %sum_shards.1), channel_id=1, replica_groups=mesh['grp'=2,'dim'=8,'blk'=2] {'dim','blk'}, dimensions={0} | all-to-all | bytes 786432 | tf_op jit(solution)/shard_map/all_to_all | solution.py:411
  74.4 0.5 kernel_weights.1
  74.9 0.0 collective-permute-done.1.last_x_ref
  74.9 0.0 collective-permute-done.2.other_s_ref
  74.9 28.0 %velocity.1 = f32[256,16384]{1,0:T(8,128)} custom-call(s32[1]{0:T(128)} %bitcast.core_ref, f32[256,16384]{1,0:T(8,128)} %x_ref.5, f32[256,16384]{1,0:T(8,128)} %s_ref.1, f32[256,8192]{1,0:T(8,128)} %collective-permute-done.other_ref.first_x_ref, f32[256,8192]{1,0:T(8,128)} %collective-permute-done.1.last_x_ref, ...), custom_call_target="tpu_custom_call" | custom-call | flops 1024 | bytes 1024 | tf_op jit(solution)/shard_map/velocity/pallas_call | solution.py:381
Async XLA Ops:
  6.6 13.6 %collective-permute-start = (f32[256,8192]{1,0:T(8,128)}, f32[256,8192]{1,0:T(8,128)}, u32[]{:S(2)}, u32[]{:S(2)}) collective-permute-start(f32[256,8192]{1,0:T(8,128)} %cut_positions.2), channel_id=1, source_target_pairs={{0,1},{1,0},{2,3},{3,2},{4,5},{5,4},{6,7},{7,6},{8,9},{9,8},{10,11... | collective-permute-start | bytes 25165832 | tf_op jit(solution)/shard_map/ppermute | solution.py:390
  20.3 54.6 %collective-permute-start.2 = (f32[256,16384]{1,0:T(8,128)}, f32[256,16384]{1,0:T(8,128)}, u32[]{:S(2)}, u32[]{:S(2)}) collective-permute-start(f32[256,16384]{1,0:T(8,128)} %s_ref.1), channel_id=1, source_target_pairs={{0,1},{1,0},{2,3},{3,2},{4,5},{5,4},{6,7},{7,6},{8,9},{9,8},{10,11... | collective-permute-start | bytes 50331656 | tf_op jit(solution)/shard_map/ppermute | solution.py:390
  36.3 38.6 %collective-permute-start.1 = (f32[256,8192]{1,0:T(8,128)}, f32[256,8192]{1,0:T(8,128)}, u32[]{:S(2)}, u32[]{:S(2)}) collective-permute-start(f32[256,8192]{1,0:T(8,128)} %cut_positions.3), channel_id=1, source_target_pairs={{0,1},{1,0},{2,3},{3,2},{4,5},{5,4},{6,7},{7,6},{8,9},{9,8},{10,11... | collective-permute-start | bytes 25165832 | tf_op jit(solution)/shard_map/ppermute | solution.py:390
  36.5 19.5 %all-to-all-start = ((f32[16,24,256]{2,1,0:T(8,128)}), f32[16,24,256]{2,1,0:T(8,128)S(1)}, u32[]{:S(2)}, u32[]{:S(2)}) async-start(f32[16,24,256]{2,1,0:T(8,128)} %pair_gram.1), calls=%async_computation | async-start | bytes 786432 | tf_op jit(solution)/shard_map/all_to_all | solution.py:410
  56.0 0.8 copy-start

commit v15 on v14

--- a/solution.py
+++ b/solution.py
@@ -54,11 +54,8 @@
                 act(pltpu.make_async_copy(source.at[:, columns], buffer.at[slot], sems.at[n, slot]))
 
             if isinstance(source, tuple):
-                begin = 0
-                for piece in source:
-                    end = begin + piece.shape[1] // tile
-                    pl.when((at >= begin) & (at < end))(functools.partial(one, piece, at - begin))
-                    begin = end
+                pl.when(at < steps // 2)(functools.partial(one, source[0], at))
+                pl.when(at >= steps // 2)(functools.partial(one, source[1], at - steps // 2))
             else:
                 one(source, lax.rem(first + at, source.shape[1] // tile))
 
@@ -131,12 +128,10 @@
     gram_ref[...] += nt_dot(halves_ref[...], halves_ref[:rows, :])
 
 
-def cut_kernel(begin, of_other, core_ref, x_ref, out_ref, buffer, in_sems, out_sems):
+def cut_kernel(core_ref, x_ref, out_ref, buffer, in_sems, out_sems):
     columns = out_ref.shape[1]
-    half = x_ref.shape[1] // 2
-    side = 1 - core_ref[0] if of_other else core_ref[0]
     step = columns // in_sems.shape[0]
-    start = pl.multiple_of(side * half + begin, step)
+    start = pl.multiple_of((1 - core_ref[0]) * columns, step)
     ins, outs = [], []
     for n in range(in_sems.shape[0]):
         there = pl.ds(n * step, step)
@@ -152,11 +147,11 @@
         copy.wait()
 
 
-def cut(core, array, begin, width, of_other):
-    rows = array.shape[0]
+def cut(core, array):
+    rows, width = array.shape[0], array.shape[1] // 2
     pieces = max(1, width // 512)
     return pl.pallas_call(
-        functools.partial(cut_kernel, begin, of_other),
+        cut_kernel,
         in_specs=[pl.BlockSpec(memory_space=pltpu.SMEM), in_hbm()],
         out_specs=in_hbm(),
         out_shape=f32(rows, width),
@@ -166,14 +161,12 @@
             pltpu.SemaphoreType.DMA((pieces,)),
         ],
         compiler_params=params(56),
-        cost_estimate=pl.CostEstimate(
-            flops=0, bytes_accessed=1024 if of_other else 8 * rows * width, transcendentals=0
-        ),
+        cost_estimate=pl.CostEstimate(flops=1024, bytes_accessed=1024, transcendentals=0),
         name="cut_positions",
     )(core, array)
 
 
-def own_kernel(core_ref, x_ref, out_ref, gram_ref, squares_ref, halves_ref, buffer, sems):
+def own_kernel(core_ref, x_ref, copy_ref, out_ref, gram_ref, squares_ref, halves_ref, buffer, sems):
     steps = pl.num_programs(0)
 
     @pl.when(pl.program_id(0) == 0)
@@ -181,7 +174,12 @@
         gram_ref[...] = jnp.zeros_like(gram_ref)
         squares_ref[...] = jnp.zeros_like(squares_ref)
 
-    (x,) = fetch([x_ref], [buffer], sems)
+    (x,) = fetch([x_ref], [buffer], sems, core_ref[0] * (steps // 2))
+
+    @pl.when(pl.program_id(0) < steps // 2)
+    def _():
+        copy_ref[...] = x[...]
+
     add_own(x, halves_ref, gram_ref, squares_ref)
 
     @pl.when(pl.program_id(0) == steps - 1)
@@ -201,10 +199,13 @@
 
 def own_part(core, particles):
     rows, columns = particles.shape
-    tile = min(GRAM_TILE, columns)
+    tile = min(GRAM_TILE, columns // 2)
+    steps = columns // tile
     packed = f32(rows // 2, rows)
     return call(
-        own_kernel, "own_gram", columns // tile, [in_hbm()], whole(packed), packed,
+        own_kernel, "own_gram", steps, [in_hbm()],
+        [pl.BlockSpec((rows, tile), lambda i, core: (0, jnp.minimum(i, steps // 2 - 1))), whole(packed)],
+        [f32(rows, columns // 2), packed],
         [
             pltpu.VMEM((2 * rows, rows), jnp.float32),
             pltpu.VMEM((rows, 128), jnp.float32),
@@ -215,9 +216,7 @@
     )(core, particles)
 
 
-def pair_kernel(
-    core_ref, mine_ref, other_ref, packed_ref, out_ref, gram_ref, squares_ref, my_halves, halves, *scratch
-):
+def pair_kernel(core_ref, mine_ref, other_ref, packed_ref, out_ref, gram_ref, squares_ref, my_halves, halves, *scratch):
     my_buffer, buffer, sems = scratch
     steps = pl.num_programs(0)
     rows = gram_ref.shape[0]
@@ -251,12 +250,12 @@
             out_ref[shard, depth:, :] = packed_ref[shard * few:(shard + 1) * few, :]
 
 
-def pair_part(core, particles, visitors, packed, count):
-    rows, width = particles.shape[0], particles.shape[1] // 2
+def pair_part(core, particles, visitor, packed, count):
+    rows, width = visitor.shape
     tile = min(GRAM_TILE, width)
     out = f32(count, rows * 3 // 2 // count, rows)
     return call(
-        pair_kernel, "pair_gram", width // tile, [in_hbm()] * 2 + [whole(packed)], whole(out), out,
+        pair_kernel, "pair_gram", width // tile, [in_hbm(), in_hbm(), whole(packed)], whole(out), out,
         [
             pltpu.VMEM((rows, rows), jnp.float32),
             pltpu.VMEM((2 * rows, 128), jnp.float32),
@@ -265,7 +264,7 @@
             *slots(GRAM_DEPTH, 2, rows, tile),
         ],
         56,
-    )(core, particles, *visitors, packed)
+    )(core, particles, visitor, packed)
 
 
 def sum_kernel(place_ref, arrived_ref, out_ref):
@@ -296,7 +295,7 @@
         sum_kernel,
         in_specs=[pl.BlockSpec(memory_space=pltpu.SMEM), pl.BlockSpec(memory_space=pltpu.VMEM)],
         out_shape=f32(*arrived.shape),
-        compiler_params=params(58),
+        compiler_params=params(12),
         name="sum_shards",
     )(place, arrived)
 
@@ -344,13 +343,13 @@
 
 
 def velocity_kernel(
-    core_ref, x_ref, s_ref, first_x_ref, last_x_ref, other_s_ref, hi_ref, lo_ref, weight_ref, half_ref, out_ref, moved_ref, *scratch
+    core_ref, x_ref, s_ref, first_x_ref, second_x_ref, other_s_ref, hi_ref, lo_ref, weight_ref, half_ref, out_ref, moved_ref, *scratch
 ):
     rows, columns = out_ref.shape
     half = half_ref[...]
     weights = jnp.concatenate([hi_ref[...], lo_ref[...]], axis=0)
     x, s, other_x, other_s = fetch(
-        [x_ref, s_ref, (first_x_ref, last_x_ref), other_s_ref],
+        [x_ref, s_ref, (first_x_ref, second_x_ref), other_s_ref],
         scratch[:4],
         scratch[4],
         core_ref[0] * (pl.num_programs(0) // 2),
@@ -396,17 +395,17 @@
     core = lax.axis_index("blk").reshape(1)
     place = lax.axis_index("dim").reshape(1) * 2 + core
 
-    width = particles.shape[1] // 2
-    sent = cut(core, particles, 0, width, True)
-    visitors = [swap(sent)]
+    core, place = lax.optimization_barrier((core, place))
+
+    sent = cut(core, particles)
+    visitor = swap(sent)
     particles_next, _ = lax.optimization_barrier((particles, sent))
-    packed = own_part(core, particles_next)
-    scores_late, *_ = lax.optimization_barrier((scores, visitors[0], packed))
+    kept, packed = own_part(core, particles_next)
+    kept, scores_late, _ = lax.optimization_barrier((kept, scores, visitor))
+    visitors = [visitor, swap(kept)]
     visitor_scores = swap(scores_late)
 
-    shards = pair_part(core, particles, visitors, packed, lax.axis_size(BOTH))
-    particles_next, _ = lax.optimization_barrier((particles, shards))
-    visitors.append(swap(cut(core, particles_next, 0, width, False)))
+    shards = pair_part(core, particles, visitor, packed, lax.axis_size(BOTH))
     shards = summed_shards(place, lax.all_to_all(shards, BOTH, 0, 0))
     weights = weights_part(core, lax.all_to_all(shards, BOTH, 0, 0), scale_base)
     return velocity_part(core, particles, scores, visitors, visitor_scores, weights)

time: 103 us -> 94 us (0.913)
  blocking collectives: 15.7 us -> 35.1 us
  waiting for transfers between devices: 15.1 us -> 0.01 us
  starting transfers between devices: 8.41 us -> 1.09 us
  Pallas kernels: 62.8 us -> 57.4 us
    all_to_all x0 -> x1, blocking collectives: none -> 19.4 us  [body(): shards = summed_shards(place, lax.all_to_all(shards, BOTH, 0, 0))]
    all_to_all x1 -> x0, waiting for transfers between devices: 12.2 us -> none  [body(): shards = summed_shards(place, lax.all_to_all(shards, BOTH, 0, 0))]
    all_to_all x1 -> x0, starting transfers between devices: 7.32 us -> none  [body(): shards = summed_shards(place, lax.all_to_all(shards, BOTH, 0, 0))]
    pallas_call x4 -> x3, Pallas kernels: 32.4 us -> 28.8 us  [the longest x1 13.2 us: own_part(): call(own_kernel, 'own_gram', steps, [in_hbm()], [pl.BlockSpec((rows, tile...]
    ppermute x3, waiting for transfers between devices: 2.94 us -> 0.01 us  [swap(): return lax.ppermute(array, 'blk', [(0, 1), (1, 0)])]
    pallas_call x1, Pallas kernels: 1.89 us -> 0.14 us  [summed_shards(): pl.pallas_call(sum_kernel, in_specs=[pl.BlockSpec(memory_space=pltpu.SMEM...]
  transfers between devices with their start and end apart: 4 -> 3, of which waited for: 2 -> 0; matrix products, arithmetic and copies ran while one was open for 0% -> 0% of each run, Pallas kernels for 27% -> 24%
where the time goes in v15:
time: 94 us; the launch traced here: 93.7 us
  Pallas kernels  57.4 us (61%)
  blocking collectives  35.1 us (37%)
  starting transfers between devices  1.09 us (1%)
    pallas_call x1, Pallas kernels, velocity_part(): call(velocity_kernel, 'velocity', steps, [in_hbm()] * 5 + [whole(w) for w...  28 us
    all_to_all x1, blocking collectives, body(): shards = summed_shards(place, lax.all_to_all(shards, BOTH, 0, 0))  19.4 us
    all_to_all x1, blocking collectives, body(): weights = weights_part(core, lax.all_to_all(shards, BOTH, 0, 0), scale_base)  15.7 us
    pallas_call x1, Pallas kernels, own_part(): call(own_kernel, 'own_gram', steps, [in_hbm()], [pl.BlockSpec((rows, tile...  13.2 us
    pallas_call x1, Pallas kernels, pair_part(): call(pair_kernel, 'pair_gram', width // tile, [in_hbm(), in_hbm(), whole(...  9 us
    pallas_call x1, Pallas kernels, cut(): pl.pallas_call(cut_kernel, in_specs=[pl.BlockSpec(memory_space=pltpu.SMEM...  6.62 us
  transfers between devices with their start and end apart: 3, of which 0 were waited for; matrix products, arithmetic and copies ran while one was open for 0% of the time, Pallas kernels for 24%

profile of v15, /device:TPU:0, one launch (start us, length us, event | category | flops | bytes accessed | tf_op | source)
XLA Modules:
  0.0 93.7 jit_solution(17092439067279000195)
XLA Ops:
  0.0 6.6 %cut_positions.1 = f32[256,8192]{1,0:T(8,128)} custom-call(s32[1]{0:T(128)} %bitcast.core_ref, f32[256,16384]{1,0:T(8,128)} %x_ref.4), custom_call_target="tpu_custom_call" | custom-call | flops 1024 | bytes 1024 | tf_op jit(solution)/shard_map/cut_positions/pallas_call | solution.py:153
  6.6 0.5 collective-permute-start
  7.1 13.2 %own_gram.1 = (f32[256,8192]{1,0:T(8,128)}, f32[128,256]{1,0:T(8,128)}) custom-call(s32[1]{0:T(128)} %bitcast.core_ref, f32[256,16384]{1,0:T(8,128)} %x_ref.4), custom_call_target="tpu_custom_call" | custom-call | flops 1024 | bytes 1024 | tf_op jit(solution)/shard_map/own_gram/pallas_call | solution.py:205
  20.3 0.0 collective-permute-done.other_ref.first_x_ref
  20.3 0.3 collective-permute-start.2
  20.6 0.3 collective-permute-start.1
  20.9 9.0 %pair_gram.1 = f32[16,24,256]{2,1,0:T(8,128)} custom-call(s32[1]{0:T(128)} %bitcast.core_ref, f32[256,16384]{1,0:T(8,128)} %x_ref.4, f32[256,8192]{1,0:T(8,128)} %collective-permute-done.other_ref.first_x_ref, f32[128,256]{1,0:T(8,128)} %get-tuple-element.22.packed_ref), custom_call_target="tpu_custom_call" | custom-call | flops 1024 | bytes 1024 | tf_op jit(solution)/shard_map/pair_gram/pallas_call | solution.py:257
  29.9 19.4 %all_to_all.10.arrived_ref = f32[16,24,256]{2,1,0:T(8,128)S(1)} all-to-all(f32[16,24,256]{2,1,0:T(8,128)} %pair_gram.1), channel_id=1, replica_groups=mesh['grp'=2,'dim'=8,'blk'=2] {'dim','blk'}, dimensions={0} | all-to-all | bytes 786432 | tf_op jit(solution)/shard_map/all_to_all | solution.py:409
  49.3 0.1 sum_shards.1
  49.4 15.7 %all_to_all.11.shards_ref = f32[16,24,256]{2,1,0:T(8,128)S(1)} all-to-all(f32[16,24,256]{2,1,0:T(8,128)S(1)} %sum_shards.1), channel_id=1, replica_groups=mesh['grp'=2,'dim'=8,'blk'=2] {'dim','blk'}, dimensions={0} | all-to-all | bytes 786432 | tf_op jit(solution)/shard_map/all_to_all | solution.py:410
  65.2 0.5 kernel_weights.1
  65.7 0.0 collective-permute-done.1.second_x_ref
  65.7 0.0 collective-permute-done.2.other_s_ref
  65.7 28.0 %velocity.1 = f32[256,16384]{1,0:T(8,128)} custom-call(s32[1]{0:T(128)} %bitcast.core_ref, f32[256,16384]{1,0:T(8,128)} %x_ref.4, f32[256,16384]{1,0:T(8,128)} %s_ref.1, f32[256,8192]{1,0:T(8,128)} %collective-permute-done.other_ref.first_x_ref, f32[256,8192]{1,0:T(8,128)} %collective-permute-done.1.second_x_ref, ...), custom_call_target="tpu_custom_call" | custom-call | flops 1024 | bytes 1024 | tf_op jit(solution)/shard_map/velocity/pallas_call | solution.py:380
Async XLA Ops:
  6.6 13.7 %collective-permute-start = (f32[256,8192]{1,0:T(8,128)}, f32[256,8192]{1,0:T(8,128)}, u32[]{:S(2)}, u32[]{:S(2)}) collective-permute-start(f32[256,8192]{1,0:T(8,128)} %cut_positions.1), channel_id=1, source_target_pairs={{0,1},{1,0},{2,3},{3,2},{4,5},{5,4},{6,7},{7,6},{8,9},{9,8},{10,11... | collective-permute-start | bytes 25165832 | tf_op jit(solution)/shard_map/ppermute | solution.py:389
  20.3 45.4 %collective-permute-start.2 = (f32[256,16384]{1,0:T(8,128)}, f32[256,16384]{1,0:T(8,128)}, u32[]{:S(2)}, u32[]{:S(2)}) collective-permute-start(f32[256,16384]{1,0:T(8,128)} %s_ref.1), channel_id=1, source_target_pairs={{0,1},{1,0},{2,3},{3,2},{4,5},{5,4},{6,7},{7,6},{8,9},{9,8},{10,11... | collective-permute-start | bytes 50331656 | tf_op jit(solution)/shard_map/ppermute | solution.py:389
  20.6 45.0 %collective-permute-start.1 = (f32[256,8192]{1,0:T(8,128)}, f32[256,8192]{1,0:T(8,128)}, u32[]{:S(2)}, u32[]{:S(2)}) collective-permute-start(f32[256,8192]{1,0:T(8,128)} %get-tuple-element.19), channel_id=1, source_target_pairs={{0,1},{1,0},{2,3},{3,2},{4,5},{5,4},{6,7},{7,6},{8,9},{9,8},{10,11... | collective-permute-start | bytes 25165832 | tf_op jit(solution)/shard_map/ppermute | solution.py:389

commit v16 on v13

--- a/solution.py
+++ b/solution.py
@@ -54,8 +54,11 @@
                 act(pltpu.make_async_copy(source.at[:, columns], buffer.at[slot], sems.at[n, slot]))
 
             if isinstance(source, tuple):
-                pl.when(at < steps // 2)(functools.partial(one, source[0], at))
-                pl.when(at >= steps // 2)(functools.partial(one, source[1], at - steps // 2))
+                begin = 0
+                for piece in source:
+                    end = begin + piece.shape[1] // tile
+                    pl.when((at >= begin) & (at < end))(functools.partial(one, piece, at - begin))
+                    begin = end
             else:
                 one(source, lax.rem(first + at, source.shape[1] // tile))
 
@@ -128,15 +131,17 @@
     gram_ref[...] += nt_dot(halves_ref[...], halves_ref[:rows, :])
 
 
-def sent_kernel(core_ref, x_ref, copy_ref, gram_ref, squares_ref, halves_ref, buffer, sems):
+def sent_kernel(piece, core_ref, x_ref, *refs):
+    gram_in, squares_in = refs[:2] if piece else (None, None)
+    copy_ref, gram_ref, squares_ref, halves_ref, buffer, sems = refs[-6:]
     steps = pl.num_programs(0)
 
     @pl.when(pl.program_id(0) == 0)
     def _():
-        gram_ref[...] = jnp.zeros_like(gram_ref)
-        squares_ref[...] = jnp.zeros_like(squares_ref)
-
-    (x,) = fetch([x_ref], [buffer], sems, (1 - core_ref[0]) * steps)
+        gram_ref[...] = gram_in[...] if piece else jnp.zeros_like(gram_ref)
+        squares_ref[...] = squares_in[...] if piece else jnp.zeros_like(squares_ref)
+
+    (x,) = fetch([x_ref], [buffer], sems, (1 - core_ref[0]) * 2 * steps + piece * steps)
     copy_ref[...] = x[...]
     add_own(x, halves_ref, gram_ref, squares_ref)
 
@@ -171,23 +176,29 @@
 def own_parts(core, particles):
     rows, columns = particles.shape
     width = columns // 2
-    tile = min(GRAM_TILE, width)
+    tile = min(GRAM_TILE, width // 2)
     block = pl.BlockSpec((rows, tile), lambda i, core: (0, i))
     sums = [f32(2 * rows, rows), f32(rows, 128)]
     scratch = [pltpu.VMEM((2 * rows, tile), jnp.bfloat16), *slots(GRAM_DEPTH, 1, rows, tile)]
-    sent, *partial = call(
-        sent_kernel, "own_gram_sent", width // tile, [in_hbm()], [block] + [whole(o) for o in sums],
-        [f32(rows, width)] + sums, scratch, 56,
-    )(core, particles)
+    sent, partial = [], []
+    for piece in range(2):
+        copy, *partial = call(
+            functools.partial(sent_kernel, piece), "own_gram_sent", width // tile // 2,
+            [in_hbm()] + [whole(p) for p in partial], [block] + [whole(o) for o in sums],
+            [f32(rows, width // 2)] + sums, scratch, 60,
+        )(core, particles, *partial)
+        sent.append(copy)
     packed = f32(rows // 2, rows)
     kept, packed = call(
         kept_kernel, "own_gram_kept", width // tile, [in_hbm()] + [whole(o) for o in sums], [block, whole(packed)],
-        [f32(rows, width), packed], [pltpu.VMEM(o.shape, jnp.float32) for o in sums] + scratch, 56,
+        [f32(rows, width), packed], [pltpu.VMEM(o.shape, jnp.float32) for o in sums] + scratch, 60,
     )(core, particles, *partial)
     return sent, kept, packed
 
 
-def pair_kernel(core_ref, mine_ref, other_ref, packed_ref, out_ref, gram_ref, squares_ref, my_halves, halves, *scratch):
+def pair_kernel(
+    core_ref, mine_ref, first_ref, second_ref, packed_ref, out_ref, gram_ref, squares_ref, my_halves, halves, *scratch
+):
     my_buffer, buffer, sems = scratch
     steps = pl.num_programs(0)
     rows = gram_ref.shape[0]
@@ -197,7 +208,7 @@
         gram_ref[...] = jnp.zeros_like(gram_ref)
         squares_ref[...] = jnp.zeros_like(squares_ref)
 
-    mine, other = fetch([mine_ref, other_ref], [my_buffer, buffer], sems, core_ref[0] * steps)
+    mine, other = fetch([mine_ref, (first_ref, second_ref)], [my_buffer, buffer], sems, core_ref[0] * steps)
     for offset, source, halves_ref in ((0, mine, my_halves), (rows, other, halves)):
         for row, column in strips(*source.shape):
             part = source[row, column]
@@ -221,12 +232,12 @@
             out_ref[shard, depth:, :] = packed_ref[shard * few:(shard + 1) * few, :]
 
 
-def pair_part(core, particles, visitor, packed, count):
-    rows, width = visitor.shape
-    tile = min(GRAM_TILE, width)
+def pair_part(core, particles, visitors, packed, count):
+    rows, width = particles.shape[0], particles.shape[1] // 2
+    tile = min(GRAM_TILE, width // 2)
     out = f32(count, rows * 3 // 2 // count, rows)
     return call(
-        pair_kernel, "pair_gram", width // tile, [in_hbm(), in_hbm(), whole(packed)], whole(out), out,
+        pair_kernel, "pair_gram", width // tile, [in_hbm()] * 3 + [whole(packed)], whole(out), out,
         [
             pltpu.VMEM((rows, rows), jnp.float32),
             pltpu.VMEM((2 * rows, 128), jnp.float32),
@@ -234,8 +245,8 @@
             pltpu.VMEM((2 * rows, tile), jnp.bfloat16),
             *slots(GRAM_DEPTH, 2, rows, tile),
         ],
-        56,
-    )(core, particles, visitor, packed)
+        60,
+    )(core, particles, *visitors, packed)
 
 
 def sum_kernel(place_ref, arrived_ref, out_ref):
@@ -314,13 +325,13 @@
 
 
 def velocity_kernel(
-    core_ref, x_ref, s_ref, first_x_ref, second_x_ref, other_s_ref, hi_ref, lo_ref, weight_ref, half_ref, out_ref, moved_ref, *scratch
+    core_ref, x_ref, s_ref, first_x_ref, second_x_ref, last_x_ref, other_s_ref, hi_ref, lo_ref, weight_ref, half_ref, out_ref, moved_ref, *scratch
 ):
     rows, columns = out_ref.shape
     half = half_ref[...]
     weights = jnp.concatenate([hi_ref[...], lo_ref[...]], axis=0)
     x, s, other_x, other_s = fetch(
-        [x_ref, s_ref, (first_x_ref, second_x_ref), other_s_ref],
+        [x_ref, s_ref, (first_x_ref, second_x_ref, last_x_ref), other_s_ref],
         scratch[:4],
         scratch[4],
         core_ref[0] * (pl.num_programs(0) // 2),
@@ -346,10 +357,10 @@
 
 def velocity_part(core, particles, scores, visitors, visitor_scores, weights):
     rows, columns = particles.shape
-    tile = min(VELOCITY_TILE, columns // 2)
+    tile = min(VELOCITY_TILE, columns // 4)
     steps = columns // tile
     return call(
-        velocity_kernel, "velocity", steps, [in_hbm()] * 5 + [whole(w) for w in weights],
+        velocity_kernel, "velocity", steps, [in_hbm()] * 6 + [whole(w) for w in weights],
         pl.BlockSpec((rows, tile), lambda i, core: (0, lax.rem(core[0] * (steps // 2) + i, steps))),
         f32(rows, columns), [pltpu.VMEM((4 * rows, tile), jnp.bfloat16), *slots(VELOCITY_DEPTH, 4, rows, tile)],
         52,
@@ -366,13 +377,15 @@
     core = lax.axis_index("blk").reshape(1)
     place = lax.axis_index("dim").reshape(1) * 2 + core
 
+    core, place = lax.optimization_barrier((core, place))
+
     sent, kept, packed = own_parts(core, particles)
-    visitor = swap(sent)
-    kept, scores_late, _ = lax.optimization_barrier((kept, scores, visitor))
-    visitors = [visitor, swap(kept)]
+    visitors = [swap(part) for part in sent]
+    kept, scores_late, *_ = lax.optimization_barrier((kept, scores, *visitors))
     visitor_scores = swap(scores_late)
 
-    shards = pair_part(core, particles, visitor, packed, lax.axis_size(BOTH))
+    shards = pair_part(core, particles, visitors, packed, lax.axis_size(BOTH))
+    visitors.append(swap(kept))
     shards = summed_shards(place, lax.all_to_all(shards, BOTH, 0, 0))
     weights = weights_part(core, lax.all_to_all(shards, BOTH, 0, 0), scale_base)
     return velocity_part(core, particles, scores, visitors, visitor_scores, weights)

time: 95.2 us -> 94.9 us (level)
  blocking collectives: 15.7 us -> 35.3 us
  waiting for transfers between devices: 16.1 us -> 0.01 us
  starting transfers between devices: 8.36 us -> 1.25 us
  Pallas kernels: 54.7 us -> 58 us
    all_to_all x0 -> x1, blocking collectives: none -> 19.6 us  [body(): shards = summed_shards(place, lax.all_to_all(shards, BOTH, 0, 0))]
    all_to_all x1 -> x0, waiting for transfers between devices: 12.2 us -> none  [body(): shards = summed_shards(place, lax.all_to_all(shards, BOTH, 0, 0))]
    all_to_all x1 -> x0, starting transfers between devices: 7.32 us -> none  [body(): shards = summed_shards(place, lax.all_to_all(shards, BOTH, 0, 0))]
    ppermute x3 -> x4, waiting for transfers between devices: 3.87 us -> 0.01 us  [swap(): return lax.ppermute(array, 'blk', [(0, 1), (1, 0)])]
    pallas_call x3 -> x4, Pallas kernels: 44.8 us -> 48 us  [the longest x1 28 us: velocity_part(): call(velocity_kernel, 'velocity', steps, [in_hbm()] * 6 + [whole(w) for w...]
  transfers between devices with their start and end apart: 4 -> 4, of which waited for: 2 -> 0; matrix products, arithmetic and copies ran while one was open for 0% -> 0% of each run, Pallas kernels for 20% -> 26%
where the time goes in v16:
time: 94.9 us; the launch traced here: 94.6 us
  Pallas kernels  58 us (61%)
  blocking collectives  35.3 us (37%)
  starting transfers between devices  1.25 us (1%)
    pallas_call x1, Pallas kernels, velocity_part(): call(velocity_kernel, 'velocity', steps, [in_hbm()] * 6 + [whole(w) for w...  28 us
    all_to_all x1, blocking collectives, body(): shards = summed_shards(place, lax.all_to_all(shards, BOTH, 0, 0))  19.6 us
    all_to_all x1, blocking collectives, body(): weights = weights_part(core, lax.all_to_all(shards, BOTH, 0, 0), scale_base)  15.7 us
    pallas_call x2, Pallas kernels, own_parts(): call(functools.partial(sent_kernel, piece), 'own_gram_sent', width // til...  11.1 us
    pallas_call x1, Pallas kernels, own_parts(): call(kept_kernel, 'own_gram_kept', width // tile, [in_hbm()] + [whole(o)...  9.26 us
    pallas_call x1, Pallas kernels, pair_part(): call(pair_kernel, 'pair_gram', width // tile, [in_hbm()] * 3 + [whole(pac...  8.99 us
  transfers between devices with their start and end apart: 4, of which 0 were waited for; matrix products, arithmetic and copies ran while one was open for 0% of the time, Pallas kernels for 26%

profile of v16, /device:TPU:0, one launch (start us, length us, event | category | flops | bytes accessed | tf_op | source)
XLA Modules:
  0.0 94.6 jit_solution(3343741049082152385)
XLA Ops:
  0.0 4.9 %own_gram_sent.2 = (f32[256,4096]{1,0:T(8,128)}, f32[512,256]{1,0:T(8,128)}, f32[256,128]{1,0:T(8,128)}) custom-call(s32[1]{0:T(128)} %bitcast.core_ref, f32[256,16384]{1,0:T(8,128)} %x_ref.7), custom_call_target="tpu_custom_call" | custom-call | flops 1024 | bytes 1024 | tf_op jit(solution)/shard_map/own_gram_sent/pallas_call | solution.py:185
  5.0 0.5 collective-permute-start
  5.5 6.1 %own_gram_sent.3 = (f32[256,4096]{1,0:T(8,128)}, f32[512,256]{1,0:T(8,128)}, f32[256,128]{1,0:T(8,128)}) custom-call(s32[1]{0:T(128)} %bitcast.core_ref, f32[256,16384]{1,0:T(8,128)} %x_ref.7, f32[512,256]{1,0:T(8,128)} %get-tuple-element.23.refs_0_, f32[256,128]{1,0:T(8,128)} %get-tuple-element.24.refs_1_), custom_call_target="tpu_custom_call" | custom-call | flops 1024 | bytes 1024 | tf_op jit(solution)/shard_map/own_gram_sent/pallas_call | solution.py:185
  11.6 0.1 collective-permute-start.1
  11.7 9.3 %own_gram_kept.1 = (f32[256,8192]{1,0:T(8,128)}, f32[128,256]{1,0:T(8,128)}) custom-call(s32[1]{0:T(128)} %bitcast.core_ref, f32[256,16384]{1,0:T(8,128)} %x_ref.7, f32[512,256]{1,0:T(8,128)} %get-tuple-element.26.gram_in, f32[256,128]{1,0:T(8,128)} %get-tuple-element.27.squares_in), custom_call_target="tpu_custom_call" | custom-call | flops 1024 | bytes 1024 | tf_op jit(solution)/shard_map/own_gram_kept/pallas_call | solution.py:192
  21.0 0.0 collective-permute-done.first_ref.first_x_ref
  21.0 0.0 collective-permute-done.1.second_ref.second_x_ref
  21.0 0.5 collective-permute-start.3
  21.5 0.1 collective-permute-start.2
  21.6 9.0 %pair_gram.1 = f32[16,24,256]{2,1,0:T(8,128)} custom-call(s32[1]{0:T(128)} %bitcast.core_ref, f32[256,16384]{1,0:T(8,128)} %x_ref.7, f32[256,4096]{1,0:T(8,128)} %collective-permute-done.first_ref.first_x_ref, f32[256,4096]{1,0:T(8,128)} %collective-permute-done.1.second_ref.second_x_ref, f32[128,256]{1,0:T(8,128)} %get-tuple-element.32.packed_ref), custom_call_target="tpu_custom_call" | custom-call | flops 1024 | bytes 1024 | tf_op jit(solution)/shard_map/pair_gram/pallas_call | solution.py:239
  30.6 19.6 %all_to_all.10.arrived_ref = f32[16,24,256]{2,1,0:T(8,128)S(1)} all-to-all(f32[16,24,256]{2,1,0:T(8,128)} %pair_gram.1), channel_id=1, replica_groups=mesh['grp'=2,'dim'=8,'blk'=2] {'dim','blk'}, dimensions={0} | all-to-all | bytes 786432 | tf_op jit(solution)/shard_map/all_to_all | solution.py:389
  50.2 0.1 sum_shards.1
  50.4 15.7 %all_to_all.11.shards_ref = f32[16,24,256]{2,1,0:T(8,128)S(1)} all-to-all(f32[16,24,256]{2,1,0:T(8,128)S(1)} %sum_shards.1), channel_id=1, replica_groups=mesh['grp'=2,'dim'=8,'blk'=2] {'dim','blk'}, dimensions={0} | all-to-all | bytes 786432 | tf_op jit(solution)/shard_map/all_to_all | solution.py:390
  66.1 0.5 kernel_weights.1
  66.6 0.0 collective-permute-done.2.last_x_ref
  66.6 0.0 collective-permute-done.3.other_s_ref
  66.6 28.0 %velocity.1 = f32[256,16384]{1,0:T(8,128)} custom-call(s32[1]{0:T(128)} %bitcast.core_ref, f32[256,16384]{1,0:T(8,128)} %x_ref.7, f32[256,16384]{1,0:T(8,128)} %s_ref.1, f32[256,4096]{1,0:T(8,128)} %collective-permute-done.first_ref.first_x_ref, f32[256,4096]{1,0:T(8,128)} %collective-permute-done.1.second_ref.second_x_ref, ...), custom_call_target="tpu_custom_call" | custom-call | flops 1024 | bytes 1024 | tf_op jit(solution)/shard_map/velocity/pallas_call | solution.py:362
Async XLA Ops:
  5.0 16.1 %collective-permute-start = (f32[256,4096]{1,0:T(8,128)}, f32[256,4096]{1,0:T(8,128)}, u32[]{:S(2)}, u32[]{:S(2)}) collective-permute-start(f32[256,4096]{1,0:T(8,128)} %get-tuple-element.22), channel_id=1, source_target_pairs={{0,1},{1,0},{2,3},{3,2},{4,5},{5,4},{6,7},{7,6},{8,9},{9,8},{10,11... | collective-permute-start | bytes 12582920 | tf_op jit(solution)/shard_map/ppermute | solution.py:371
  11.6 9.4 %collective-permute-start.1 = (f32[256,4096]{1,0:T(8,128)}, f32[256,4096]{1,0:T(8,128)}, u32[]{:S(2)}, u32[]{:S(2)}) collective-permute-start(f32[256,4096]{1,0:T(8,128)} %get-tuple-element.25), channel_id=1, source_target_pairs={{0,1},{1,0},{2,3},{3,2},{4,5},{5,4},{6,7},{7,6},{8,9},{9,8},{10,11... | collective-permute-start | bytes 12582920 | tf_op jit(solution)/shard_map/ppermute | solution.py:371
  21.0 45.6 %collective-permute-start.3 = (f32[256,16384]{1,0:T(8,128)}, f32[256,16384]{1,0:T(8,128)}, u32[]{:S(2)}, u32[]{:S(2)}) collective-permute-start(f32[256,16384]{1,0:T(8,128)} %s_ref.1), channel_id=1, source_target_pairs={{0,1},{1,0},{2,3},{3,2},{4,5},{5,4},{6,7},{7,6},{8,9},{9,8},{10,11... | collective-permute-start | bytes 50331656 | tf_op jit(solution)/shard_map/ppermute | solution.py:371
  21.5 45.1 %collective-permute-start.2 = (f32[256,8192]{1,0:T(8,128)}, f32[256,8192]{1,0:T(8,128)}, u32[]{:S(2)}, u32[]{:S(2)}) collective-permute-start(f32[256,8192]{1,0:T(8,128)} %get-tuple-element.29), channel_id=1, source_target_pairs={{0,1},{1,0},{2,3},{3,2},{4,5},{5,4},{6,7},{7,6},{8,9},{9,8},{10,11... | collective-permute-start | bytes 25165832 | tf_op jit(solution)/shard_map/ppermute | solution.py:371
